TPU v7x, 32 devices: a whole 2x2x4 slice. The times are simulated.
32 devices in a mesh: pipe: 4 (over z), hid: 8 (over y, x, core).
Axes of the slice: x: 2, y: 2, z: 4, core: 2. Of those that a mesh axis runs over, the one named last changes fastest.
Arguments:
- section_inputs: bfloat16 [4, 3, 256, 1024], P('pipe', None, 'hid'), may hold values from -6 to 6
- w_in: bfloat16 [4, 1024, 32768], P('pipe', None, 'hid'), may hold values from -0.1875 to 0.1875
- w_out: bfloat16 [4, 32768, 1024], P('pipe', 'hid'), may hold values from -0.03125 to 0.03125
- warm_factor: float32 [4, 1024, 16], P('pipe'), may hold values from -6 to 6
- pending_left: float32 [4, 256, 16], P('pipe'), may hold values from -0.375 to 0.375
- pending_right: float32 [4, 1024, 16], P('pipe'), may hold values from -24 to 24
- incoming_left: float32 [3, 256, 16], replicated, may hold values from -0.375 to 0.375
- incoming_right: float32 [3, 1024, 16], replicated, may hold values from -24 to 24
Outputs:
- section_grads: float32 [4, 256, 1024], P('pipe', 'hid')
- final_left: float32 [4, 256, 16], P('pipe', 'hid')
- final_right: float32 [4, 1024, 16], P('pipe')
All inputs are finite; a program needn't handle non-finite values.
Results may differ from a plain program's by a relative error of at most 0.02.
Values may be sent and summed in bfloat16 or wider, within the bound.
No kernel may reach another device: no remote copies, remote signals or barrier semaphores. Data moves between devices by JAX's collectives and lax.ppermute only.
A program may use at most 64 MiB of HBM per device.

v0:
```python
import jax
import jax.numpy as jnp
from jax import lax
from jax.sharding import PartitionSpec as P

TICKS = 3


def shifted(value, axis, steps):
    count = lax.axis_size(axis)
    leading, last = (max(0, -steps), min(count, count - steps))
    return lax.ppermute(value, axis, [(source, source + steps) for source in range(leading, last)])


def solve_lower(lower_factor, matrix):
    return jax.scipy.linalg.solve_triangular(lower_factor, matrix.T, lower=True).T


def high_dot(first, second):
    return jnp.dot(
        first, second, precision=lax.Precision.HIGHEST, preferred_element_type=jnp.float32
    )


def rows_product(first, second):
    return lax.dot_general(
        first,
        second,
        (((0,), (0,)), ((), ())),
        precision=lax.Precision.HIGHEST,
        preferred_element_type=jnp.float32,
    )


def body(
    section_inputs,
    w_in,
    w_out,
    warm_factor,
    pending_left,
    pending_right,
    incoming_left,
    incoming_right,
):
    w_in_section = w_in[0]
    w_out_section = w_out[0]
    is_top = lax.axis_index("pipe") == lax.axis_size("pipe") - 1
    rows_own = section_inputs.shape[2]
    lane_index = lax.axis_index("hid")
    row_offset = lane_index * rows_own
    held_left = pending_left[0]
    held_right = pending_right[0]
    warm_basis = warm_factor[0]
    merged_rows = None
    left_rows = None
    right_new = None
    for tick_index in range(TICKS):
        left_factor = jnp.where(is_top, incoming_left[tick_index], held_left)
        right_factor = jnp.where(is_top, incoming_right[tick_index], held_right)
        cotangent = lax.dot_general(
            left_factor,
            right_factor,
            (((1,), (1,)), ((), ())),
            precision=lax.Precision.HIGHEST,
            preferred_element_type=jnp.float32,
        )
        cotangent_low = cotangent.astype(jnp.bfloat16)
        upward = lax.dot_general(
            cotangent_low,
            w_out_section,
            (((1,), (1,)), ((), ())),
            preferred_element_type=jnp.float32,
        )
        preact = jnp.dot(
            lax.all_gather(section_inputs[0, tick_index], "hid", axis=0, tiled=True),
            w_in_section,
            preferred_element_type=jnp.float32,
        )
        hidden_grad = jnp.where(preact > 0, upward, jnp.zeros_like(upward)).astype(jnp.bfloat16)
        last_tick = tick_index + 1 == TICKS
        partial_value = lax.dot_general(
            hidden_grad, w_in_section, (((1,), (1,)), ((), ())), preferred_element_type=jnp.float32
        )
        summed = lax.psum(partial_value, "hid")
        merged = cotangent + summed
        projected = high_dot(merged, warm_basis)
        gram_matrix = rows_product(projected, projected)
        lower_factor = jnp.linalg.cholesky(gram_matrix)
        left_new = solve_lower(lower_factor, projected)
        right_new = rows_product(merged, left_new)
        merged_rows = lax.dynamic_slice_in_dim(merged, row_offset, rows_own, 0)
        left_rows = lax.dynamic_slice_in_dim(left_new, row_offset, rows_own, 0)
        if not last_tick:
            held_left, held_right = shifted((left_new, right_new), "pipe", -1)
        warm_basis = right_new
    return (merged_rows[None], left_rows[None], right_new[None])


def solution(mesh):
    placed = (
        P("pipe", None, "hid", None),
        P("pipe", None, "hid"),
        P("pipe", "hid", None),
        P("pipe", None, None),
        P("pipe", None, None),
        P("pipe", None, None),
        P(),
        P(),
    )
    return jax.shard_map(
        body,
        mesh=mesh,
        in_specs=placed,
        out_specs=(P("pipe", "hid", None), P("pipe", "hid", None), P("pipe", None, None)),
        check_vma=False,
    )
```

profile of v0, /device:TPU:0, one launch (start us, length us, event | category | flops | bytes accessed | tf_op | source)
XLA Modules:
  0.0 284.9 jit_solution(40448668773514473)
XLA Ops:
  7.2 0.0 copy-start
  7.2 0.0 all-reduce.4.cloned.1.call-start
  7.2 0.9 fusion.101
  8.2 11.3 %all-gather = bf16[1,1,256,1024]{3,2,1,0:T(8,128)(2,1)S(1)} all-gather(bf16[1,1,32,1024]{3,2,1,0:T(8,128)(2,1)S(1)} %get-tuple-element.6), channel_id=2, replica_groups=mesh['pipe'=4,'hid'=8] {'hid'}, dimensions={2}, use_global_device_ids=true | all-gather | bytes 589824 | tf_op jit(solution)/shard_map/all_gather | solution.py:75
  19.5 5.8 %fusion.36 = pred[256,4096]{1,0:T(32,128)(4,1)S(1)} fusion(bf16[1,1024,4096]{2,1,0:T(8,128)(2,1)} %param.12, bf16[1,1,256,1024]{3,2,1,0:T(8,128)(2,1)S(1)} %all-gather), kind=kOutput, calls=%fused_computation.24 | convolution fusion | flops 2148532224 | bytes 9961472 | tf_op jit(solution)/shard_map/dot_general | solution.py:74
  25.3 1.0 fusion.64
  26.4 11.4 %fusion.14 = f32[256,1024]{1,0:T(8,128)} fusion(bf16[1,1024,4096]{2,1,0:T(8,128)(2,1)} %param.12, pred[256,4096]{1,0:T(32,128)(4,1)S(1)} %fusion.36, bf16[1,4096,1024]{2,1,0:T(8,128)(2,1)} %param.13, f32[256,1024]{1,0:T(8,128)S(1)} %fusion.64), kind=kOutput, calls=%fused_computation.14 | convolution fusion | flops 4297326592 | bytes 19922944 | tf_op jit(solution)/shard_map/dot_general | solution.py:81
  37.7 0.0 all-reduce.4.cloned.1.call-update
  37.7 0.0 all-reduce.6.cloned.1.call-start
  37.8 10.8 %all-gather.1 = bf16[1,1,256,1024]{3,2,1,0:T(8,128)(2,1)S(1)} all-gather(bf16[1,1,32,1024]{3,2,1,0:T(8,128)(2,1)S(1)} %get-tuple-element.7), channel_id=3, replica_groups=mesh['pipe'=4,'hid'=8] {'hid'}, dimensions={2}, use_global_device_ids=true | all-gather | bytes 589824 | tf_op jit(solution)/shard_map/all_gather | solution.py:75
  48.6 46.7 %all-reduce.4.cloned.1.call-done = f32[256,1024]{1,0:T(8,128)} async-done(((f32[256,1024]{1,0:T(8,128)}), f32[256,1024]{1,0:T(8,128)}) %all-reduce.4.cloned.1.call-update) | async-done | bytes 1048592 | tf_op jit(solution)/shard_map/psum | solution.py:84
  95.3 1.4 add.28
  96.7 0.0 copy-done
  96.7 0.9 fusion.62
  97.6 0.1 fusion.102
  97.7 0.1 copy.11
  97.8 1.5 cholesky.59
  99.3 0.6 compare_reduce_fusion.2
  100.0 0.6 fusion.84
  100.6 1.2 custom-call.7
  101.8 0.2 fusion.77
  102.1 0.7 fusion.103
  102.7 1.3 collective-permute-start.1
  104.0 1.5 collective-permute-start
  105.5 5.8 %fusion.39 = pred[256,4096]{1,0:T(32,128)(4,1)S(1)} fusion(bf16[1,1024,4096]{2,1,0:T(8,128)(2,1)} %param.12, bf16[1,1,256,1024]{3,2,1,0:T(8,128)(2,1)S(1)} %all-gather.1), kind=kOutput, calls=%fused_computation.25 | convolution fusion | flops 2148532224 | bytes 9961472 | tf_op jit(solution)/shard_map/dot_general | solution.py:74
  111.3 0.0 collective-permute-done
  111.3 0.0 collective-permute-done.1
  111.3 1.0 fusion.61
  112.3 11.4 %fusion.10 = f32[256,1024]{1,0:T(8,128)} fusion(bf16[1,1024,4096]{2,1,0:T(8,128)(2,1)} %param.12, pred[256,4096]{1,0:T(32,128)(4,1)S(1)} %fusion.39, bf16[1,4096,1024]{2,1,0:T(8,128)(2,1)} %param.13, f32[256,1024]{1,0:T(8,128)S(1)} %fusion.61), kind=kOutput, calls=%fused_computation.10 | convolution fusion | flops 4297326592 | bytes 19922944 | tf_op jit(solution)/shard_map/dot_general | solution.py:81
  123.7 0.0 all-reduce.6.cloned.1.call-update
  123.7 0.0 all-reduce.8.cloned.1.call-start
  123.8 8.9 %all-gather.2 = bf16[1,1,256,1024]{3,2,1,0:T(8,128)(2,1)S(1)} all-gather(bf16[1,1,32,1024]{3,2,1,0:T(8,128)(2,1)S(1)} %get-tuple-element.5), channel_id=4, replica_groups=mesh['pipe'=4,'hid'=8] {'hid'}, dimensions={2}, use_global_device_ids=true | all-gather | bytes 589824 | tf_op jit(solution)/shard_map/all_gather | solution.py:75
  132.6 49.8 %all-reduce.6.cloned.1.call-done = f32[256,1024]{1,0:T(8,128)} async-done(((f32[256,1024]{1,0:T(8,128)}), f32[256,1024]{1,0:T(8,128)}) %all-reduce.6.cloned.1.call-update) | async-done | bytes 1048592 | tf_op jit(solution)/shard_map/psum | solution.py:84
  182.5 1.4 add.29
  183.8 0.9 fusion.104
  184.7 0.1 fusion.105
  184.9 0.1 copy.12
  185.0 1.5 cholesky.70
  186.5 0.6 compare_reduce_fusion.1
  187.1 0.6 fusion.85
  187.8 1.2 custom-call.8
  189.0 0.2 fusion.75
  189.2 0.7 fusion.106
  189.9 1.3 collective-permute-start.3
  191.2 1.5 collective-permute-start.2
  192.7 5.8 %fusion.42 = pred[256,4096]{1,0:T(32,128)(4,1)S(1)} fusion(bf16[1,1024,4096]{2,1,0:T(8,128)(2,1)} %param.12, bf16[1,1,256,1024]{3,2,1,0:T(8,128)(2,1)S(1)} %all-gather.2), kind=kOutput, calls=%fused_computation.26 | convolution fusion | flops 2148532224 | bytes 9961472 | tf_op jit(solution)/shard_map/dot_general | solution.py:74
  198.5 0.0 collective-permute-done.2
  198.5 0.0 collective-permute-done.3
  198.5 1.0 fusion.60
  199.5 11.4 %fusion.6 = f32[256,1024]{1,0:T(8,128)} fusion(bf16[1,1024,4096]{2,1,0:T(8,128)(2,1)} %param.12, pred[256,4096]{1,0:T(32,128)(4,1)S(1)} %fusion.42, bf16[1,4096,1024]{2,1,0:T(8,128)(2,1)} %param.13, f32[256,1024]{1,0:T(8,128)S(1)} %fusion.60), kind=kOutput, calls=%fused_computation.6 | convolution fusion | flops 4297326592 | bytes 19922944 | tf_op jit(solution)/shard_map/dot_general | solution.py:81
  210.9 0.0 all-reduce.8.cloned.1.call-update
  210.9 58.1 %all-reduce.8.cloned.1.call-done = f32[256,1024]{1,0:T(8,128)} async-done(((f32[256,1024]{1,0:T(8,128)}), f32[256,1024]{1,0:T(8,128)}) %all-reduce.8.cloned.1.call-update) | async-done | bytes 1048592 | tf_op jit(solution)/shard_map/psum | solution.py:84
  269.0 1.4 add.30
  270.4 0.9 fusion.107
  271.3 0.1 fusion.108
  271.4 0.1 copy.13
  271.5 1.5 cholesky.81
  273.0 0.6 compare_reduce_fusion
  273.7 0.6 fusion.86
  274.3 1.2 custom-call.9
  275.6 0.2 fusion.73
  275.8 1.3 convolution_bitcast_fusion
  277.1 0.7 dynamic-slice_bitcast_fusion.1
  277.7 0.7 dynamic-slice_bitcast_fusion
  (14 shorter events, 0.1 us)
Async XLA Ops:
  7.2 89.5 %copy-start = (f32[1,1024,16]{1,2,0:T(8,128)S(1)}, f32[1,1024,16]{1,2,0:T(8,128)}, u32[]{:S(2)}) copy-start(f32[1,1024,16]{1,2,0:T(8,128)} %param.14) | copy-start | bytes 196612
  7.2 88.1 %all-reduce.4.cloned.1.call-start = ((), (), s32[]{:S(2)}) async-start(), calls=%async_computation | async-start | bytes 2097152 | tf_op jit(solution)/shard_map/psum | solution.py:84
  19.5 5.8 %copy-start.1 = (f32[3,1024,16]{1,2,0:T(8,128)S(1)}, f32[3,1024,16]{1,2,0:T(8,128)}, u32[]{:S(2)}) copy-start(f32[3,1024,16]{1,2,0:T(8,128)} %param.18) | copy-start | bytes 589828
  19.5 5.8 %copy-start.2 = (f32[1,1024,16]{1,2,0:T(8,128)S(1)}, f32[1,1024,16]{1,2,0:T(8,128)}, u32[]{:S(2)}) copy-start(f32[1,1024,16]{1,2,0:T(8,128)} %param.16) | copy-start | bytes 196612
  19.5 5.8 %copy-start.3 = (f32[3,256,16]{1,2,0:T(8,128)S(1)}, f32[3,256,16]{1,2,0:T(8,128)}, u32[]{:S(2)}) copy-start(f32[3,256,16]{1,2,0:T(8,128)} %param.17) | copy-start | bytes 147460
  19.5 5.8 %copy-start.4 = (f32[1,256,16]{1,2,0:T(8,128)S(1)}, f32[1,256,16]{1,2,0:T(8,128)}, u32[]{:S(2)}) copy-start(f32[1,256,16]{1,2,0:T(8,128)} %param.15) | copy-start | bytes 49156
  37.7 144.7 %all-reduce.6.cloned.1.call-start = ((), (), s32[]{:S(2)}) async-start(), calls=%async_computation.1 | async-start | bytes 2097152 | tf_op jit(solution)/shard_map/psum | solution.py:84
  102.7 8.6 %collective-permute-start.1 = (f32[1024,16]{0,1:T(8,128)S(1)}, f32[1024,16]{0,1:T(8,128)S(1)}, u32[]{:S(2)}, u32[]{:S(2)}) collective-permute-start(f32[1024,16]{0,1:T(8,128)S(1)} %fusion.103), channel_id=1, source_target_pairs={{8,0},{16,8},{24,16},{9,1},{17,9},{25,17},{10,2},{18,10},{26,18},{... | collective-permute-start | bytes 196616 | tf_op jit(solution)/shard_map/ppermute | solution.py:12
  104.0 7.3 %collective-permute-start = (f32[256,16]{0,1:T(8,128)S(1)}, f32[256,16]{0,1:T(8,128)S(1)}, u32[]{:S(2)}, u32[]{:S(2)}) collective-permute-start(f32[256,16]{0,1:T(8,128)S(1)} %bitcast.137), channel_id=1, source_target_pairs={{8,0},{16,8},{24,16},{9,1},{17,9},{25,17},{10,2},{18,10},{26,18},{... | collective-permute-start | bytes 49160 | tf_op jit(solution)/shard_map/ppermute | solution.py:12
  123.7 145.3 %all-reduce.8.cloned.1.call-start = ((), (), s32[]{:S(2)}) async-start(), calls=%async_computation.2 | async-start | bytes 2097152 | tf_op jit(solution)/shard_map/psum | solution.py:84
  189.9 8.6 %collective-permute-start.3 = (f32[1024,16]{0,1:T(8,128)S(1)}, f32[1024,16]{0,1:T(8,128)S(1)}, u32[]{:S(2)}, u32[]{:S(2)}) collective-permute-start(f32[1024,16]{0,1:T(8,128)S(1)} %fusion.106), channel_id=1, source_target_pairs={{8,0},{16,8},{24,16},{9,1},{17,9},{25,17},{10,2},{18,10},{26,18},{... | collective-permute-start | bytes 196616 | tf_op jit(solution)/shard_map/ppermute | solution.py:12
  191.2 7.3 %collective-permute-start.2 = (f32[256,16]{0,1:T(8,128)S(1)}, f32[256,16]{0,1:T(8,128)S(1)}, u32[]{:S(2)}, u32[]{:S(2)}) collective-permute-start(f32[256,16]{0,1:T(8,128)S(1)} %bitcast.138), channel_id=1, source_target_pairs={{8,0},{16,8},{24,16},{9,1},{17,9},{25,17},{10,2},{18,10},{26,18},{... | collective-permute-start | bytes 49160 | tf_op jit(solution)/shard_map/ppermute | solution.py:12
Sparse Core Ops, SparseCore 0:
  37.9 57.3 all-reduce.3
  123.8 58.5 all-reduce.5
  211.0 57.9 all-reduce.7
where the time goes:
time: 285 us
  waiting for transfers between devices  155 us (54%)
  matrix products  60.9 us (21%)
  blocking collectives  31 us (11%)
  other arithmetic  16.2 us (6%)
  between operations  14 us (5%)
  starting transfers between devices  5.68 us (2%)
    psum x3, waiting for transfers between devices, body(): summed = lax.psum(partial_value, 'hid')  155 us
    dot_general x3, matrix products, body(): lax.dot_general(hidden_grad, w_in_section, (((1,), (1,)), ((), ())), pref...  34.1 us
    all_gather x3, blocking collectives, body(): lax.all_gather(section_inputs[0, tick_index], 'hid', axis=0, tiled=True)  31 us
    dot_general x3, matrix products, body(): jnp.dot(lax.all_gather(section_inputs[0, tick_index], 'hid', axis=0, tile...  17.3 us
    another operation x9, other arithmetic, body(): lower_factor = jnp.linalg.cholesky(gram_matrix)  6.42 us
  transfers between devices with their start and end apart: 7, of which 3 were waited for; matrix products, arithmetic and copies ran while one was open for 4% of the time, Pallas kernels for 0%

commit v1 on v0

v1 whole, which is shorter than its diff:
```python
import functools

import jax
import jax.numpy as jnp
from jax import lax
from jax.experimental import pallas as pl
from jax.experimental.pallas import tpu as pltpu
from jax.sharding import PartitionSpec as P

F32 = jnp.float32
BF16 = jnp.bfloat16
HIGH = lax.Precision.HIGHEST
VMEM = pl.BlockSpec(memory_space=pltpu.VMEM)
SMEM = pl.BlockSpec(memory_space=pltpu.SMEM)
LIMIT = 8 << 20


def dot(first, second, first_dim, second_dim, precision=None):
    return lax.dot_general(
        first,
        second,
        (((first_dim,), (second_dim,)), ((), ())),
        precision=precision,
        preferred_element_type=F32,
    )


def split(value):
    high = value.astype(BF16)
    low = (value - high.astype(F32)).astype(BF16)
    return jnp.concatenate([high, low], 0)


def chunks(total):
    size = min(total, 1024)
    return [(start, size) for start in range(0, total, size)]


def cotangent_of(left_t, right_t):
    rank = left_t.shape[0]
    lefts, rights = split(left_t), split(right_t)
    first = jnp.concatenate([lefts[:rank], lefts], 0)
    second = jnp.concatenate([rights, rights[:rank]], 0)
    return dot(first, second, 0, 0)


def chosen(place_ref, incoming, other):
    return jnp.where(place_ref[1] == 1, incoming, other)


def on_device(kernel, outs, operands, flops, name, smem=0, scratch=()):
    many = isinstance(outs, list)
    shapes = [jax.ShapeDtypeStruct(*out) for out in (outs if many else [outs])]
    moved = sum(o.size * o.dtype.itemsize for o in operands)
    result = pl.pallas_call(
        kernel,
        out_shape=shapes,
        in_specs=[SMEM] * smem + [VMEM] * (len(operands) - smem),
        out_specs=[VMEM] * len(shapes),
        scratch_shapes=list(scratch),
        compiler_params=pltpu.CompilerParams(vmem_limit_bytes=LIMIT),
        cost_estimate=pl.CostEstimate(
            flops=flops, bytes_accessed=moved // 4, transcendentals=0
        ),
        name=name,
    )(*operands)
    return result if many else result[0]


def up_kernel(place_ref, in_left_ref, in_right_ref, left_ref, right_ref, w_out_ref, up_ref, left_out, right_out):
    left = chosen(place_ref, in_left_ref[0], left_ref[...])
    right = chosen(place_ref, in_right_ref[0], right_ref[...])
    left_out[...] = left
    right_out[...] = right
    cotangent_low = cotangent_of(left, right).astype(BF16)
    for start, size in chunks(w_out_ref.shape[0]):
        up_ref[:, start : start + size] = dot(
            cotangent_low, w_out_ref[start : start + size, :], 1, 1
        ).astype(BF16)


def warm_kernel(warm_ref, w_in_ref, out_ref):
    stacked = split(warm_ref[...])
    rank = warm_ref.shape[0]
    for start, size in chunks(w_in_ref.shape[1]):
        both = dot(stacked, w_in_ref[:, start : start + size], 1, 0)
        out_ref[:, start : start + size] = split(both[:rank] + both[rank:])


def own_term(place_ref, left, right, warm):
    inner = dot(warm, right, 1, 1, HIGH)
    return jnp.where(place_ref[0] == 0, 1.0, 0.0) * dot(inner, left, 1, 0, HIGH)


def place_rows(offsets, place_ref, pieces, rows_ref):
    block = pieces[0].shape[0]
    for offset, piece in zip(offsets, pieces):
        place = 0
        if len(pieces) > 1:
            place = pl.multiple_of(jnp.bitwise_xor(place_ref[0], offset) * block, block)
        rows_ref[pl.ds(place, block), :] = piece[...]


def first_kernel(offsets, place_ref, *refs):
    pieces, rest = refs[: len(offsets)], refs[len(offsets) :]
    w_in_ref, up_ref, warm_in_ref, left_ref, right_ref, warm_ref, hidden_ref, proj_ref, rows_ref = rest
    place_rows(offsets, place_ref, pieces, rows_ref)
    rank = left_ref.shape[0]
    total = None
    for start, size in chunks(w_in_ref.shape[1]):
        preact = dot(rows_ref[...], w_in_ref[:, start : start + size], 1, 0)
        up = up_ref[:, start : start + size]
        hidden = jnp.where(preact > 0, up.astype(F32), 0.0).astype(BF16)
        hidden_ref[:, start : start + size] = hidden
        part = dot(hidden, warm_in_ref[:, start : start + size], 1, 1)
        total = part if total is None else total + part
    turned = total.T
    proj_ref[...] = (
        turned[:rank] + turned[rank:] + own_term(place_ref, left_ref[...], right_ref[...], warm_ref[...])
    )


def mask_kernel(offsets, step, place_ref, *refs):
    pieces, (w_in_ref, mask_ref, rows_ref) = refs[: len(offsets)], refs[len(offsets) :]
    place_rows(offsets, place_ref, [piece.at[step] for piece in pieces], rows_ref)
    for start, size in chunks(w_in_ref.shape[1]):
        preact = dot(rows_ref[...], w_in_ref[:, start : start + size], 1, 0)
        mask_ref[:, start : start + size] = jnp.where(preact > 0, 1.0, 0.0).astype(BF16)


def hidden_kernel(
    tick, place_ref, in_left_ref, in_right_ref, both_ref, warm_ref, w_out_ref, mask_ref, warm_in_ref,
    hidden_ref, proj_ref, left_out, right_out,
):
    rank, rows = left_out.shape
    left = chosen(place_ref, in_left_ref[tick], both_ref[:, :rows])
    right = chosen(place_ref, in_right_ref[tick], both_ref[:, rows:])
    left_out[...] = left
    right_out[...] = right
    cotangent_low = cotangent_of(left, right).astype(BF16)
    total = None
    for start, size in chunks(w_out_ref.shape[0]):
        up = dot(cotangent_low, w_out_ref[start : start + size, :], 1, 1)
        mask = mask_ref[:, start : start + size]
        hidden = jnp.where(mask.astype(F32) > 0, up, 0.0).astype(BF16)
        hidden_ref[:, start : start + size] = hidden
        part = dot(hidden, warm_in_ref[:, start : start + size], 1, 1)
        total = part if total is None else total + part
    turned = total.T
    proj_ref[...] = turned[:rank] + turned[rank:] + own_term(place_ref, left, right, warm_ref[...])


def merged_kernel(place_ref, left_ref, right_ref, hidden_ref, w_in_ref, merged_ref):
    share = jnp.where(place_ref[0] == 0, 1.0, 0.0)
    depth = w_in_ref.shape[0]
    size = min(depth, 256)
    for start in range(0, depth, size):
        here = slice(start, start + size)
        merged_ref[:, here] = dot(hidden_ref[...], w_in_ref[here, :], 1, 1) + share * cotangent_of(
            left_ref[...], right_ref[:, here]
        )


def right_kernel(proj_ref, merged_ref, out_ref):
    stacked = split(proj_ref[...])
    rank = proj_ref.shape[0]
    merged = merged_ref[...]
    high = merged.astype(BF16)
    low = (merged - high.astype(F32)).astype(BF16)
    both = dot(stacked, high, 1, 0) + dot(stacked, low, 1, 0)
    out_ref[...] = both[:rank] + both[rank:]


def factor_kernel(proj_ref, left_ref, inverse_ref):
    proj = proj_ref[...]
    rank = proj.shape[0]
    gram = dot(proj, proj, 1, 1, HIGH)
    line = lax.broadcasted_iota(jnp.int32, (rank, rank), 0)
    column = lax.broadcasted_iota(jnp.int32, (rank, rank), 1)
    eye = jnp.where(line == column, 1.0, 0.0)
    inverse = eye
    for step in range(rank):
        pivot_row = gram[step : step + 1, :]
        pivot = gram[step : step + 1, step : step + 1]
        scale = jnp.where(line[:, :1] > step, gram[:, step : step + 1] / pivot, 0.0)
        inverse = inverse - scale * inverse[step : step + 1, :]
        gram = gram - scale * pivot_row
    pivots = jnp.sum(gram * eye, axis=1, keepdims=True)
    inverse = inverse * lax.rsqrt(pivots)
    inverse_ref[...] = inverse
    left_ref[...] = dot(inverse, proj, 1, 0, HIGH)


def finish_kernel(inverse_ref, left_ref, sums_ref, right_ref, both_ref):
    right = dot(inverse_ref[...], sums_ref[...], 1, 0, HIGH)
    rows = left_ref.shape[1]
    right_ref[...] = right
    both_ref[:, :rows] = left_ref[...]
    both_ref[:, rows:] = right


def outgoing_kernel(place_ref, merged_ref, out_ref):
    block = out_ref.shape[1]
    for chip in range(out_ref.shape[0]):
        start = pl.multiple_of((2 * chip + 1 - place_ref[0] % 2) * block, block)
        out_ref[chip] = merged_ref[pl.ds(start, block), :].astype(BF16)


def pack_kernel(chips, place_ref, merged_ref, arrived_ref, right_ref, right_arrived_ref, own_ref, right_out, *out_refs):
    block = own_ref.shape[0]
    core, chip = place_ref[0] % 2, place_ref[0] // 2
    stacked = split(right_ref[...] + right_arrived_ref[...])
    rank = right_ref.shape[0]
    right_out[...] = stacked[:rank].astype(F32) + stacked[rank:].astype(F32)
    for turn in range(chips):
        target = jnp.bitwise_xor(chip, turn)
        start = pl.multiple_of((2 * target + core) * block, block)
        value = merged_ref[pl.ds(start, block), :] + arrived_ref[target].astype(F32)
        if turn:
            out_refs[turn - 1][:block, :] = value.astype(BF16)
            out_refs[turn - 1][block:, :] = stacked
        else:
            own_ref[...] = value


def last_kernel(inverse_ref, own_ref, right_own_ref, *refs):
    packs, (grads_ref, right_ref) = refs[:-2], refs[-2:]
    block, rank = own_ref.shape[0], inverse_ref.shape[0]
    rows = [own_ref[...]] + [pack[:block, :].astype(F32) for pack in packs]
    sums = [right_own_ref[...]] + [
        pack[block : block + rank, :].astype(F32) + pack[block + rank :, :].astype(F32) for pack in packs
    ]
    grads_ref[...] = tree_sum(rows)
    right_ref[...] = dot(inverse_ref[...], tree_sum(sums), 1, 0, HIGH)


def flip(value, axis, bits):
    count = lax.axis_size(axis)
    return lax.ppermute(value, axis, [(source, source ^ bits) for source in range(count)])


def stages(count):
    found, stride = [], 1
    while stride < count:
        members = 2 if stride == 1 else min(4, count // stride)
        found.append((stride, members))
        stride *= members
    return found


def tree_sum(parts):
    while len(parts) > 1:
        parts = [first + second for first, second in zip(parts[::2], parts[1::2])]
    return parts[0]


def all_sum(value):
    for stride, members in stages(lax.axis_size("hid")):
        value = tree_sum([value] + [flip(value, "hid", stride * k) for k in range(1, members)])
    return value


def gather_pieces(value):
    pieces = {0: value}
    plan = stages(lax.axis_size("hid"))
    for stride, members in plan[1:] + plan[:1]:
        for offset in list(pieces):
            for k in range(1, members):
                pieces[offset ^ (stride * k)] = flip(pieces[offset], "hid", stride * k)
    return list(pieces), list(pieces.values())


def body(section_inputs, w_in, w_out, warm_factor, pending_left, pending_right, incoming_left, incoming_right):
    w_in, w_out, inputs = w_in[0], w_out[0], section_inputs[0]
    ticks, rows_own, depth = inputs.shape
    hidden_units = w_out.shape[0]
    rank = warm_factor.shape[2]
    count, own = lax.axis_size("hid"), lax.axis_index("hid")
    rows = rows_own * count
    sections = lax.axis_size("pipe")
    is_top = lax.axis_index("pipe") == sections - 1
    full = 2 * rows * depth * hidden_units
    turned = lambda value: jnp.swapaxes(value, -1, -2)
    incoming = (turned(incoming_left), turned(incoming_right))
    warm = turned(warm_factor[0])
    places = jnp.stack([own, is_top.astype(own.dtype)]).astype(jnp.int32)
    wide = ((rows, hidden_units), BF16)
    left_form, right_form = ((rank, rows), F32), ((rank, depth), F32)
    chips = count // 2
    direct = stages(count) == [(1, 2), (2, chips)]

    if rows_own % 16 == 0:
        offsets, pieces = gather_pieces(inputs[0])
        _, later = gather_pieces(inputs[1:])
    else:
        gathered = lax.all_gather(inputs, "hid", axis=1, tiled=True)
        offsets, pieces, later = [0], [gathered[0]], [gathered[1:]]
    up, left, right = on_device(
        up_kernel,
        [wide, left_form, right_form],
        (places, *incoming, turned(pending_left[0]), turned(pending_right[0]), w_out),
        full,
        "up",
        1,
    )

    for tick in range(ticks):
        last = tick + 1 == ticks
        warm_in = on_device(
            warm_kernel, ((2 * rank, hidden_units), BF16), (warm, w_in), full // 2, "warm"
        )
        scratch = [pltpu.VMEM((rows, depth), BF16)]
        if tick == 0:
            hidden, proj = on_device(
                functools.partial(first_kernel, offsets),
                [wide, left_form],
                (places, *pieces, w_in, up, warm_in, left, right, warm),
                full,
                "first",
                1,
                scratch,
            )
        else:
            mask = on_device(
                functools.partial(mask_kernel, offsets, tick - 1),
                wide,
                (places, *later, w_in),
                full,
                "mask",
                1,
                scratch,
            )
            hidden, proj, left, right = on_device(
                functools.partial(hidden_kernel, tick),
                [wide, left_form, left_form, right_form],
                (places, *incoming, both, warm, w_out, mask, warm_in),
                full,
                "hidden",
                1,
            )
        merged = on_device(
            merged_kernel, ((rows, depth), F32), (places, left, right, hidden, w_in), full, "merged", 1
        )
        if last and direct:
            outgoing = on_device(
                outgoing_kernel, ((chips, rows_own, depth), BF16), (places, merged), full // 16, "outgoing", 1
            )
            arrived = flip(outgoing, "hid", 1)
        proj = all_sum(proj)
        partial_right = on_device(
            right_kernel, right_form, (proj, merged), full // 16, "right"
        )
        left_new, inverse = on_device(
            factor_kernel, [left_form, ((rank, rank), F32)], (proj,), full // 2, "factor"
        )
        if last and direct:
            packed = ((rows_own + 2 * rank, depth), BF16)
            own_rows, own_right, *packs = on_device(
                functools.partial(pack_kernel, chips),
                [((rows_own, depth), F32), right_form] + [packed] * (chips - 1),
                (places, merged, arrived, partial_right, flip(partial_right, "hid", 1)),
                full // 16,
                "pack",
                1,
            )
            packs = [flip(pack, "hid", 2 * k) for k, pack in enumerate(packs, 1)]
            grads, warm = on_device(
                last_kernel,
                [((rows_own, depth), F32), right_form],
                (inverse, own_rows, own_right, *packs),
                full // 16,
                "last",
            )
            break
        if last:
            grads = lax.psum_scatter(merged, "hid", scatter_dimension=0, tiled=True)
        warm, both = on_device(
            finish_kernel,
            [right_form, ((rank, rows + depth), F32)],
            (inverse, left_new, all_sum(partial_right)),
            full // 16,
            "finish",
        )
        if not last:
            both = lax.ppermute(both, "pipe", [(source, source - 1) for source in range(1, sections)])
    left_rows = lax.dynamic_slice_in_dim(left_new, own * rows_own, rows_own, 1)
    return grads[None], turned(left_rows)[None], turned(warm)[None]


def solution(mesh):
    placed = (
        P("pipe", None, "hid", None),
        P("pipe", None, "hid"),
        P("pipe", "hid", None),
        P("pipe", None, None),
        P("pipe", None, None),
        P("pipe", None, None),
        P(),
        P(),
    )
    return jax.shard_map(
        body,
        mesh=mesh,
        in_specs=placed,
        out_specs=(P("pipe", "hid", None), P("pipe", "hid", None), P("pipe", None, None)),
        check_vma=False,
    )
```

time: 285 us -> 106 us (0.37)
  waiting for transfers between devices: 155 us -> 17.9 us
  matrix products: 60.9 us -> 0 us
  Pallas kernels: 0 us -> 42.6 us
  blocking collectives: 31 us -> 0 us
  starting transfers between devices: 5.68 us -> 35.2 us
  other arithmetic: 16.2 us -> 0.19 us
  between operations: 14 us -> 0.98 us
  local copies, waits for them, and re-layouts: 2.54 us -> 9.15 us
    psum x3 -> x0, waiting for transfers between devices: 155 us -> none  [body(): summed = lax.psum(partial_value, 'hid')]
    dot_general x18 -> x0, matrix products: 60.3 us -> none  [the longest x3 34.1 us: body(): lax.dot_general(hidden_grad, w_in_section, (((1,), (1,)), ((), ())), pref...]
    pallas_call x0 -> x23, Pallas kernels: none -> 42.6 us  [on_device(): pl.pallas_call(kernel, out_shape=shapes, in_specs=[SMEM] * smem + [VMEM]...]
    all_gather x3 -> x0, blocking collectives: 31 us -> none  [body(): lax.all_gather(section_inputs[0, tick_index], 'hid', axis=0, tiled=True)]
    ppermute x4 -> x41, starting transfers between devices: 5.56 us -> 35.2 us  [the longest x39 32.2 us: flip(): lax.ppermute(value, axis, [(source, source ^ bits) for source in range(co...]
    ppermute x4 -> x41, waiting for transfers between devices: 0.01 us -> 17.9 us  [the longest x39 11.1 us: flip(): lax.ppermute(value, axis, [(source, source ^ bits) for source in range(co...]
    another operation x15 -> x1, other arithmetic: 12.1 us -> 0.07 us  [body(): places = jnp.stack([own, is_top.astype(own.dtype)]).astype(jnp.int32)]
    unnamed x10 -> x22, local copies, waits for them, and re-layouts: 0.02 us -> 6.69 us
  transfers between devices with their start and end apart: 7 -> 41, of which waited for: 3 -> 10; matrix products, arithmetic and copies ran while one was open for 4% -> 2% of each run, Pallas kernels for 0% -> 30%
where the time goes in v1:
time: 106 us
  Pallas kernels  42.6 us (40%)
  starting transfers between devices  35.2 us (33%)
  waiting for transfers between devices  17.9 us (17%)
  local copies, waits for them, and re-layouts  9.15 us (9%)
    pallas_call x23, Pallas kernels, on_device(): pl.pallas_call(kernel, out_shape=shapes, in_specs=[SMEM] * smem + [VMEM]...  42.6 us
    ppermute x39, starting transfers between devices, flip(): lax.ppermute(value, axis, [(source, source ^ bits) for source in range(co...  32.2 us
    ppermute x39, waiting for transfers between devices, flip(): lax.ppermute(value, axis, [(source, source ^ bits) for source in range(co...  11.1 us
    ppermute x2, waiting for transfers between devices, body(): lax.ppermute(both, 'pipe', [(source, source - 1) for source in range(1, s...  6.76 us
    unnamed x22, local copies, waits for them, and re-layouts  6.69 us
    ppermute x2, starting transfers between devices, body(): lax.ppermute(both, 'pipe', [(source, source - 1) for source in range(1, s...  3 us
  transfers between devices with their start and end apart: 41, of which 10 were waited for; matrix products, arithmetic and copies ran while one was open for 2% of the time, Pallas kernels for 30%

profile of v1, /device:TPU:0, one launch (start us, length us, event | category | flops | bytes accessed | tf_op | source)
XLA Modules:
  0.0 106.0 jit_solution(5673051743007389924)
XLA Ops:
  0.6 0.8 slice_bitcast_fusion.1.refs_0_
  1.5 2.9 %collective-permute-start = (bf16[32,1024]{1,0:T(8,128)(2,1)S(1)}, bf16[32,1024]{1,0:T(8,128)(2,1)S(1)}, u32[]{:S(2)}, u32[]{:S(2)}) collective-permute-start(bf16[32,1024]{1,0:T(8,128)(2,1)S(1)} %slice_bitcast_fusion.1.refs_0_), channel_id=1, source_target_pairs={{0,2},{1,3},{2,0},{3,1},{4,6},{5,7},{6,4},{7,5},{8,10},{9,11},{10,... | collective-permute-start | bytes 196616 | tf_op jit(solution)/shard_map/ppermute | solution.py:239
  4.4 1.5 %collective-permute-start.1 = (bf16[32,1024]{1,0:T(8,128)(2,1)S(1)}, bf16[32,1024]{1,0:T(8,128)(2,1)S(1)}, u32[]{:S(2)}, u32[]{:S(2)}) collective-permute-start(bf16[32,1024]{1,0:T(8,128)(2,1)S(1)} %slice_bitcast_fusion.1.refs_0_), channel_id=1, source_target_pairs={{0,4},{1,5},{2,6},{3,7},{4,0},{5,1},{6,2},{7,3},{8,12},{9,13},{10,... | collective-permute-start | bytes 196616 | tf_op jit(solution)/shard_map/ppermute | solution.py:239
  5.9 0.9 slice_bitcast_fusion.refs_0_
  6.9 2.0 %collective-permute-start.16 = (bf16[2,32,1024]{2,1,0:T(8,128)(2,1)S(1)}, bf16[2,32,1024]{2,1,0:T(8,128)(2,1)S(1)}, u32[]{:S(2)}, u32[]{:S(2)}) collective-permute-start(bf16[2,32,1024]{2,1,0:T(8,128)(2,1)S(1)} %slice_bitcast_fusion.refs_0_), channel_id=1, source_target_pairs={{0,2},{1,3},{2,0},{3,1},{4,6},{5,7},{6,4},{7,5},{8,10},{9,11},{10,... | collective-permute-start | bytes 393224 | tf_op jit(solution)/shard_map/ppermute | solution.py:239
  9.0 3.4 %copy-done.1 = bf16[1,4096,1024]{2,1,0:T(8,128)(2,1)S(1)} copy-done((bf16[1,4096,1024]{2,1,0:T(8,128)(2,1)S(1)}, bf16[1,4096,1024]{2,1,0:T(8,128)(2,1)}, u32[]{:S(2)}) %copy-start.1) | copy-done | bytes 8388632
  12.3 0.9 copy-done.2
  13.3 0.8 copy-done.4
  14.1 0.8 copy-done.7
  14.9 0.7 copy-done.8
  15.6 3.1 %up.1 = (bf16[256,4096]{1,0:T(8,128)(2,1)S(1)}, f32[16,256]{1,0:T(8,128)S(1)}, f32[16,1024]{1,0:T(8,128)S(1)}) custom-call(s32[2]{0:T(128)S(1)} %pad_add_fusion.place_ref, f32[3,16,256]{2,1,0:T(8,128)S(1)} %bitcast.44, f32[3,16,1024]{2,1,0:T(8,128)S(1)} %bitcast.41, f32[16,256]{1,0:T(8,128)S(1)} %bitcast.50, f32[16,1024]{1,0:T(8,128)S(1)} %bitcast.49, ...), custom_call_target="tpu_custom_call" | custom-call | flops 2147483648 | bytes 2179074 | tf_op jit(solution)/shard_map/up/pallas_call | solution.py:55
  19.5 1.4 %warm.3.refs_10_ = bf16[32,4096]{1,0:T(8,128)(2,1)S(1)} custom-call(f32[16,1024]{1,0:T(8,128)S(1)} %bitcast.47, bf16[1024,4096]{1,0:T(8,128)(2,1)S(1)} %bitcast.27), custom_call_target="tpu_custom_call" | custom-call | flops 1073741824 | bytes 2113536 | tf_op jit(solution)/shard_map/warm/pallas_call | solution.py:55
  21.0 4.0 %first.1 = (bf16[256,4096]{1,0:T(8,128)(2,1)S(1)}, f32[16,256]{1,0:T(8,128)S(1)}) custom-call(s32[2]{0:T(128)S(1)} %pad_add_fusion.place_ref, bf16[32,1024]{1,0:T(8,128)(2,1)S(1)} %slice_bitcast_fusion.1.refs_0_, bf16[32,1024]{1,0:T(8,128)(2,1)S(1)} %collective-permute-done.refs_1_, bf16[32,1024]{1,0:T(8,128)(2,1)S(1)} %collective-permute-done.1.refs_2_, ...), custom_call_target="tpu_custom_call" | custom-call | flops 2147483648 | bytes 2854914 | tf_op jit(solution)/shard_map/first/pallas_call | solution.py:55
  25.0 0.3 collective-permute-start.7
  25.4 1.5 %collective-permute-start.17 = (bf16[2,32,1024]{2,1,0:T(8,128)(2,1)S(1)}, bf16[2,32,1024]{2,1,0:T(8,128)(2,1)S(1)}, u32[]{:S(2)}, u32[]{:S(2)}) collective-permute-start(bf16[2,32,1024]{2,1,0:T(8,128)(2,1)S(1)} %slice_bitcast_fusion.refs_0_), channel_id=1, source_target_pairs={{0,4},{1,5},{2,6},{3,7},{4,0},{5,1},{6,2},{7,3},{8,12},{9,13},{10,... | collective-permute-start | bytes 393224 | tf_op jit(solution)/shard_map/ppermute | solution.py:239
  26.9 2.9 %collective-permute-start.10 = (f32[16,256]{1,0:T(8,128)S(1)}, f32[16,256]{1,0:T(8,128)S(1)}, u32[]{:S(2)}, u32[]{:S(2)}) collective-permute-start(f32[16,256]{1,0:T(8,128)S(1)} %add.63), channel_id=1, source_target_pairs={{0,6},{1,7},{2,4},{3,5},{4,2},{5,3},{6,0},{7,1},{8,14},{9,15},{10,... | collective-permute-start | bytes 49160 | tf_op jit(solution)/shard_map/ppermute | solution.py:239
  29.9 0.5 collective-permute-start.8
  30.5 3.0 %merged.3.merged_ref = f32[256,1024]{1,0:T(8,128)S(1)} custom-call(s32[2]{0:T(128)S(1)} %pad_add_fusion.place_ref, f32[16,256]{1,0:T(8,128)S(1)} %get-tuple-element.34.refs_11_.left_ref, f32[16,1024]{1,0:T(8,128)S(1)} %get-tuple-element.35.refs_12_.right_ref, bf16[256,4096]{1,0:T(8,128)(2,1)S(1)} %get-tuple-element.39.hidden_ref, bf16[1024,4096]{1,0:T(8,128)(2,1)S(1)} %bitcast.29), custom_call_target="tpu_custom_call" | custom-call | flops 2147483648 | bytes 2641922 | tf_op jit(solution)/shard_map/merged/pallas_call | solution.py:55
  33.5 0.8 collective-permute-done.17.refs_2_
  34.3 0.5 collective-permute-start.20
  34.9 0.4 collective-permute-start.22
  35.4 0.3 right.3
  35.8 1.6 %factor.3 = (f32[16,256]{1,0:T(8,128)S(1)}, f32[16,16]{1,0:T(8,128)S(1)}) custom-call(f32[16,256]{1,0:T(8,128)S(1)} %add_add_fusion.4.proj_ref), custom_call_target="tpu_custom_call" | custom-call | flops 1073741824 | bytes 4096 | tf_op jit(solution)/shard_map/factor/pallas_call | solution.py:55
  37.4 1.3 %collective-permute-start.12 = (f32[16,1024]{1,0:T(8,128)S(1)}, f32[16,1024]{1,0:T(8,128)S(1)}, u32[]{:S(2)}, u32[]{:S(2)}) collective-permute-start(f32[16,1024]{1,0:T(8,128)S(1)} %add.67), channel_id=1, source_target_pairs={{0,2},{1,3},{2,0},{3,1},{4,6},{5,7},{6,4},{7,5},{8,10},{9,11},{10,... | collective-permute-start | bytes 196616 | tf_op jit(solution)/shard_map/ppermute | solution.py:239
  38.7 1.5 %collective-permute-start.13 = (f32[16,1024]{1,0:T(8,128)S(1)}, f32[16,1024]{1,0:T(8,128)S(1)}, u32[]{:S(2)}, u32[]{:S(2)}) collective-permute-start(f32[16,1024]{1,0:T(8,128)S(1)} %add.67), channel_id=1, source_target_pairs={{0,4},{1,5},{2,6},{3,7},{4,0},{5,1},{6,2},{7,3},{8,12},{9,13},{10,... | collective-permute-start | bytes 196616 | tf_op jit(solution)/shard_map/ppermute | solution.py:239
  40.2 0.8 collective-permute-start.14
  40.9 3.0 %mask.2.mask_ref = bf16[256,4096]{1,0:T(8,128)(2,1)S(1)} custom-call(s32[2]{0:T(128)S(1)} %pad_add_fusion.place_ref, bf16[2,32,1024]{2,1,0:T(8,128)(2,1)S(1)} %slice_bitcast_fusion.refs_0_, bf16[2,32,1024]{2,1,0:T(8,128)(2,1)S(1)} %collective-permute-done.16.refs_1_, bf16[2,32,1024]{2,1,0:T(8,128)(2,1)S(1)} %collective-permute-done.17.refs_2_, ...), custom_call_target="tpu_custom_call" | custom-call | flops 2147483648 | bytes 2359298 | tf_op jit(solution)/shard_map/mask/pallas_call | solution.py:55
  43.9 1.4 %collective-permute-done.14 = f32[16,1024]{1,0:T(8,128)S(1)} collective-permute-done((f32[16,1024]{1,0:T(8,128)S(1)}, f32[16,1024]{1,0:T(8,128)S(1)}, u32[]{:S(2)}, u32[]{:S(2)}) %collective-permute-start.14) | collective-permute-done | bytes 65568 | tf_op jit(solution)/shard_map/ppermute | solution.py:239
  45.5 1.5 %collective-permute-start.15 = (f32[16,1280]{1,0:T(8,128)S(1)}, f32[16,1280]{1,0:T(8,128)S(1)}, u32[]{:S(2)}, u32[]{:S(2)}) collective-permute-start(f32[16,1280]{1,0:T(8,128)S(1)} %get-tuple-element.40), channel_id=1, source_target_pairs={{8,0},{16,8},{24,16},{9,1},{17,9},{25,17},{10,2},{18,10},{26,18},{... | collective-permute-start | bytes 245768 | tf_op jit(solution)/shard_map/ppermute | solution.py:385
  47.1 1.4 %warm.4.warm_in_ref = bf16[32,4096]{1,0:T(8,128)(2,1)S(1)} custom-call(f32[16,1024]{1,0:T(8,128)S(1)} %get-tuple-element.41.warm_ref, bf16[1024,4096]{1,0:T(8,128)(2,1)S(1)} %bitcast.31), custom_call_target="tpu_custom_call" | custom-call | flops 1073741824 | bytes 2113536 | tf_op jit(solution)/shard_map/warm/pallas_call | solution.py:55
  48.5 3.4 %collective-permute-done.15.both_ref = f32[16,1280]{1,0:T(8,128)S(1)} collective-permute-done((f32[16,1280]{1,0:T(8,128)S(1)}, f32[16,1280]{1,0:T(8,128)S(1)}, u32[]{:S(2)}, u32[]{:S(2)}) %collective-permute-start.15) | collective-permute-done | bytes 81952 | tf_op jit(solution)/shard_map/ppermute | solution.py:385
  51.9 4.1 %hidden.2 = (bf16[256,4096]{1,0:T(8,128)(2,1)S(1)}, f32[16,256]{1,0:T(8,128)S(1)}, f32[16,256]{1,0:T(8,128)S(1)}, f32[16,1024]{1,0:T(8,128)S(1)}) custom-call(s32[2]{0:T(128)S(1)} %pad_add_fusion.place_ref, f32[3,16,256]{2,1,0:T(8,128)S(1)} %bitcast.45, f32[3,16,1024]{2,1,0:T(8,128)S(1)} %bitcast.42, f32[16,1280]{1,0:T(8,128)S(1)} %collective-permute-done.15.both_ref, ...), custom_call_target="tpu_custom_call" | custom-call | flops 2147483648 | bytes 2785282 | tf_op jit(solution)/shard_map/hidden/pallas_call | solution.py:55
  56.1 1.2 %collective-permute-done.23 = f32[16,256]{1,0:T(8,128)S(1)} collective-permute-done((f32[16,256]{1,0:T(8,128)S(1)}, f32[16,256]{1,0:T(8,128)S(1)}, u32[]{:S(2)}, u32[]{:S(2)}) %collective-permute-start.23) | collective-permute-done | bytes 16416 | tf_op jit(solution)/shard_map/ppermute | solution.py:239
  57.3 0.8 collective-permute-start.24
  58.1 0.5 collective-permute-start.25
  58.6 2.1 %collective-permute-start.26 = (f32[16,256]{1,0:T(8,128)S(1)}, f32[16,256]{1,0:T(8,128)S(1)}, u32[]{:S(2)}, u32[]{:S(2)}) collective-permute-start(f32[16,256]{1,0:T(8,128)S(1)} %add.71), channel_id=1, source_target_pairs={{0,6},{1,7},{2,4},{3,5},{4,2},{5,3},{6,0},{7,1},{8,14},{9,15},{10,... | collective-permute-start | bytes 49160 | tf_op jit(solution)/shard_map/ppermute | solution.py:239
  60.8 3.0 %merged.4.merged_ref = f32[256,1024]{1,0:T(8,128)S(1)} custom-call(s32[2]{0:T(128)S(1)} %pad_add_fusion.place_ref, f32[16,256]{1,0:T(8,128)S(1)} %get-tuple-element.45.left_ref, f32[16,1024]{1,0:T(8,128)S(1)} %get-tuple-element.46.right_ref, bf16[256,4096]{1,0:T(8,128)(2,1)S(1)} %get-tuple-element.47.hidden_ref, bf16[1024,4096]{1,0:T(8,128)(2,1)S(1)} %bitcast.32), custom_call_target="tpu_custom_call" | custom-call | flops 2147483648 | bytes 2641922 | tf_op jit(solution)/shard_map/merged/pallas_call | solution.py:55
  64.2 3.0 %mask.3.mask_ref = bf16[256,4096]{1,0:T(8,128)(2,1)S(1)} custom-call(s32[2]{0:T(128)S(1)} %pad_add_fusion.place_ref, bf16[2,32,1024]{2,1,0:T(8,128)(2,1)S(1)} %slice_bitcast_fusion.refs_0_, bf16[2,32,1024]{2,1,0:T(8,128)(2,1)S(1)} %collective-permute-done.16.refs_1_, bf16[2,32,1024]{2,1,0:T(8,128)(2,1)S(1)} %collective-permute-done.17.refs_2_, ...), custom_call_target="tpu_custom_call" | custom-call | flops 2147483648 | bytes 2359298 | tf_op jit(solution)/shard_map/mask/pallas_call | solution.py:55
  67.2 0.9 collective-permute-start.28
  68.1 1.3 %collective-permute-start.29 = (f32[16,1024]{1,0:T(8,128)S(1)}, f32[16,1024]{1,0:T(8,128)S(1)}, u32[]{:S(2)}, u32[]{:S(2)}) collective-permute-start(f32[16,1024]{1,0:T(8,128)S(1)} %add.75), channel_id=1, source_target_pairs={{0,4},{1,5},{2,6},{3,7},{4,0},{5,1},{6,2},{7,3},{8,12},{9,13},{10,... | collective-permute-start | bytes 196616 | tf_op jit(solution)/shard_map/ppermute | solution.py:239
  69.4 1.4 %collective-permute-start.30 = (f32[16,1024]{1,0:T(8,128)S(1)}, f32[16,1024]{1,0:T(8,128)S(1)}, u32[]{:S(2)}, u32[]{:S(2)}) collective-permute-start(f32[16,1024]{1,0:T(8,128)S(1)} %add.75), channel_id=1, source_target_pairs={{0,6},{1,7},{2,4},{3,5},{4,2},{5,3},{6,0},{7,1},{8,14},{9,15},{10,... | collective-permute-start | bytes 196616 | tf_op jit(solution)/shard_map/ppermute | solution.py:239
  70.7 1.6 %factor.4 = (f32[16,256]{1,0:T(8,128)S(1)}, f32[16,16]{1,0:T(8,128)S(1)}) custom-call(f32[16,256]{1,0:T(8,128)S(1)} %add_add_fusion.3.proj_ref), custom_call_target="tpu_custom_call" | custom-call | flops 1073741824 | bytes 4096 | tf_op jit(solution)/shard_map/factor/pallas_call | solution.py:55
  72.3 2.2 %collective-permute-done.30 = f32[16,1024]{1,0:T(8,128)S(1)} collective-permute-done((f32[16,1024]{1,0:T(8,128)S(1)}, f32[16,1024]{1,0:T(8,128)S(1)}, u32[]{:S(2)}, u32[]{:S(2)}) %collective-permute-start.30) | collective-permute-done | bytes 65568 | tf_op jit(solution)/shard_map/ppermute | solution.py:239
  74.7 1.5 %collective-permute-start.31 = (f32[16,1280]{1,0:T(8,128)S(1)}, f32[16,1280]{1,0:T(8,128)S(1)}, u32[]{:S(2)}, u32[]{:S(2)}) collective-permute-start(f32[16,1280]{1,0:T(8,128)S(1)} %get-tuple-element.48), channel_id=1, source_target_pairs={{8,0},{16,8},{24,16},{9,1},{17,9},{25,17},{10,2},{18,10},{26,18},{... | collective-permute-start | bytes 245768 | tf_op jit(solution)/shard_map/ppermute | solution.py:385
  76.3 1.4 %warm.5.warm_in_ref = bf16[32,4096]{1,0:T(8,128)(2,1)S(1)} custom-call(f32[16,1024]{1,0:T(8,128)S(1)} %get-tuple-element.49.warm_ref, bf16[1024,4096]{1,0:T(8,128)(2,1)S(1)} %bitcast.34), custom_call_target="tpu_custom_call" | custom-call | flops 1073741824 | bytes 2113536 | tf_op jit(solution)/shard_map/warm/pallas_call | solution.py:55
  77.7 3.4 %collective-permute-done.31.both_ref = f32[16,1280]{1,0:T(8,128)S(1)} collective-permute-done((f32[16,1280]{1,0:T(8,128)S(1)}, f32[16,1280]{1,0:T(8,128)S(1)}, u32[]{:S(2)}, u32[]{:S(2)}) %collective-permute-start.31) | collective-permute-done | bytes 81952 | tf_op jit(solution)/shard_map/ppermute | solution.py:385
  81.1 4.1 %hidden.3 = (bf16[256,4096]{1,0:T(8,128)(2,1)S(1)}, f32[16,256]{1,0:T(8,128)S(1)}, f32[16,256]{1,0:T(8,128)S(1)}, f32[16,1024]{1,0:T(8,128)S(1)}) custom-call(s32[2]{0:T(128)S(1)} %pad_add_fusion.place_ref, f32[3,16,256]{2,1,0:T(8,128)S(1)} %bitcast.46, f32[3,16,1024]{2,1,0:T(8,128)S(1)} %bitcast.43, f32[16,1280]{1,0:T(8,128)S(1)} %collective-permute-done.31.both_ref, ...), custom_call_target="tpu_custom_call" | custom-call | flops 2147483648 | bytes 2785282 | tf_op jit(solution)/shard_map/hidden/pallas_call | solution.py:55
  85.3 1.2 %collective-permute-done.32 = f32[16,256]{1,0:T(8,128)S(1)} collective-permute-done((f32[16,256]{1,0:T(8,128)S(1)}, f32[16,256]{1,0:T(8,128)S(1)}, u32[]{:S(2)}, u32[]{:S(2)}) %collective-permute-start.32) | collective-permute-done | bytes 16416 | tf_op jit(solution)/shard_map/ppermute | solution.py:239
  86.4 0.8 collective-permute-start.33
  87.3 1.1 %collective-permute-start.34 = (f32[16,256]{1,0:T(8,128)S(1)}, f32[16,256]{1,0:T(8,128)S(1)}, u32[]{:S(2)}, u32[]{:S(2)}) collective-permute-start(f32[16,256]{1,0:T(8,128)S(1)} %add.79), channel_id=1, source_target_pairs={{0,4},{1,5},{2,6},{3,7},{4,0},{5,1},{6,2},{7,3},{8,12},{9,13},{10,... | collective-permute-start | bytes 49160 | tf_op jit(solution)/shard_map/ppermute | solution.py:239
  88.4 1.6 %collective-permute-start.35 = (f32[16,256]{1,0:T(8,128)S(1)}, f32[16,256]{1,0:T(8,128)S(1)}, u32[]{:S(2)}, u32[]{:S(2)}) collective-permute-start(f32[16,256]{1,0:T(8,128)S(1)} %add.79), channel_id=1, source_target_pairs={{0,6},{1,7},{2,4},{3,5},{4,2},{5,3},{6,0},{7,1},{8,14},{9,15},{10,... | collective-permute-start | bytes 49160 | tf_op jit(solution)/shard_map/ppermute | solution.py:239
  89.9 3.0 %merged.5.merged_ref = f32[256,1024]{1,0:T(8,128)S(1)} custom-call(s32[2]{0:T(128)S(1)} %pad_add_fusion.place_ref, f32[16,256]{1,0:T(8,128)S(1)} %get-tuple-element.52.left_ref, f32[16,1024]{1,0:T(8,128)S(1)} %get-tuple-element.53.right_ref, bf16[256,4096]{1,0:T(8,128)(2,1)S(1)} %get-tuple-element.54.hidden_ref, bf16[1024,4096]{1,0:T(8,128)(2,1)S(1)} %bitcast.35), custom_call_target="tpu_custom_call" | custom-call | flops 2147483648 | bytes 2641922 | tf_op jit(solution)/shard_map/merged/pallas_call | solution.py:55
  93.0 0.6 outgoing.1
  94.0 0.5 collective-permute-start.37
  94.5 0.9 collective-permute-done.37.right_arrived_ref
  95.4 0.6 pack.1
  96.0 0.9 collective-permute-start.38
  96.9 1.1 %collective-permute-start.39 = (bf16[64,1024]{1,0:T(8,128)(2,1)S(1)}, bf16[64,1024]{1,0:T(8,128)(2,1)S(1)}, u32[]{:S(2)}, u32[]{:S(2)}) collective-permute-start(bf16[64,1024]{1,0:T(8,128)(2,1)S(1)} %get-tuple-element.58), channel_id=1, source_target_pairs={{0,4},{1,5},{2,6},{3,7},{4,0},{5,1},{6,2},{7,3},{8,12},{9,13},{10,... | collective-permute-start | bytes 393224 | tf_op jit(solution)/shard_map/ppermute | solution.py:239
  98.0 1.6 %collective-permute-start.40 = (bf16[64,1024]{1,0:T(8,128)(2,1)S(1)}, bf16[64,1024]{1,0:T(8,128)(2,1)S(1)}, u32[]{:S(2)}, u32[]{:S(2)}) collective-permute-start(bf16[64,1024]{1,0:T(8,128)(2,1)S(1)} %get-tuple-element.59), channel_id=1, source_target_pairs={{0,6},{1,7},{2,4},{3,5},{4,2},{5,3},{6,0},{7,1},{8,14},{9,15},{10,... | collective-permute-start | bytes 393224 | tf_op jit(solution)/shard_map/ppermute | solution.py:239
  99.5 1.6 %factor.5 = (f32[16,256]{1,0:T(8,128)S(1)}, f32[16,16]{1,0:T(8,128)S(1)}) custom-call(f32[16,256]{1,0:T(8,128)S(1)} %add_add_fusion.2.proj_ref), custom_call_target="tpu_custom_call" | custom-call | flops 1073741824 | bytes 4096 | tf_op jit(solution)/shard_map/factor/pallas_call | solution.py:55
  101.1 0.7 dynamic-slice_bitcast_fusion
  101.8 0.6 collective-permute-done.38.refs_0_
  102.4 2.8 %collective-permute-done.39.refs_1_ = bf16[64,1024]{1,0:T(8,128)(2,1)S(1)} collective-permute-done((bf16[64,1024]{1,0:T(8,128)(2,1)S(1)}, bf16[64,1024]{1,0:T(8,128)(2,1)S(1)}, u32[]{:S(2)}, u32[]{:S(2)}) %collective-permute-start.39) | collective-permute-done | bytes 131104 | tf_op jit(solution)/shard_map/ppermute | solution.py:239
  105.2 0.9 last.1
  (78 shorter events, 2.7 us)
Async XLA Ops:
  1.5 17.2 %collective-permute-start = (bf16[32,1024]{1,0:T(8,128)(2,1)S(1)}, bf16[32,1024]{1,0:T(8,128)(2,1)S(1)}, u32[]{:S(2)}, u32[]{:S(2)}) collective-permute-start(bf16[32,1024]{1,0:T(8,128)(2,1)S(1)} %slice_bitcast_fusion.1.refs_0_), channel_id=1, source_target_pairs={{0,2},{1,3},{2,0},{3,1},{4,6},{5,7},{6,4},{7,5},{8,10},{9,11},{10,... | collective-permute-start | bytes 196616 | tf_op jit(solution)/shard_map/ppermute | solution.py:239
  4.4 14.6 %collective-permute-start.1 = (bf16[32,1024]{1,0:T(8,128)(2,1)S(1)}, bf16[32,1024]{1,0:T(8,128)(2,1)S(1)}, u32[]{:S(2)}, u32[]{:S(2)}) collective-permute-start(bf16[32,1024]{1,0:T(8,128)(2,1)S(1)} %slice_bitcast_fusion.1.refs_0_), channel_id=1, source_target_pairs={{0,4},{1,5},{2,6},{3,7},{4,0},{5,1},{6,2},{7,3},{8,12},{9,13},{10,... | collective-permute-start | bytes 196616 | tf_op jit(solution)/shard_map/ppermute | solution.py:239
  5.9 13.4 %collective-permute-start.2 = (bf16[32,1024]{1,0:T(8,128)(2,1)S(1)}, bf16[32,1024]{1,0:T(8,128)(2,1)S(1)}, u32[]{:S(2)}, u32[]{:S(2)}) collective-permute-start(bf16[32,1024]{1,0:T(8,128)(2,1)S(1)} %slice_bitcast_fusion.1.refs_0_), channel_id=1, source_target_pairs={{0,6},{1,7},{2,4},{3,5},{4,2},{5,3},{6,0},{7,1},{8,14},{9,15},{10,... | collective-permute-start | bytes 196616 | tf_op jit(solution)/shard_map/ppermute | solution.py:239
  5.9 15.1 %collective-permute-start.3 = (bf16[32,1024]{1,0:T(8,128)(2,1)S(1)}, bf16[32,1024]{1,0:T(8,128)(2,1)S(1)}, u32[]{:S(2)}, u32[]{:S(2)}) collective-permute-start(bf16[32,1024]{1,0:T(8,128)(2,1)S(1)} %slice_bitcast_fusion.1.refs_0_), channel_id=1, source_target_pairs={{0,1},{1,0},{2,3},{3,2},{4,5},{5,4},{6,7},{7,6},{8,9},{9,8},{10,11... | collective-permute-start | bytes 196616 | tf_op jit(solution)/shard_map/ppermute | solution.py:239
  6.9 23.6 %collective-permute-start.16 = (bf16[2,32,1024]{2,1,0:T(8,128)(2,1)S(1)}, bf16[2,32,1024]{2,1,0:T(8,128)(2,1)S(1)}, u32[]{:S(2)}, u32[]{:S(2)}) collective-permute-start(bf16[2,32,1024]{2,1,0:T(8,128)(2,1)S(1)} %slice_bitcast_fusion.refs_0_), channel_id=1, source_target_pairs={{0,2},{1,3},{2,0},{3,1},{4,6},{5,7},{6,4},{7,5},{8,10},{9,11},{10,... | collective-permute-start | bytes 393224 | tf_op jit(solution)/shard_map/ppermute | solution.py:239
  9.0 3.4 %copy-start.1 = (bf16[1,4096,1024]{2,1,0:T(8,128)(2,1)S(1)}, bf16[1,4096,1024]{2,1,0:T(8,128)(2,1)}, u32[]{:S(2)}) copy-start(bf16[1,4096,1024]{2,1,0:T(8,128)(2,1)} %param.10) | copy-start | bytes 25165828
  12.3 0.9 copy-start.2
  13.3 0.8 copy-start.4
  14.1 0.8 copy-start.7
  14.9 0.7 copy-start.8
  15.6 3.9 %copy-start = (bf16[1,1024,4096]{2,1,0:T(8,128)(2,1)S(1)}, bf16[1,1024,4096]{2,1,0:T(8,128)(2,1)}, u32[]{:S(2)}) copy-start(bf16[1,1024,4096]{2,1,0:T(8,128)(2,1)} %param.9) | copy-start | bytes 25165828
  15.6 3.9 %copy-start.6 = (f32[1,1024,16]{1,2,0:T(8,128)S(1)}, f32[1,1024,16]{1,2,0:T(8,128)}, u32[]{:S(2)}) copy-start(f32[1,1024,16]{1,2,0:T(8,128)} %param.11) | copy-start | bytes 196612
  18.7 2.3 %collective-permute-start.4 = (bf16[32,1024]{1,0:T(8,128)(2,1)S(1)}, bf16[32,1024]{1,0:T(8,128)(2,1)S(1)}, u32[]{:S(2)}, u32[]{:S(2)}) collective-permute-start(bf16[32,1024]{1,0:T(8,128)(2,1)S(1)} %collective-permute-done.refs_1_), channel_id=1, source_target_pairs={{0,1},{1,0},{2,3},{3,2},{4,5},{5,4},{6,7},{7,6},{8,9},{9,8},{10,11... | collective-permute-start | bytes 196616 | tf_op jit(solution)/shard_map/ppermute | solution.py:239
  19.0 2.0 %collective-permute-start.5 = (bf16[32,1024]{1,0:T(8,128)(2,1)S(1)}, bf16[32,1024]{1,0:T(8,128)(2,1)S(1)}, u32[]{:S(2)}, u32[]{:S(2)}) collective-permute-start(bf16[32,1024]{1,0:T(8,128)(2,1)S(1)} %collective-permute-done.1.refs_2_), channel_id=1, source_target_pairs={{0,1},{1,0},{2,3},{3,2},{4,5},{5,4},{6,7},{7,6},{8,9},{9,8},{10,11... | collective-permute-start | bytes 196616 | tf_op jit(solution)/shard_map/ppermute | solution.py:239
  19.3 1.7 %collective-permute-start.6 = (bf16[32,1024]{1,0:T(8,128)(2,1)S(1)}, bf16[32,1024]{1,0:T(8,128)(2,1)S(1)}, u32[]{:S(2)}, u32[]{:S(2)}) collective-permute-start(bf16[32,1024]{1,0:T(8,128)(2,1)S(1)} %collective-permute-done.2.refs_3_), channel_id=1, source_target_pairs={{0,1},{1,0},{2,3},{3,2},{4,5},{5,4},{6,7},{7,6},{8,9},{9,8},{10,11... | collective-permute-start | bytes 196616 | tf_op jit(solution)/shard_map/ppermute | solution.py:239
  25.0 1.9 %collective-permute-start.7 = (f32[16,256]{1,0:T(8,128)S(1)}, f32[16,256]{1,0:T(8,128)S(1)}, u32[]{:S(2)}, u32[]{:S(2)}) collective-permute-start(f32[16,256]{1,0:T(8,128)S(1)} %get-tuple-element.36), channel_id=1, source_target_pairs={{0,1},{1,0},{2,3},{3,2},{4,5},{5,4},{6,7},{7,6},{8,9},{9,8},{10,11... | collective-permute-start | bytes 49160 | tf_op jit(solution)/shard_map/ppermute | solution.py:239
  25.4 9.0 %collective-permute-start.17 = (bf16[2,32,1024]{2,1,0:T(8,128)(2,1)S(1)}, bf16[2,32,1024]{2,1,0:T(8,128)(2,1)S(1)}, u32[]{:S(2)}, u32[]{:S(2)}) collective-permute-start(bf16[2,32,1024]{2,1,0:T(8,128)(2,1)S(1)} %slice_bitcast_fusion.refs_0_), channel_id=1, source_target_pairs={{0,4},{1,5},{2,6},{3,7},{4,0},{5,1},{6,2},{7,3},{8,12},{9,13},{10,... | collective-permute-start | bytes 393224 | tf_op jit(solution)/shard_map/ppermute | solution.py:239
  26.9 7.5 %collective-permute-start.18 = (bf16[2,32,1024]{2,1,0:T(8,128)(2,1)S(1)}, bf16[2,32,1024]{2,1,0:T(8,128)(2,1)S(1)}, u32[]{:S(2)}, u32[]{:S(2)}) collective-permute-start(bf16[2,32,1024]{2,1,0:T(8,128)(2,1)S(1)} %slice_bitcast_fusion.refs_0_), channel_id=1, source_target_pairs={{0,6},{1,7},{2,4},{3,5},{4,2},{5,3},{6,0},{7,1},{8,14},{9,15},{10,... | collective-permute-start | bytes 393224 | tf_op jit(solution)/shard_map/ppermute | solution.py:239
  26.9 7.9 %collective-permute-start.10 = (f32[16,256]{1,0:T(8,128)S(1)}, f32[16,256]{1,0:T(8,128)S(1)}, u32[]{:S(2)}, u32[]{:S(2)}) collective-permute-start(f32[16,256]{1,0:T(8,128)S(1)} %add.63), channel_id=1, source_target_pairs={{0,6},{1,7},{2,4},{3,5},{4,2},{5,3},{6,0},{7,1},{8,14},{9,15},{10,... | collective-permute-start | bytes 49160 | tf_op jit(solution)/shard_map/ppermute | solution.py:239
  29.9 5.0 %collective-permute-start.8 = (f32[16,256]{1,0:T(8,128)S(1)}, f32[16,256]{1,0:T(8,128)S(1)}, u32[]{:S(2)}, u32[]{:S(2)}) collective-permute-start(f32[16,256]{1,0:T(8,128)S(1)} %add.63), channel_id=1, source_target_pairs={{0,2},{1,3},{2,0},{3,1},{4,6},{5,7},{6,4},{7,5},{8,10},{9,11},{10,... | collective-permute-start | bytes 49160 | tf_op jit(solution)/shard_map/ppermute | solution.py:239
  30.4 4.9 %collective-permute-start.9 = (f32[16,256]{1,0:T(8,128)S(1)}, f32[16,256]{1,0:T(8,128)S(1)}, u32[]{:S(2)}, u32[]{:S(2)}) collective-permute-start(f32[16,256]{1,0:T(8,128)S(1)} %add.63), channel_id=1, source_target_pairs={{0,4},{1,5},{2,6},{3,7},{4,0},{5,1},{6,2},{7,3},{8,12},{9,13},{10,... | collective-permute-start | bytes 49160 | tf_op jit(solution)/shard_map/ppermute | solution.py:239
  34.3 4.3 %collective-permute-start.19 = (bf16[2,32,1024]{2,1,0:T(8,128)(2,1)S(1)}, bf16[2,32,1024]{2,1,0:T(8,128)(2,1)S(1)}, u32[]{:S(2)}, u32[]{:S(2)}) collective-permute-start(bf16[2,32,1024]{2,1,0:T(8,128)(2,1)S(1)} %slice_bitcast_fusion.refs_0_), channel_id=1, source_target_pairs={{0,1},{1,0},{2,3},{3,2},{4,5},{5,4},{6,7},{7,6},{8,9},{9,8},{10,11... | collective-permute-start | bytes 393224 | tf_op jit(solution)/shard_map/ppermute | solution.py:239
  34.3 5.8 %collective-permute-start.20 = (bf16[2,32,1024]{2,1,0:T(8,128)(2,1)S(1)}, bf16[2,32,1024]{2,1,0:T(8,128)(2,1)S(1)}, u32[]{:S(2)}, u32[]{:S(2)}) collective-permute-start(bf16[2,32,1024]{2,1,0:T(8,128)(2,1)S(1)} %collective-permute-done.16.refs_1_), channel_id=1, source_target_pairs={{0,1},{1,0},{2,3},{3,2},{4,5},{5,4},{6,7},{7,6},{8,9},{9,8},{10,11... | collective-permute-start | bytes 393224 | tf_op jit(solution)/shard_map/ppermute | solution.py:239
  34.9 6.1 %collective-permute-start.21 = (bf16[2,32,1024]{2,1,0:T(8,128)(2,1)S(1)}, bf16[2,32,1024]{2,1,0:T(8,128)(2,1)S(1)}, u32[]{:S(2)}, u32[]{:S(2)}) collective-permute-start(bf16[2,32,1024]{2,1,0:T(8,128)(2,1)S(1)} %collective-permute-done.17.refs_2_), channel_id=1, source_target_pairs={{0,1},{1,0},{2,3},{3,2},{4,5},{5,4},{6,7},{7,6},{8,9},{9,8},{10,11... | collective-permute-start | bytes 393224 | tf_op jit(solution)/shard_map/ppermute | solution.py:239
  34.9 6.0 %collective-permute-start.22 = (bf16[2,32,1024]{2,1,0:T(8,128)(2,1)S(1)}, bf16[2,32,1024]{2,1,0:T(8,128)(2,1)S(1)}, u32[]{:S(2)}, u32[]{:S(2)}) collective-permute-start(bf16[2,32,1024]{2,1,0:T(8,128)(2,1)S(1)} %collective-permute-done.18.refs_3_), channel_id=1, source_target_pairs={{0,1},{1,0},{2,3},{3,2},{4,5},{5,4},{6,7},{7,6},{8,9},{9,8},{10,11... | collective-permute-start | bytes 393224 | tf_op jit(solution)/shard_map/ppermute | solution.py:239
  35.7 1.6 %collective-permute-start.11 = (f32[16,1024]{1,0:T(8,128)S(1)}, f32[16,1024]{1,0:T(8,128)S(1)}, u32[]{:S(2)}, u32[]{:S(2)}) collective-permute-start(f32[16,1024]{1,0:T(8,128)S(1)} %right.3), channel_id=1, source_target_pairs={{0,1},{1,0},{2,3},{3,2},{4,5},{5,4},{6,7},{7,6},{8,9},{9,8},{10,11... | collective-permute-start | bytes 196616 | tf_op jit(solution)/shard_map/ppermute | solution.py:239
  35.8 16.1 %slice-start = ((s8[8388608]{0:T(1024)(128)(4,1)}), s8[4194304]{0:T(1024)(128)(4,1)S(1)}, s32[]{:S(2)}) async-start(s8[8388608]{0:T(1024)(128)(4,1)} %bitcast.37), calls=%async_computation | async-start | bytes 8388608
  37.4 14.5 %slice-start.1 = ((s8[8388608]{0:T(1024)(128)(4,1)}), s8[4194304]{0:T(1024)(128)(4,1)S(1)}, s32[]{:S(2)}) async-start(s8[8388608]{0:T(1024)(128)(4,1)} %bitcast.37), calls=%async_computation.1 | async-start | bytes 8388608
  37.4 6.5 %collective-permute-start.12 = (f32[16,1024]{1,0:T(8,128)S(1)}, f32[16,1024]{1,0:T(8,128)S(1)}, u32[]{:S(2)}, u32[]{:S(2)}) collective-permute-start(f32[16,1024]{1,0:T(8,128)S(1)} %add.67), channel_id=1, source_target_pairs={{0,2},{1,3},{2,0},{3,1},{4,6},{5,7},{6,4},{7,5},{8,10},{9,11},{10,... | collective-permute-start | bytes 196616 | tf_op jit(solution)/shard_map/ppermute | solution.py:239
  38.7 5.3 %collective-permute-start.13 = (f32[16,1024]{1,0:T(8,128)S(1)}, f32[16,1024]{1,0:T(8,128)S(1)}, u32[]{:S(2)}, u32[]{:S(2)}) collective-permute-start(f32[16,1024]{1,0:T(8,128)S(1)} %add.67), channel_id=1, source_target_pairs={{0,4},{1,5},{2,6},{3,7},{4,0},{5,1},{6,2},{7,3},{8,12},{9,13},{10,... | collective-permute-start | bytes 196616 | tf_op jit(solution)/shard_map/ppermute | solution.py:239
  40.2 5.2 %collective-permute-start.14 = (f32[16,1024]{1,0:T(8,128)S(1)}, f32[16,1024]{1,0:T(8,128)S(1)}, u32[]{:S(2)}, u32[]{:S(2)}) collective-permute-start(f32[16,1024]{1,0:T(8,128)S(1)} %add.67), channel_id=1, source_target_pairs={{0,6},{1,7},{2,4},{3,5},{4,2},{5,3},{6,0},{7,1},{8,14},{9,15},{10,... | collective-permute-start | bytes 196616 | tf_op jit(solution)/shard_map/ppermute | solution.py:239
  45.5 6.3 %collective-permute-start.15 = (f32[16,1280]{1,0:T(8,128)S(1)}, f32[16,1280]{1,0:T(8,128)S(1)}, u32[]{:S(2)}, u32[]{:S(2)}) collective-permute-start(f32[16,1280]{1,0:T(8,128)S(1)} %get-tuple-element.40), channel_id=1, source_target_pairs={{8,0},{16,8},{24,16},{9,1},{17,9},{25,17},{10,2},{18,10},{26,18},{... | collective-permute-start | bytes 245768 | tf_op jit(solution)/shard_map/ppermute | solution.py:385
  47.0 4.9 %copy-start.3 = (f32[3,1024,16]{1,2,0:T(8,128)S(1)}, f32[3,1024,16]{1,2,0:T(8,128)}, u32[]{:S(2)}) copy-start(f32[3,1024,16]{1,2,0:T(8,128)} %param.15) | copy-start | bytes 589828
  47.0 4.9 %copy-start.5 = (f32[3,256,16]{1,2,0:T(8,128)S(1)}, f32[3,256,16]{1,2,0:T(8,128)}, u32[]{:S(2)}) copy-start(f32[3,256,16]{1,2,0:T(8,128)} %param.14) | copy-start | bytes 147460
  56.0 1.2 %collective-permute-start.23 = (f32[16,256]{1,0:T(8,128)S(1)}, f32[16,256]{1,0:T(8,128)S(1)}, u32[]{:S(2)}, u32[]{:S(2)}) collective-permute-start(f32[16,256]{1,0:T(8,128)S(1)} %get-tuple-element.42), channel_id=1, source_target_pairs={{0,1},{1,0},{2,3},{3,2},{4,5},{5,4},{6,7},{7,6},{8,9},{9,8},{10,11... | collective-permute-start | bytes 49160 | tf_op jit(solution)/shard_map/ppermute | solution.py:239
  57.3 6.5 %collective-permute-start.24 = (f32[16,256]{1,0:T(8,128)S(1)}, f32[16,256]{1,0:T(8,128)S(1)}, u32[]{:S(2)}, u32[]{:S(2)}) collective-permute-start(f32[16,256]{1,0:T(8,128)S(1)} %add.71), channel_id=1, source_target_pairs={{0,2},{1,3},{2,0},{3,1},{4,6},{5,7},{6,4},{7,5},{8,10},{9,11},{10,... | collective-permute-start | bytes 49160 | tf_op jit(solution)/shard_map/ppermute | solution.py:239
  58.1 5.7 %collective-permute-start.25 = (f32[16,256]{1,0:T(8,128)S(1)}, f32[16,256]{1,0:T(8,128)S(1)}, u32[]{:S(2)}, u32[]{:S(2)}) collective-permute-start(f32[16,256]{1,0:T(8,128)S(1)} %add.71), channel_id=1, source_target_pairs={{0,4},{1,5},{2,6},{3,7},{4,0},{5,1},{6,2},{7,3},{8,12},{9,13},{10,... | collective-permute-start | bytes 49160 | tf_op jit(solution)/shard_map/ppermute | solution.py:239
  58.6 5.2 %collective-permute-start.26 = (f32[16,256]{1,0:T(8,128)S(1)}, f32[16,256]{1,0:T(8,128)S(1)}, u32[]{:S(2)}, u32[]{:S(2)}) collective-permute-start(f32[16,256]{1,0:T(8,128)S(1)} %add.71), channel_id=1, source_target_pairs={{0,6},{1,7},{2,4},{3,5},{4,2},{5,3},{6,0},{7,1},{8,14},{9,15},{10,... | collective-permute-start | bytes 49160 | tf_op jit(solution)/shard_map/ppermute | solution.py:239
  64.2 3.0 %collective-permute-start.27 = (f32[16,1024]{1,0:T(8,128)S(1)}, f32[16,1024]{1,0:T(8,128)S(1)}, u32[]{:S(2)}, u32[]{:S(2)}) collective-permute-start(f32[16,1024]{1,0:T(8,128)S(1)} %right.4), channel_id=1, source_target_pairs={{0,1},{1,0},{2,3},{3,2},{4,5},{5,4},{6,7},{7,6},{8,9},{9,8},{10,11... | collective-permute-start | bytes 196616 | tf_op jit(solution)/shard_map/ppermute | solution.py:239
  67.2 5.1 %collective-permute-start.28 = (f32[16,1024]{1,0:T(8,128)S(1)}, f32[16,1024]{1,0:T(8,128)S(1)}, u32[]{:S(2)}, u32[]{:S(2)}) collective-permute-start(f32[16,1024]{1,0:T(8,128)S(1)} %add.75), channel_id=1, source_target_pairs={{0,2},{1,3},{2,0},{3,1},{4,6},{5,7},{6,4},{7,5},{8,10},{9,11},{10,... | collective-permute-start | bytes 196616 | tf_op jit(solution)/shard_map/ppermute | solution.py:239
  68.1 4.3 %collective-permute-start.29 = (f32[16,1024]{1,0:T(8,128)S(1)}, f32[16,1024]{1,0:T(8,128)S(1)}, u32[]{:S(2)}, u32[]{:S(2)}) collective-permute-start(f32[16,1024]{1,0:T(8,128)S(1)} %add.75), channel_id=1, source_target_pairs={{0,4},{1,5},{2,6},{3,7},{4,0},{5,1},{6,2},{7,3},{8,12},{9,13},{10,... | collective-permute-start | bytes 196616 | tf_op jit(solution)/shard_map/ppermute | solution.py:239
  69.4 5.2 %collective-permute-start.30 = (f32[16,1024]{1,0:T(8,128)S(1)}, f32[16,1024]{1,0:T(8,128)S(1)}, u32[]{:S(2)}, u32[]{:S(2)}) collective-permute-start(f32[16,1024]{1,0:T(8,128)S(1)} %add.75), channel_id=1, source_target_pairs={{0,6},{1,7},{2,4},{3,5},{4,2},{5,3},{6,0},{7,1},{8,14},{9,15},{10,... | collective-permute-start | bytes 196616 | tf_op jit(solution)/shard_map/ppermute | solution.py:239
  74.7 6.3 %collective-permute-start.31 = (f32[16,1280]{1,0:T(8,128)S(1)}, f32[16,1280]{1,0:T(8,128)S(1)}, u32[]{:S(2)}, u32[]{:S(2)}) collective-permute-start(f32[16,1280]{1,0:T(8,128)S(1)} %get-tuple-element.48), channel_id=1, source_target_pairs={{8,0},{16,8},{24,16},{9,1},{17,9},{25,17},{10,2},{18,10},{26,18},{... | collective-permute-start | bytes 245768 | tf_op jit(solution)/shard_map/ppermute | solution.py:385
  85.2 1.2 %collective-permute-start.32 = (f32[16,256]{1,0:T(8,128)S(1)}, f32[16,256]{1,0:T(8,128)S(1)}, u32[]{:S(2)}, u32[]{:S(2)}) collective-permute-start(f32[16,256]{1,0:T(8,128)S(1)} %get-tuple-element.50), channel_id=1, source_target_pairs={{0,1},{1,0},{2,3},{3,2},{4,5},{5,4},{6,7},{7,6},{8,9},{9,8},{10,11... | collective-permute-start | bytes 49160 | tf_op jit(solution)/shard_map/ppermute | solution.py:239
  86.4 7.2 %collective-permute-start.33 = (f32[16,256]{1,0:T(8,128)S(1)}, f32[16,256]{1,0:T(8,128)S(1)}, u32[]{:S(2)}, u32[]{:S(2)}) collective-permute-start(f32[16,256]{1,0:T(8,128)S(1)} %add.79), channel_id=1, source_target_pairs={{0,2},{1,3},{2,0},{3,1},{4,6},{5,7},{6,4},{7,5},{8,10},{9,11},{10,... | collective-permute-start | bytes 49160 | tf_op jit(solution)/shard_map/ppermute | solution.py:239
  87.3 6.4 %collective-permute-start.34 = (f32[16,256]{1,0:T(8,128)S(1)}, f32[16,256]{1,0:T(8,128)S(1)}, u32[]{:S(2)}, u32[]{:S(2)}) collective-permute-start(f32[16,256]{1,0:T(8,128)S(1)} %add.79), channel_id=1, source_target_pairs={{0,4},{1,5},{2,6},{3,7},{4,0},{5,1},{6,2},{7,3},{8,12},{9,13},{10,... | collective-permute-start | bytes 49160 | tf_op jit(solution)/shard_map/ppermute | solution.py:239
  88.4 5.3 %collective-permute-start.35 = (f32[16,256]{1,0:T(8,128)S(1)}, f32[16,256]{1,0:T(8,128)S(1)}, u32[]{:S(2)}, u32[]{:S(2)}) collective-permute-start(f32[16,256]{1,0:T(8,128)S(1)} %add.79), channel_id=1, source_target_pairs={{0,6},{1,7},{2,4},{3,5},{4,2},{5,3},{6,0},{7,1},{8,14},{9,15},{10,... | collective-permute-start | bytes 49160 | tf_op jit(solution)/shard_map/ppermute | solution.py:239
  93.6 1.8 %collective-permute-start.36 = (bf16[4,32,1024]{2,1,0:T(8,128)(2,1)S(1)}, bf16[4,32,1024]{2,1,0:T(8,128)(2,1)S(1)}, u32[]{:S(2)}, u32[]{:S(2)}) collective-permute-start(bf16[4,32,1024]{2,1,0:T(8,128)(2,1)S(1)} %outgoing.1), channel_id=1, source_target_pairs={{0,1},{1,0},{2,3},{3,2},{4,5},{5,4},{6,7},{7,6},{8,9},{9,8},{10,11... | collective-permute-start | bytes 786440 | tf_op jit(solution)/shard_map/ppermute | solution.py:239
  94.0 1.4 %collective-permute-start.37 = (f32[16,1024]{1,0:T(8,128)S(1)}, f32[16,1024]{1,0:T(8,128)S(1)}, u32[]{:S(2)}, u32[]{:S(2)}) collective-permute-start(f32[16,1024]{1,0:T(8,128)S(1)} %right.5.right_ref), channel_id=1, source_target_pairs={{0,1},{1,0},{2,3},{3,2},{4,5},{5,4},{6,7},{7,6},{8,9},{9,8},{10,11... | collective-permute-start | bytes 196616 | tf_op jit(solution)/shard_map/ppermute | solution.py:239
  96.0 6.4 %collective-permute-start.38 = (bf16[64,1024]{1,0:T(8,128)(2,1)S(1)}, bf16[64,1024]{1,0:T(8,128)(2,1)S(1)}, u32[]{:S(2)}, u32[]{:S(2)}) collective-permute-start(bf16[64,1024]{1,0:T(8,128)(2,1)S(1)} %get-tuple-element.57), channel_id=1, source_target_pairs={{0,2},{1,3},{2,0},{3,1},{4,6},{5,7},{6,4},{7,5},{8,10},{9,11},{10,... | collective-permute-start | bytes 393224 | tf_op jit(solution)/shard_map/ppermute | solution.py:239
  96.9 8.3 %collective-permute-start.39 = (bf16[64,1024]{1,0:T(8,128)(2,1)S(1)}, bf16[64,1024]{1,0:T(8,128)(2,1)S(1)}, u32[]{:S(2)}, u32[]{:S(2)}) collective-permute-start(bf16[64,1024]{1,0:T(8,128)(2,1)S(1)} %get-tuple-element.58), channel_id=1, source_target_pairs={{0,4},{1,5},{2,6},{3,7},{4,0},{5,1},{6,2},{7,3},{8,12},{9,13},{10,... | collective-permute-start | bytes 393224 | tf_op jit(solution)/shard_map/ppermute | solution.py:239
  98.0 7.2 %collective-permute-start.40 = (bf16[64,1024]{1,0:T(8,128)(2,1)S(1)}, bf16[64,1024]{1,0:T(8,128)(2,1)S(1)}, u32[]{:S(2)}, u32[]{:S(2)}) collective-permute-start(bf16[64,1024]{1,0:T(8,128)(2,1)S(1)} %get-tuple-element.59), channel_id=1, source_target_pairs={{0,6},{1,7},{2,4},{3,5},{4,2},{5,3},{6,0},{7,1},{8,14},{9,15},{10,... | collective-permute-start | bytes 393224 | tf_op jit(solution)/shard_map/ppermute | solution.py:239

commit v2 on v1

v2 whole, which is shorter than its diff:
```python
import functools

import jax
import jax.numpy as jnp
from jax import lax
from jax.experimental import pallas as pl
from jax.experimental.pallas import tpu as pltpu
from jax.sharding import PartitionSpec as P

F32 = jnp.float32
BF16 = jnp.bfloat16
HIGH = lax.Precision.HIGHEST
VMEM = pl.BlockSpec(memory_space=pltpu.VMEM)
HBM = pl.BlockSpec(memory_space=pltpu.HBM)
MIB = 1 << 20


def dot(first, second, first_dim, second_dim, precision=None):
    return lax.dot_general(
        first,
        second,
        (((first_dim,), (second_dim,)), ((), ())),
        precision=precision,
        preferred_element_type=F32,
    )


def split(value):
    high = value.astype(BF16)
    low = (value - high.astype(F32)).astype(BF16)
    return jnp.concatenate([high, low], 0)


def chunks(total, most=512):
    size = min(total, most)
    return [(start, size) for start in range(0, total, size)]


def left_parts(left_t):
    left = left_t.T
    high = left.astype(BF16)
    low = (left - high.astype(F32)).astype(BF16)
    return jnp.concatenate([high, high, low], 1)


def right_parts(right_t):
    high = right_t.astype(BF16)
    low = (right_t - high.astype(F32)).astype(BF16)
    return jnp.concatenate([high, low, high], 0)


def cotangent_of(lefts, right_t):
    return dot(lefts, right_parts(right_t), 1, 0)


def chosen(incoming, other):
    return jnp.where(lax.axis_index("pipe") == lax.axis_size("pipe") - 1, incoming, other)


def own_columns(depth):
    share = depth // lax.axis_size("hid")
    if share % 128 == 0:
        return pl.ds(pl.multiple_of(lax.axis_index("hid") * share, share), share), 1.0
    return slice(0, depth), jnp.where(lax.axis_index("hid") == 0, 1.0, 0.0)


def own_width(depth):
    share = depth // lax.axis_size("hid")
    return share if share % 128 == 0 else depth


def on_device(kernel, outs, operands, flops, name, scratch=(), far=0, limit=8):
    many = isinstance(outs, list)
    shapes = [jax.ShapeDtypeStruct(*out) for out in (outs if many else [outs])]
    result = pl.pallas_call(
        kernel,
        out_shape=shapes,
        in_specs=[VMEM] * (len(operands) - far) + [HBM] * far,
        out_specs=[VMEM] * len(shapes),
        scratch_shapes=list(scratch),
        compiler_params=pltpu.CompilerParams(vmem_limit_bytes=limit * MIB),
        cost_estimate=pl.CostEstimate(flops=flops, bytes_accessed=1 << 20, transcendentals=0),
        name=name,
    )(*operands)
    return result if many else result[0]


def fetch(pairs, sems):
    copies = [pltpu.make_async_copy(source, target, sems.at[k]) for k, (source, target) in enumerate(pairs)]
    for copy in copies:
        copy.start()
    return copies


def up_kernel(
    in_left, in_right, pend_left, pend_right, warm_ref, w_out,
    up_ref, block_ref, proj_ref, w_out_ref, right_ref, sems,
):
    parts = chunks(w_out_ref.shape[0], 1024)
    arrivals = fetch([(w_out.at[pl.ds(*part)], w_out_ref.at[pl.ds(*part)]) for part in parts], sems)
    left = chosen(in_left[0], pend_left[...])
    right_ref[...] = chosen(in_right[0], pend_right[...])
    lefts = left_parts(left)
    own_share(lefts, right_ref, warm_ref, block_ref, proj_ref)
    cotangent_low = cotangent_of(lefts, right_ref[...]).astype(BF16)
    for part, (start, size) in enumerate(parts):
        arrivals[part].wait()
        up_ref[:, start : start + size] = dot(cotangent_low, w_out_ref[start : start + size, :], 1, 1).astype(BF16)


def own_share(lefts, right_ref, warm_ref, block_ref, proj_ref):
    here, factor = own_columns(right_ref.shape[1])
    block = cotangent_of(lefts, right_ref[:, here]) * factor
    block_ref[...] = block
    high = block.astype(BF16)
    low = (block - high.astype(F32)).astype(BF16)
    warm = split(warm_ref[:, here])
    proj_ref[...] = jnp.zeros_like(proj_ref)
    add_projected(dot(high, warm, 1, 1) + dot(low, warm, 1, 1), proj_ref)


def warm_into(stacked, w_in_ref, out_ref, start, size):
    rank = stacked.shape[0] // 2
    both = dot(stacked, w_in_ref[:, start : start + size], 1, 0)
    out_ref[:, start : start + size] = split(both[:rank] + both[rank:])


def warm_kernel(warm_ref, w_in_ref, out_ref):
    stacked = split(warm_ref[...])
    for start, size in chunks(w_in_ref.shape[1]):
        warm_into(stacked, w_in_ref, out_ref, start, size)


def enter_kernel(warm_ref, w_in, out_ref, w_in_ref, sems):
    parts = chunks(w_in_ref.shape[1])
    arrivals = fetch([(w_in.at[:, pl.ds(*part)], w_in_ref.at[:, pl.ds(*part)]) for part in parts], sems)
    stacked = split(warm_ref[...])
    for part, (start, size) in enumerate(parts):
        arrivals[part].wait()
        warm_into(stacked, w_in_ref, out_ref, start, size)


def place_rows(offsets, pieces, rows_ref):
    block = pieces[0].shape[0]
    for offset, piece in zip(offsets, pieces):
        place = 0
        if len(pieces) > 1:
            place = pl.multiple_of(jnp.bitwise_xor(lax.axis_index("hid"), offset) * block, block)
        rows_ref[pl.ds(place, block), :] = piece[...]


def project(hidden, warm_in_ref, start, size, total):
    part = dot(hidden, warm_in_ref[:, start : start + size], 1, 1)
    return part if total is None else total + part


def add_projected(total, proj_ref):
    rank = proj_ref.shape[0]
    turned = total.T
    proj_ref[...] += turned[:rank] + turned[rank:]


def first_kernel(offsets, *refs):
    pieces, rest = refs[: len(offsets)], refs[len(offsets) :]
    w_in_ref, up_ref, warm_in_ref, share_ref, hidden_ref, proj_ref, rows_ref = rest
    place_rows(offsets, [piece.at[0] for piece in pieces], rows_ref)
    total = None
    for start, size in chunks(w_in_ref.shape[1]):
        preact = dot(rows_ref[...], w_in_ref[:, start : start + size], 1, 0)
        hidden = jnp.where(preact > 0, up_ref[:, start : start + size].astype(F32), 0.0).astype(BF16)
        hidden_ref[:, start : start + size] = hidden
        total = project(hidden, warm_in_ref, start, size, total)
    proj_ref[...] = share_ref[...]
    add_projected(total, proj_ref)


def mask_kernel(offsets, step, *refs):
    pieces, (w_in_ref, _, mask_ref, rows_ref) = refs[: len(offsets)], refs[len(offsets) :]
    place_rows(offsets, [piece.at[step] for piece in pieces], rows_ref)
    for start, size in chunks(w_in_ref.shape[1]):
        preact = dot(rows_ref[...], w_in_ref[:, start : start + size], 1, 0)
        mask_ref[:, start : start + size] = jnp.where(preact > 0, 1.0, 0.0).astype(BF16)


def hidden_kernel(
    tick, in_left_ref, in_right_ref, both_ref, warm_ref, w_out_ref, mask_ref, warm_in_ref,
    hidden_ref, proj_ref, block_ref, right_ref,
):
    rows = hidden_ref.shape[0]
    lefts = left_parts(chosen(in_left_ref[tick], both_ref[:, :rows]))
    right_ref[...] = chosen(in_right_ref[tick], both_ref[:, rows:])
    cotangent_low = cotangent_of(lefts, right_ref[...]).astype(BF16)
    own_share(lefts, right_ref, warm_ref, block_ref, proj_ref)
    total = None
    for start, size in chunks(w_out_ref.shape[0]):
        up = dot(cotangent_low, w_out_ref[start : start + size, :], 1, 1)
        mask = mask_ref[:, start : start + size]
        hidden = jnp.where(mask.astype(F32) > 0, up, 0.0).astype(BF16)
        hidden_ref[:, start : start + size] = hidden
        total = project(hidden, warm_in_ref, start, size, total)
    add_projected(total, proj_ref)


def merged_kernel(block_ref, hidden_ref, w_in_ref, merged_ref):
    depth = w_in_ref.shape[0]
    size = min(depth, 256)
    for start in range(0, depth, size):
        here = slice(start, start + size)
        merged_ref[:, here] = dot(hidden_ref[...], w_in_ref[here, :], 1, 1)
    here, _ = own_columns(depth)
    merged_ref[:, here] += block_ref[...]


def right_kernel(proj_ref, merged_ref, out_ref):
    stacked = split(proj_ref[...])
    rank = proj_ref.shape[0]
    merged = merged_ref[...]
    high = merged.astype(BF16)
    low = (merged - high.astype(F32)).astype(BF16)
    both = dot(stacked, high, 1, 0) + dot(stacked, low, 1, 0)
    out_ref[...] = both[:rank] + both[rank:]


def factor_kernel(proj_ref, left_ref, inverse_ref):
    proj = proj_ref[...]
    rank = proj.shape[0]
    gram = dot(proj, proj, 1, 1, HIGH)
    line = lax.broadcasted_iota(jnp.int32, (rank, rank), 0)
    column = lax.broadcasted_iota(jnp.int32, (rank, rank), 1)
    eye = jnp.where(line == column, 1.0, 0.0)
    inverse = eye
    for step in range(rank):
        pivot_row = gram[step : step + 1, :]
        pivot = gram[step : step + 1, step : step + 1]
        scale = jnp.where(line[:, :1] > step, gram[:, step : step + 1] / pivot, 0.0)
        inverse = inverse - scale * inverse[step : step + 1, :]
        gram = gram - scale * pivot_row
    pivots = jnp.sum(gram * eye, axis=1, keepdims=True)
    inverse = inverse * lax.rsqrt(pivots)
    inverse_ref[...] = inverse
    left_ref[...] = dot(inverse, proj, 1, 0, HIGH)


def finish_kernel(inverse_ref, left_ref, sums_ref, right_ref, both_ref):
    right = dot(inverse_ref[...], sums_ref[...], 1, 0, HIGH)
    rows = left_ref.shape[1]
    right_ref[...] = right
    both_ref[:, :rows] = left_ref[...]
    both_ref[:, rows:] = right


def outgoing_kernel(merged_ref, out_ref):
    block = out_ref.shape[1]
    for chip in range(out_ref.shape[0]):
        start = pl.multiple_of((2 * chip + 1 - lax.axis_index("hid") % 2) * block, block)
        out_ref[chip] = merged_ref[pl.ds(start, block), :].astype(BF16)


def pack_kernel(chips, merged_ref, arrived_ref, right_ref, right_arrived_ref, own_ref, right_out, *out_refs):
    block = own_ref.shape[0]
    core, chip = lax.axis_index("hid") % 2, lax.axis_index("hid") // 2
    stacked = split(right_ref[...] + right_arrived_ref[...])
    rank = right_ref.shape[0]
    right_out[...] = stacked[:rank].astype(F32) + stacked[rank:].astype(F32)
    for turn in range(chips):
        target = jnp.bitwise_xor(chip, turn)
        start = pl.multiple_of((2 * target + core) * block, block)
        value = merged_ref[pl.ds(start, block), :] + arrived_ref[target].astype(F32)
        if turn:
            out_refs[turn - 1][:block, :] = value.astype(BF16)
            out_refs[turn - 1][block:, :] = stacked
        else:
            own_ref[...] = value


def last_kernel(inverse_ref, own_ref, right_own_ref, *refs):
    packs, (grads_ref, right_ref) = refs[:-2], refs[-2:]
    block, rank = own_ref.shape[0], inverse_ref.shape[0]
    rows = [own_ref[...]] + [pack[:block, :].astype(F32) for pack in packs]
    sums = [right_own_ref[...]] + [
        pack[block : block + rank, :].astype(F32) + pack[block + rank :, :].astype(F32) for pack in packs
    ]
    grads_ref[...] = tree_sum(rows)
    right_ref[...] = dot(inverse_ref[...], tree_sum(sums), 1, 0, HIGH)


def flip(value, axis, bits):
    count = lax.axis_size(axis)
    return lax.ppermute(value, axis, [(source, source ^ bits) for source in range(count)])


def stages(count):
    found, stride = [], 1
    while stride < count:
        members = 2 if stride == 1 else min(4, count // stride)
        found.append((stride, members))
        stride *= members
    return found


def tree_sum(parts):
    while len(parts) > 1:
        parts = [first + second for first, second in zip(parts[::2], parts[1::2])]
    return parts[0]


def all_sum(value):
    for stride, members in stages(lax.axis_size("hid")):
        value = tree_sum([value] + [flip(value, "hid", stride * k) for k in range(1, members)])
    return value


def gather_pieces(pieces, plan):
    pieces = dict(pieces)
    for stride, members in plan:
        for offset in list(pieces):
            for k in range(1, members):
                pieces[offset ^ (stride * k)] = flip(pieces[offset], "hid", stride * k)
    return pieces


def body(section_inputs, w_in, w_out, warm_factor, pending_left, pending_right, incoming_left, incoming_right):
    w_in, w_out, inputs = w_in[0], w_out[0], section_inputs[0]
    ticks, rows_own, depth = inputs.shape
    hidden_units = w_out.shape[0]
    rank = warm_factor.shape[2]
    count, own = lax.axis_size("hid"), lax.axis_index("hid")
    rows = rows_own * count
    sections = lax.axis_size("pipe")
    full = 2 * rows * depth * hidden_units
    turned = lambda value: jnp.swapaxes(value, -1, -2)
    incoming = (turned(incoming_left), turned(incoming_right))
    warm = turned(warm_factor[0])
    wide = ((rows, hidden_units), BF16)
    left_form, right_form = ((rank, rows), F32), ((rank, depth), F32)
    chips = count // 2
    direct = stages(count) == [(1, 2), (2, chips)]

    plan = stages(count)
    by_rows = rows_own % 16 == 0
    if by_rows:
        blocks = gather_pieces({0: inputs}, plan[1:])
    else:
        blocks = {0: lax.all_gather(inputs, "hid", axis=1, tiled=True)}
    block_form = ((rows, own_width(depth)), F32)
    sems = [pltpu.SemaphoreType.DMA((len(chunks(hidden_units)),))]
    warm_in, w_in = on_device(
        enter_kernel,
        [((2 * rank, hidden_units), BF16), (w_in.shape, BF16)],
        (warm, w_in),
        full,
        "enter",
        sems,
        1,
        43,
    )
    early = lax.optimization_barrier((warm, warm_in))[0]
    up, block, share, w_out = on_device(
        up_kernel,
        [wide, block_form, left_form, (w_out.shape, BF16)],
        (*incoming, turned(pending_left[0]), turned(pending_right[0]), early, w_out),
        full,
        "up",
        [pltpu.VMEM(*right_form)] + sems,
        1,
        38,
    )
    if by_rows:
        held = lax.optimization_barrier((list(blocks.values()), share))[0]
        blocks = gather_pieces(zip(blocks, held), plan[:1])
    offsets, pieces = list(blocks), list(blocks.values())

    for tick in range(ticks):
        last = tick + 1 == ticks
        scratch = [pltpu.VMEM((rows, depth), BF16)]
        if tick == 0:
            hidden, proj = on_device(
                functools.partial(first_kernel, offsets),
                [wide, left_form],
                (*pieces, w_in, up, warm_in, share),
                full,
                "first",
                scratch,
            )
        else:
            warm_in = on_device(
                warm_kernel, ((2 * rank, hidden_units), BF16), (warm, w_in), full // 2, "warm"
            )
            mask = on_device(
                functools.partial(mask_kernel, offsets, tick),
                wide,
                (*pieces, w_in, leaving),
                full,
                "mask",
                scratch,
            )
            hidden, proj, block = on_device(
                functools.partial(hidden_kernel, tick),
                [wide, left_form, block_form],
                (*incoming, both, warm, w_out, mask, warm_in),
                full,
                "hidden",
                [pltpu.VMEM(*right_form)],
            )
        merged = on_device(merged_kernel, ((rows, depth), F32), (block, hidden, w_in), full, "merged")
        if last and direct:
            outgoing = on_device(
                outgoing_kernel, ((chips, rows_own, depth), BF16), (merged,), full // 16, "outgoing"
            )
            arrived = flip(outgoing, "hid", 1)
        proj = all_sum(proj)
        partial_right = on_device(
            right_kernel, right_form, (proj, merged), full // 16, "right"
        )
        left_new, inverse = on_device(
            factor_kernel, [left_form, ((rank, rank), F32)], (proj,), full // 2, "factor"
        )
        if last and direct:
            packed = ((rows_own + 2 * rank, depth), BF16)
            own_rows, own_right, *packs = on_device(
                functools.partial(pack_kernel, chips),
                [((rows_own, depth), F32), right_form] + [packed] * (chips - 1),
                (merged, arrived, partial_right, flip(partial_right, "hid", 1)),
                full // 16,
                "pack",
            )
            packs = [flip(pack, "hid", 2 * k) for k, pack in enumerate(packs, 1)]
            grads, warm = on_device(
                last_kernel,
                [((rows_own, depth), F32), right_form],
                (inverse, own_rows, own_right, *packs),
                full // 16,
                "last",
            )
            break
        if last:
            grads = lax.psum_scatter(merged, "hid", scatter_dimension=0, tiled=True)
        warm, leaving = on_device(
            finish_kernel,
            [right_form, ((rank, rows + depth), F32)],
            (inverse, left_new, all_sum(partial_right)),
            full // 16,
            "finish",
        )
        if not last:
            both = lax.ppermute(leaving, "pipe", [(source, source - 1) for source in range(1, sections)])
    left_rows = lax.dynamic_slice_in_dim(left_new, own * rows_own, rows_own, 1)
    return grads[None], turned(left_rows)[None], turned(warm)[None]


def solution(mesh):
    placed = (
        P("pipe", None, "hid", None),
        P("pipe", None, "hid"),
        P("pipe", "hid", None),
        P("pipe", None, None),
        P("pipe", None, None),
        P("pipe", None, None),
        P(),
        P(),
    )
    return jax.shard_map(
        body,
        mesh=mesh,
        in_specs=placed,
        out_specs=(P("pipe", "hid", None), P("pipe", "hid", None), P("pipe", None, None)),
        check_vma=False,
    )
```

time: 106 us -> 95 us (0.90)
  local copies, waits for them, and re-layouts: 9.15 us -> 1.56 us
  starting transfers between devices: 35.2 us -> 30.3 us
  waiting for transfers between devices: 17.9 us -> 21.2 us
  Pallas kernels: 42.6 us -> 40.8 us
    ppermute x39 -> x32, waiting for transfers between devices: 11.1 us -> 19.2 us  [flip(): lax.ppermute(value, axis, [(source, source ^ bits) for source in range(co...]
    unnamed x22 -> x14, local copies, waits for them, and re-layouts: 6.69 us -> 0.86 us
    ppermute x39 -> x32, starting transfers between devices: 32.2 us -> 27.3 us  [flip(): lax.ppermute(value, axis, [(source, source ^ bits) for source in range(co...]
    ppermute x2, waiting for transfers between devices: 6.76 us -> 2.06 us  [body(): lax.ppermute(leaving, 'pipe', [(source, source - 1) for source in range(1...]
    pallas_call x23, Pallas kernels: 42.6 us -> 40.8 us  [on_device(): pl.pallas_call(kernel, out_shape=shapes, in_specs=[VMEM] * (len(operands)...]
  transfers between devices with their start and end apart: 41 -> 34, of which waited for: 10 -> 22; matrix products, arithmetic and copies ran while one was open for 2% -> 1% of each run, Pallas kernels for 30% -> 30%
where the time goes in v2:
time: 95 us; the launch traced here: 94.8 us
  Pallas kernels  40.8 us (43%)
  starting transfers between devices  30.3 us (32%)
  waiting for transfers between devices  21.2 us (22%)
  local copies, waits for them, and re-layouts  1.56 us (2%)
    pallas_call x23, Pallas kernels, on_device(): pl.pallas_call(kernel, out_shape=shapes, in_specs=[VMEM] * (len(operands)...  40.8 us
    ppermute x32, starting transfers between devices, flip(): lax.ppermute(value, axis, [(source, source ^ bits) for source in range(co...  27.3 us
    ppermute x32, waiting for transfers between devices, flip(): lax.ppermute(value, axis, [(source, source ^ bits) for source in range(co...  19.2 us
    ppermute x2, starting transfers between devices, body(): lax.ppermute(leaving, 'pipe', [(source, source - 1) for source in range(1...  3 us
    ppermute x2, waiting for transfers between devices, body(): lax.ppermute(leaving, 'pipe', [(source, source - 1) for source in range(1...  2.06 us
  transfers between devices with their start and end apart: 34, of which 22 were waited for; matrix products, arithmetic and copies ran while one was open for 1% of the time, Pallas kernels for 30%

profile of v2, /device:TPU:0, one launch (start us, length us, event | category | flops | bytes accessed | tf_op | source)
XLA Modules:
  0.0 94.8 jit_solution(5435310616552893838)
XLA Ops:
  0.6 3.0 %collective-permute-start = (bf16[3,32,1024]{2,1,0:T(8,128)(2,1)}, bf16[3,32,1024]{2,1,0:T(8,128)(2,1)S(1)}, u32[]{:S(2)}, u32[]{:S(2)}) collective-permute-start(bf16[3,32,1024]{2,1,0:T(8,128)(2,1)} %bitcast.22), channel_id=1, source_target_pairs={{0,2},{1,3},{2,0},{3,1},{4,6},{5,7},{6,4},{7,5},{8,10},{9,11},{10,... | collective-permute-start | bytes 589832 | tf_op jit(solution)/shard_map/ppermute | solution.py:289
  3.6 1.5 %collective-permute-start.1 = (bf16[3,32,1024]{2,1,0:T(8,128)(2,1)}, bf16[3,32,1024]{2,1,0:T(8,128)(2,1)S(1)}, u32[]{:S(2)}, u32[]{:S(2)}) collective-permute-start(bf16[3,32,1024]{2,1,0:T(8,128)(2,1)} %bitcast.23), channel_id=1, source_target_pairs={{0,4},{1,5},{2,6},{3,7},{4,0},{5,1},{6,2},{7,3},{8,12},{9,13},{10,... | collective-permute-start | bytes 589832 | tf_op jit(solution)/shard_map/ppermute | solution.py:289
  5.2 0.8 copy-done.3
  6.0 3.9 %enter.1 = (bf16[32,4096]{1,0:T(8,128)(2,1)S(1)}, bf16[1024,4096]{1,0:T(8,128)(2,1)S(1)}) custom-call(f32[16,1024]{1,0:T(8,128)S(1)} %bitcast.35, bf16[1024,4096]{1,0:T(8,128)(2,1)} %bitcast.39), custom_call_target="tpu_custom_call" | custom-call | flops 2147483648 | bytes 1048576 | tf_op jit(solution)/shard_map/enter/pallas_call | solution.py:75
  10.0 4.7 %up.1 = (bf16[256,4096]{1,0:T(8,128)(2,1)S(1)}, f32[256,128]{1,0:T(8,128)S(1)}, f32[16,256]{1,0:T(8,128)S(1)}, bf16[4096,1024]{1,0:T(8,128)(2,1)S(1)}) custom-call(f32[3,16,256]{2,1,0:T(8,128)S(1)} %bitcast.32, f32[3,16,1024]{2,1,0:T(8,128)S(1)} %bitcast.29, f32[16,256]{1,0:T(8,128)S(1)} %bitcast.38, f32[16,1024]{1,0:T(8,128)S(1)} %bitcast.37, ...), custom_call_target="tpu_custom_call" | custom-call | flops 2147483648 | bytes 1048576 | tf_op jit(solution)/shard_map/up/pallas_call | solution.py:75
  14.8 0.5 collective-permute-start.4
  15.4 0.4 collective-permute-start.6
  15.8 0.4 collective-permute-done.3.refs_4_
  16.2 0.3 collective-permute-done.4.refs_5_
  16.8 0.3 collective-permute-done.6.refs_7_
  17.1 3.2 %first.1 = (bf16[256,4096]{1,0:T(8,128)(2,1)S(1)}, f32[16,256]{1,0:T(8,128)S(1)}) custom-call(bf16[3,32,1024]{2,1,0:T(8,128)(2,1)S(1)} %bitcast.26, bf16[3,32,1024]{2,1,0:T(8,128)(2,1)S(1)} %collective-permute-done.refs_1_, bf16[3,32,1024]{2,1,0:T(8,128)(2,1)S(1)} %collective-permute-done.1.refs_2_, bf16[3,32,1024]{2,1,0:T(8,128)(2,1)S(1)} %collective-permute-done.2.refs_3_, ...), custom_call_target="tpu_custom_call" | custom-call | flops 2147483648 | bytes 1048576 | tf_op jit(solution)/shard_map/first/pallas_call | solution.py:75
  20.5 1.0 %collective-permute-done.7 = f32[16,256]{1,0:T(8,128)S(1)} collective-permute-done((f32[16,256]{1,0:T(8,128)S(1)}, f32[16,256]{1,0:T(8,128)S(1)}, u32[]{:S(2)}, u32[]{:S(2)}) %collective-permute-start.7) | collective-permute-done | bytes 16416 | tf_op jit(solution)/shard_map/ppermute | solution.py:289
  21.5 2.9 %collective-permute-start.10 = (f32[16,256]{1,0:T(8,128)S(1)}, f32[16,256]{1,0:T(8,128)S(1)}, u32[]{:S(2)}, u32[]{:S(2)}) collective-permute-start(f32[16,256]{1,0:T(8,128)S(1)} %add.63), channel_id=1, source_target_pairs={{0,6},{1,7},{2,4},{3,5},{4,2},{5,3},{6,0},{7,1},{8,14},{9,15},{10,... | collective-permute-start | bytes 49160 | tf_op jit(solution)/shard_map/ppermute | solution.py:289
  24.4 0.5 collective-permute-start.8
  25.0 2.4 %merged.3.merged_ref = f32[256,1024]{1,0:T(8,128)S(1)} custom-call(f32[256,128]{1,0:T(8,128)S(1)} %get-tuple-element.51.block_ref, bf16[256,4096]{1,0:T(8,128)(2,1)S(1)} %get-tuple-element.52.hidden_ref, bf16[1024,4096]{1,0:T(8,128)(2,1)S(1)} %get-tuple-element.46.refs_8_.w_in_ref), custom_call_target="tpu_custom_call" | custom-call | flops 2147483648 | bytes 1048576 | tf_op jit(solution)/shard_map/merged/pallas_call | solution.py:75
  27.4 0.7 collective-permute-done.8
  28.1 0.5 collective-permute-done.9
  28.7 0.3 right.3
  29.0 1.3 %collective-permute-done.11 = f32[16,1024]{1,0:T(8,128)S(1)} collective-permute-done((f32[16,1024]{1,0:T(8,128)S(1)}, f32[16,1024]{1,0:T(8,128)S(1)}, u32[]{:S(2)}, u32[]{:S(2)}) %collective-permute-start.11) | collective-permute-done | bytes 65568 | tf_op jit(solution)/shard_map/ppermute | solution.py:289
  30.3 1.5 %collective-permute-start.12 = (f32[16,1024]{1,0:T(8,128)S(1)}, f32[16,1024]{1,0:T(8,128)S(1)}, u32[]{:S(2)}, u32[]{:S(2)}) collective-permute-start(f32[16,1024]{1,0:T(8,128)S(1)} %add.67), channel_id=1, source_target_pairs={{0,2},{1,3},{2,0},{3,1},{4,6},{5,7},{6,4},{7,5},{8,10},{9,11},{10,... | collective-permute-start | bytes 196616 | tf_op jit(solution)/shard_map/ppermute | solution.py:289
  31.8 0.7 collective-permute-start.13
  32.5 1.3 %collective-permute-start.14 = (f32[16,1024]{1,0:T(8,128)S(1)}, f32[16,1024]{1,0:T(8,128)S(1)}, u32[]{:S(2)}, u32[]{:S(2)}) collective-permute-start(f32[16,1024]{1,0:T(8,128)S(1)} %add.67), channel_id=1, source_target_pairs={{0,6},{1,7},{2,4},{3,5},{4,2},{5,3},{6,0},{7,1},{8,14},{9,15},{10,... | collective-permute-start | bytes 196616 | tf_op jit(solution)/shard_map/ppermute | solution.py:289
  33.8 1.6 %factor.3 = (f32[16,256]{1,0:T(8,128)S(1)}, f32[16,16]{1,0:T(8,128)S(1)}) custom-call(f32[16,256]{1,0:T(8,128)S(1)} %add_add_fusion.4.proj_ref), custom_call_target="tpu_custom_call" | custom-call | flops 1073741824 | bytes 1048576 | tf_op jit(solution)/shard_map/factor/pallas_call | solution.py:75
  35.4 1.4 %collective-permute-done.13 = f32[16,1024]{1,0:T(8,128)S(1)} collective-permute-done((f32[16,1024]{1,0:T(8,128)S(1)}, f32[16,1024]{1,0:T(8,128)S(1)}, u32[]{:S(2)}, u32[]{:S(2)}) %collective-permute-start.13) | collective-permute-done | bytes 65568 | tf_op jit(solution)/shard_map/ppermute | solution.py:289
  36.8 0.9 collective-permute-done.14
  37.9 1.5 %collective-permute-start.15 = (f32[16,1280]{1,0:T(8,128)S(1)}, f32[16,1280]{1,0:T(8,128)S(1)}, u32[]{:S(2)}, u32[]{:S(2)}) collective-permute-start(f32[16,1280]{1,0:T(8,128)S(1)} %get-tuple-element.53.refs_9_), channel_id=1, source_target_pairs={{8,0},{16,8},{24,16},{9,1},{17,9},{25,17},{10,2},{18,10},{26,18},{... | collective-permute-start | bytes 245768 | tf_op jit(solution)/shard_map/ppermute | solution.py:446
  39.4 2.4 %mask.2.mask_ref = bf16[256,4096]{1,0:T(8,128)(2,1)S(1)} custom-call(bf16[3,32,1024]{2,1,0:T(8,128)(2,1)S(1)} %bitcast.27, bf16[3,32,1024]{2,1,0:T(8,128)(2,1)S(1)} %collective-permute-done.refs_1_, bf16[3,32,1024]{2,1,0:T(8,128)(2,1)S(1)} %collective-permute-done.1.refs_2_, bf16[3,32,1024]{2,1,0:T(8,128)(2,1)S(1)} %collective-permute-done.2.refs_3_, ...), custom_call_target="tpu_custom_call" | custom-call | flops 2147483648 | bytes 1048576 | tf_op jit(solution)/shard_map/mask/pallas_call | solution.py:75
  41.7 1.4 %warm.2.warm_in_ref = bf16[32,4096]{1,0:T(8,128)(2,1)S(1)} custom-call(f32[16,1024]{1,0:T(8,128)S(1)} %get-tuple-element.54.warm_ref, bf16[1024,4096]{1,0:T(8,128)(2,1)S(1)} %get-tuple-element.46.refs_8_.w_in_ref), custom_call_target="tpu_custom_call" | custom-call | flops 1073741824 | bytes 1048576 | tf_op jit(solution)/shard_map/warm/pallas_call | solution.py:75
  43.2 1.1 %collective-permute-done.15.both_ref = f32[16,1280]{1,0:T(8,128)S(1)} collective-permute-done((f32[16,1280]{1,0:T(8,128)S(1)}, f32[16,1280]{1,0:T(8,128)S(1)}, u32[]{:S(2)}, u32[]{:S(2)}) %collective-permute-start.15) | collective-permute-done | bytes 81952 | tf_op jit(solution)/shard_map/ppermute | solution.py:446
  44.2 3.7 %hidden.2 = (bf16[256,4096]{1,0:T(8,128)(2,1)S(1)}, f32[16,256]{1,0:T(8,128)S(1)}, f32[256,128]{1,0:T(8,128)S(1)}) custom-call(f32[3,16,256]{2,1,0:T(8,128)S(1)} %bitcast.33, f32[3,16,1024]{2,1,0:T(8,128)S(1)} %bitcast.30, f32[16,1280]{1,0:T(8,128)S(1)} %collective-permute-done.15.both_ref, f32[16,1024]{1,0:T(8,128)S(1)} %get-tuple-element.54.warm_ref, ...), custom_call_target="tpu_custom_call" | custom-call | flops 2147483648 | bytes 1048576 | tf_op jit(solution)/shard_map/hidden/pallas_call | solution.py:75
  48.0 1.2 %collective-permute-done.16 = f32[16,256]{1,0:T(8,128)S(1)} collective-permute-done((f32[16,256]{1,0:T(8,128)S(1)}, f32[16,256]{1,0:T(8,128)S(1)}, u32[]{:S(2)}, u32[]{:S(2)}) %collective-permute-start.16) | collective-permute-done | bytes 16416 | tf_op jit(solution)/shard_map/ppermute | solution.py:289
  49.2 0.5 collective-permute-start.17
  49.7 1.3 %collective-permute-start.18 = (f32[16,256]{1,0:T(8,128)S(1)}, f32[16,256]{1,0:T(8,128)S(1)}, u32[]{:S(2)}, u32[]{:S(2)}) collective-permute-start(f32[16,256]{1,0:T(8,128)S(1)} %add.71), channel_id=1, source_target_pairs={{0,4},{1,5},{2,6},{3,7},{4,0},{5,1},{6,2},{7,3},{8,12},{9,13},{10,... | collective-permute-start | bytes 49160 | tf_op jit(solution)/shard_map/ppermute | solution.py:289
  51.0 1.6 %collective-permute-start.19 = (f32[16,256]{1,0:T(8,128)S(1)}, f32[16,256]{1,0:T(8,128)S(1)}, u32[]{:S(2)}, u32[]{:S(2)}) collective-permute-start(f32[16,256]{1,0:T(8,128)S(1)} %add.71), channel_id=1, source_target_pairs={{0,6},{1,7},{2,4},{3,5},{4,2},{5,3},{6,0},{7,1},{8,14},{9,15},{10,... | collective-permute-start | bytes 49160 | tf_op jit(solution)/shard_map/ppermute | solution.py:289
  52.7 2.4 %merged.4.merged_ref = f32[256,1024]{1,0:T(8,128)S(1)} custom-call(f32[256,128]{1,0:T(8,128)S(1)} %get-tuple-element.59.block_ref, bf16[256,4096]{1,0:T(8,128)(2,1)S(1)} %get-tuple-element.60.hidden_ref, bf16[1024,4096]{1,0:T(8,128)(2,1)S(1)} %get-tuple-element.46.refs_8_.w_in_ref), custom_call_target="tpu_custom_call" | custom-call | flops 2147483648 | bytes 1048576 | tf_op jit(solution)/shard_map/merged/pallas_call | solution.py:75
  55.1 0.6 collective-permute-done.19
  55.7 0.3 right.4
  56.0 1.3 %collective-permute-done.20 = f32[16,1024]{1,0:T(8,128)S(1)} collective-permute-done((f32[16,1024]{1,0:T(8,128)S(1)}, f32[16,1024]{1,0:T(8,128)S(1)}, u32[]{:S(2)}, u32[]{:S(2)}) %collective-permute-start.20) | collective-permute-done | bytes 65568 | tf_op jit(solution)/shard_map/ppermute | solution.py:289
  57.3 1.6 %collective-permute-start.21 = (f32[16,1024]{1,0:T(8,128)S(1)}, f32[16,1024]{1,0:T(8,128)S(1)}, u32[]{:S(2)}, u32[]{:S(2)}) collective-permute-start(f32[16,1024]{1,0:T(8,128)S(1)} %add.75), channel_id=1, source_target_pairs={{0,2},{1,3},{2,0},{3,1},{4,6},{5,7},{6,4},{7,5},{8,10},{9,11},{10,... | collective-permute-start | bytes 196616 | tf_op jit(solution)/shard_map/ppermute | solution.py:289
  58.8 0.7 collective-permute-start.22
  59.5 1.3 %collective-permute-start.23 = (f32[16,1024]{1,0:T(8,128)S(1)}, f32[16,1024]{1,0:T(8,128)S(1)}, u32[]{:S(2)}, u32[]{:S(2)}) collective-permute-start(f32[16,1024]{1,0:T(8,128)S(1)} %add.75), channel_id=1, source_target_pairs={{0,6},{1,7},{2,4},{3,5},{4,2},{5,3},{6,0},{7,1},{8,14},{9,15},{10,... | collective-permute-start | bytes 196616 | tf_op jit(solution)/shard_map/ppermute | solution.py:289
  60.8 1.6 %factor.4 = (f32[16,256]{1,0:T(8,128)S(1)}, f32[16,16]{1,0:T(8,128)S(1)}) custom-call(f32[16,256]{1,0:T(8,128)S(1)} %add_add_fusion.3.proj_ref), custom_call_target="tpu_custom_call" | custom-call | flops 1073741824 | bytes 1048576 | tf_op jit(solution)/shard_map/factor/pallas_call | solution.py:75
  62.4 1.4 %collective-permute-done.22 = f32[16,1024]{1,0:T(8,128)S(1)} collective-permute-done((f32[16,1024]{1,0:T(8,128)S(1)}, f32[16,1024]{1,0:T(8,128)S(1)}, u32[]{:S(2)}, u32[]{:S(2)}) %collective-permute-start.22) | collective-permute-done | bytes 65568 | tf_op jit(solution)/shard_map/ppermute | solution.py:289
  63.8 0.9 collective-permute-done.23
  64.9 1.5 %collective-permute-start.24 = (f32[16,1280]{1,0:T(8,128)S(1)}, f32[16,1280]{1,0:T(8,128)S(1)}, u32[]{:S(2)}, u32[]{:S(2)}) collective-permute-start(f32[16,1280]{1,0:T(8,128)S(1)} %get-tuple-element.61.refs_9_), channel_id=1, source_target_pairs={{8,0},{16,8},{24,16},{9,1},{17,9},{25,17},{10,2},{18,10},{26,18},{... | collective-permute-start | bytes 245768 | tf_op jit(solution)/shard_map/ppermute | solution.py:446
  66.4 2.4 %mask.3.mask_ref = bf16[256,4096]{1,0:T(8,128)(2,1)S(1)} custom-call(bf16[3,32,1024]{2,1,0:T(8,128)(2,1)S(1)} %bitcast.28, bf16[3,32,1024]{2,1,0:T(8,128)(2,1)S(1)} %collective-permute-done.refs_1_, bf16[3,32,1024]{2,1,0:T(8,128)(2,1)S(1)} %collective-permute-done.1.refs_2_, bf16[3,32,1024]{2,1,0:T(8,128)(2,1)S(1)} %collective-permute-done.2.refs_3_, ...), custom_call_target="tpu_custom_call" | custom-call | flops 2147483648 | bytes 1048576 | tf_op jit(solution)/shard_map/mask/pallas_call | solution.py:75
  68.8 1.4 %warm.3.warm_in_ref = bf16[32,4096]{1,0:T(8,128)(2,1)S(1)} custom-call(f32[16,1024]{1,0:T(8,128)S(1)} %get-tuple-element.62.warm_ref, bf16[1024,4096]{1,0:T(8,128)(2,1)S(1)} %get-tuple-element.46.refs_8_.w_in_ref), custom_call_target="tpu_custom_call" | custom-call | flops 1073741824 | bytes 1048576 | tf_op jit(solution)/shard_map/warm/pallas_call | solution.py:75
  70.2 1.0 %collective-permute-done.24.both_ref = f32[16,1280]{1,0:T(8,128)S(1)} collective-permute-done((f32[16,1280]{1,0:T(8,128)S(1)}, f32[16,1280]{1,0:T(8,128)S(1)}, u32[]{:S(2)}, u32[]{:S(2)}) %collective-permute-start.24) | collective-permute-done | bytes 81952 | tf_op jit(solution)/shard_map/ppermute | solution.py:446
  71.2 3.7 %hidden.3 = (bf16[256,4096]{1,0:T(8,128)(2,1)S(1)}, f32[16,256]{1,0:T(8,128)S(1)}, f32[256,128]{1,0:T(8,128)S(1)}) custom-call(f32[3,16,256]{2,1,0:T(8,128)S(1)} %bitcast.34, f32[3,16,1024]{2,1,0:T(8,128)S(1)} %bitcast.31, f32[16,1280]{1,0:T(8,128)S(1)} %collective-permute-done.24.both_ref, f32[16,1024]{1,0:T(8,128)S(1)} %get-tuple-element.62.warm_ref, ...), custom_call_target="tpu_custom_call" | custom-call | flops 2147483648 | bytes 1048576 | tf_op jit(solution)/shard_map/hidden/pallas_call | solution.py:75
  75.0 1.2 %collective-permute-done.25 = f32[16,256]{1,0:T(8,128)S(1)} collective-permute-done((f32[16,256]{1,0:T(8,128)S(1)}, f32[16,256]{1,0:T(8,128)S(1)}, u32[]{:S(2)}, u32[]{:S(2)}) %collective-permute-start.25) | collective-permute-done | bytes 16416 | tf_op jit(solution)/shard_map/ppermute | solution.py:289
  76.2 0.6 collective-permute-start.26
  76.7 1.3 %collective-permute-start.27 = (f32[16,256]{1,0:T(8,128)S(1)}, f32[16,256]{1,0:T(8,128)S(1)}, u32[]{:S(2)}, u32[]{:S(2)}) collective-permute-start(f32[16,256]{1,0:T(8,128)S(1)} %add.79), channel_id=1, source_target_pairs={{0,4},{1,5},{2,6},{3,7},{4,0},{5,1},{6,2},{7,3},{8,12},{9,13},{10,... | collective-permute-start | bytes 49160 | tf_op jit(solution)/shard_map/ppermute | solution.py:289
  78.0 1.6 %collective-permute-start.28 = (f32[16,256]{1,0:T(8,128)S(1)}, f32[16,256]{1,0:T(8,128)S(1)}, u32[]{:S(2)}, u32[]{:S(2)}) collective-permute-start(f32[16,256]{1,0:T(8,128)S(1)} %add.79), channel_id=1, source_target_pairs={{0,6},{1,7},{2,4},{3,5},{4,2},{5,3},{6,0},{7,1},{8,14},{9,15},{10,... | collective-permute-start | bytes 49160 | tf_op jit(solution)/shard_map/ppermute | solution.py:289
  79.7 2.4 %merged.5.merged_ref = f32[256,1024]{1,0:T(8,128)S(1)} custom-call(f32[256,128]{1,0:T(8,128)S(1)} %get-tuple-element.65.block_ref, bf16[256,4096]{1,0:T(8,128)(2,1)S(1)} %get-tuple-element.66.hidden_ref, bf16[1024,4096]{1,0:T(8,128)(2,1)S(1)} %get-tuple-element.46.refs_8_.w_in_ref), custom_call_target="tpu_custom_call" | custom-call | flops 2147483648 | bytes 1048576 | tf_op jit(solution)/shard_map/merged/pallas_call | solution.py:75
  82.2 0.5 collective-permute-done.28
  82.7 0.3 right.5.right_ref
  83.0 1.2 %collective-permute-done.30.right_arrived_ref = f32[16,1024]{1,0:T(8,128)S(1)} collective-permute-done((f32[16,1024]{1,0:T(8,128)S(1)}, f32[16,1024]{1,0:T(8,128)S(1)}, u32[]{:S(2)}, u32[]{:S(2)}) %collective-permute-start.30) | collective-permute-done | bytes 65568 | tf_op jit(solution)/shard_map/ppermute | solution.py:289
  84.3 1.6 %collective-permute-start.31 = (bf16[64,1024]{1,0:T(8,128)(2,1)S(1)}, bf16[64,1024]{1,0:T(8,128)(2,1)S(1)}, u32[]{:S(2)}, u32[]{:S(2)}) collective-permute-start(bf16[64,1024]{1,0:T(8,128)(2,1)S(1)} %get-tuple-element.69), channel_id=1, source_target_pairs={{0,2},{1,3},{2,0},{3,1},{4,6},{5,7},{6,4},{7,5},{8,10},{9,11},{10,... | collective-permute-start | bytes 393224 | tf_op jit(solution)/shard_map/ppermute | solution.py:289
  85.9 0.7 collective-permute-start.32
  86.6 1.3 %collective-permute-start.33 = (bf16[64,1024]{1,0:T(8,128)(2,1)S(1)}, bf16[64,1024]{1,0:T(8,128)(2,1)S(1)}, u32[]{:S(2)}, u32[]{:S(2)}) collective-permute-start(bf16[64,1024]{1,0:T(8,128)(2,1)S(1)} %get-tuple-element.71), channel_id=1, source_target_pairs={{0,6},{1,7},{2,4},{3,5},{4,2},{5,3},{6,0},{7,1},{8,14},{9,15},{10,... | collective-permute-start | bytes 393224 | tf_op jit(solution)/shard_map/ppermute | solution.py:289
  87.9 1.6 %factor.5 = (f32[16,256]{1,0:T(8,128)S(1)}, f32[16,16]{1,0:T(8,128)S(1)}) custom-call(f32[16,256]{1,0:T(8,128)S(1)} %add_add_fusion.2.proj_ref), custom_call_target="tpu_custom_call" | custom-call | flops 1073741824 | bytes 1048576 | tf_op jit(solution)/shard_map/factor/pallas_call | solution.py:75
  89.4 0.7 dynamic-slice_bitcast_fusion
  90.3 3.7 %collective-permute-done.32.refs_1_ = bf16[64,1024]{1,0:T(8,128)(2,1)S(1)} collective-permute-done((bf16[64,1024]{1,0:T(8,128)(2,1)S(1)}, bf16[64,1024]{1,0:T(8,128)(2,1)S(1)}, u32[]{:S(2)}, u32[]{:S(2)}) %collective-permute-start.32) | collective-permute-done | bytes 131104 | tf_op jit(solution)/shard_map/ppermute | solution.py:289
  94.0 0.9 last.1
  (52 shorter events, 1.8 us)
Async XLA Ops:
  0.6 14.0 %collective-permute-start = (bf16[3,32,1024]{2,1,0:T(8,128)(2,1)}, bf16[3,32,1024]{2,1,0:T(8,128)(2,1)S(1)}, u32[]{:S(2)}, u32[]{:S(2)}) collective-permute-start(bf16[3,32,1024]{2,1,0:T(8,128)(2,1)} %bitcast.22), channel_id=1, source_target_pairs={{0,2},{1,3},{2,0},{3,1},{4,6},{5,7},{6,4},{7,5},{8,10},{9,11},{10,... | collective-permute-start | bytes 589832 | tf_op jit(solution)/shard_map/ppermute | solution.py:289
  3.6 11.0 %collective-permute-start.1 = (bf16[3,32,1024]{2,1,0:T(8,128)(2,1)}, bf16[3,32,1024]{2,1,0:T(8,128)(2,1)S(1)}, u32[]{:S(2)}, u32[]{:S(2)}) collective-permute-start(bf16[3,32,1024]{2,1,0:T(8,128)(2,1)} %bitcast.23), channel_id=1, source_target_pairs={{0,4},{1,5},{2,6},{3,7},{4,0},{5,1},{6,2},{7,3},{8,12},{9,13},{10,... | collective-permute-start | bytes 589832 | tf_op jit(solution)/shard_map/ppermute | solution.py:289
  5.2 9.5 %collective-permute-start.2 = (bf16[3,32,1024]{2,1,0:T(8,128)(2,1)}, bf16[3,32,1024]{2,1,0:T(8,128)(2,1)S(1)}, u32[]{:S(2)}, u32[]{:S(2)}) collective-permute-start(bf16[3,32,1024]{2,1,0:T(8,128)(2,1)} %bitcast.24), channel_id=1, source_target_pairs={{0,6},{1,7},{2,4},{3,5},{4,2},{5,3},{6,0},{7,1},{8,14},{9,15},{10,... | collective-permute-start | bytes 589832 | tf_op jit(solution)/shard_map/ppermute | solution.py:289
  5.2 0.8 copy-start.3
  6.0 3.9 %copy-start.1 = (f32[3,1024,16]{1,2,0:T(8,128)S(1)}, f32[3,1024,16]{1,2,0:T(8,128)}, u32[]{:S(2)}) copy-start(f32[3,1024,16]{1,2,0:T(8,128)} %param.15) | copy-start | bytes 589828
  6.0 3.9 %copy-start.2 = (f32[3,256,16]{1,2,0:T(8,128)S(1)}, f32[3,256,16]{1,2,0:T(8,128)}, u32[]{:S(2)}) copy-start(f32[3,256,16]{1,2,0:T(8,128)} %param.14) | copy-start | bytes 147460
  6.0 3.9 %copy-start.4 = (f32[1,1024,16]{1,2,0:T(8,128)S(1)}, f32[1,1024,16]{1,2,0:T(8,128)}, u32[]{:S(2)}) copy-start(f32[1,1024,16]{1,2,0:T(8,128)} %param.11) | copy-start | bytes 196612
  6.0 3.9 %copy-start.5 = (f32[1,1024,16]{1,2,0:T(8,128)S(1)}, f32[1,1024,16]{1,2,0:T(8,128)}, u32[]{:S(2)}) copy-start(f32[1,1024,16]{1,2,0:T(8,128)} %param.13) | copy-start | bytes 196612
  6.0 3.9 %copy-start.6 = (f32[1,256,16]{1,2,0:T(8,128)S(1)}, f32[1,256,16]{1,2,0:T(8,128)}, u32[]{:S(2)}) copy-start(f32[1,256,16]{1,2,0:T(8,128)} %param.12) | copy-start | bytes 49156
  10.0 4.7 %copy-start = (bf16[1,3,32,1024]{3,2,1,0:T(8,128)(2,1)S(1)}, bf16[1,3,32,1024]{3,2,1,0:T(8,128)(2,1)}, u32[]{:S(2)}) copy-start(bf16[1,3,32,1024]{3,2,1,0:T(8,128)(2,1)} %param.8) | copy-start | bytes 589828
  14.7 1.5 %collective-permute-start.3 = (bf16[3,32,1024]{2,1,0:T(8,128)(2,1)S(1)}, bf16[3,32,1024]{2,1,0:T(8,128)(2,1)S(1)}, u32[]{:S(2)}, u32[]{:S(2)}) collective-permute-start(bf16[3,32,1024]{2,1,0:T(8,128)(2,1)S(1)} %bitcast.25), channel_id=1, source_target_pairs={{0,1},{1,0},{2,3},{3,2},{4,5},{5,4},{6,7},{7,6},{8,9},{9,8},{10,11... | collective-permute-start | bytes 589832 | tf_op jit(solution)/shard_map/ppermute | solution.py:289
  14.8 1.7 %collective-permute-start.4 = (bf16[3,32,1024]{2,1,0:T(8,128)(2,1)S(1)}, bf16[3,32,1024]{2,1,0:T(8,128)(2,1)S(1)}, u32[]{:S(2)}, u32[]{:S(2)}) collective-permute-start(bf16[3,32,1024]{2,1,0:T(8,128)(2,1)S(1)} %collective-permute-done.refs_1_), channel_id=1, source_target_pairs={{0,1},{1,0},{2,3},{3,2},{4,5},{5,4},{6,7},{7,6},{8,9},{9,8},{10,11... | collective-permute-start | bytes 589832 | tf_op jit(solution)/shard_map/ppermute | solution.py:289
  15.3 1.5 %collective-permute-start.5 = (bf16[3,32,1024]{2,1,0:T(8,128)(2,1)S(1)}, bf16[3,32,1024]{2,1,0:T(8,128)(2,1)S(1)}, u32[]{:S(2)}, u32[]{:S(2)}) collective-permute-start(bf16[3,32,1024]{2,1,0:T(8,128)(2,1)S(1)} %collective-permute-done.1.refs_2_), channel_id=1, source_target_pairs={{0,1},{1,0},{2,3},{3,2},{4,5},{5,4},{6,7},{7,6},{8,9},{9,8},{10,11... | collective-permute-start | bytes 589832 | tf_op jit(solution)/shard_map/ppermute | solution.py:289
  15.4 1.7 %collective-permute-start.6 = (bf16[3,32,1024]{2,1,0:T(8,128)(2,1)S(1)}, bf16[3,32,1024]{2,1,0:T(8,128)(2,1)S(1)}, u32[]{:S(2)}, u32[]{:S(2)}) collective-permute-start(bf16[3,32,1024]{2,1,0:T(8,128)(2,1)S(1)} %collective-permute-done.2.refs_3_), channel_id=1, source_target_pairs={{0,1},{1,0},{2,3},{3,2},{4,5},{5,4},{6,7},{7,6},{8,9},{9,8},{10,11... | collective-permute-start | bytes 589832 | tf_op jit(solution)/shard_map/ppermute | solution.py:289
  20.2 1.2 %collective-permute-start.7 = (f32[16,256]{1,0:T(8,128)S(1)}, f32[16,256]{1,0:T(8,128)S(1)}, u32[]{:S(2)}, u32[]{:S(2)}) collective-permute-start(f32[16,256]{1,0:T(8,128)S(1)} %get-tuple-element.48), channel_id=1, source_target_pairs={{0,1},{1,0},{2,3},{3,2},{4,5},{5,4},{6,7},{7,6},{8,9},{9,8},{10,11... | collective-permute-start | bytes 49160 | tf_op jit(solution)/shard_map/ppermute | solution.py:289
  21.5 5.9 %collective-permute-start.10 = (f32[16,256]{1,0:T(8,128)S(1)}, f32[16,256]{1,0:T(8,128)S(1)}, u32[]{:S(2)}, u32[]{:S(2)}) collective-permute-start(f32[16,256]{1,0:T(8,128)S(1)} %add.63), channel_id=1, source_target_pairs={{0,6},{1,7},{2,4},{3,5},{4,2},{5,3},{6,0},{7,1},{8,14},{9,15},{10,... | collective-permute-start | bytes 49160 | tf_op jit(solution)/shard_map/ppermute | solution.py:289
  24.4 3.7 %collective-permute-start.8 = (f32[16,256]{1,0:T(8,128)S(1)}, f32[16,256]{1,0:T(8,128)S(1)}, u32[]{:S(2)}, u32[]{:S(2)}) collective-permute-start(f32[16,256]{1,0:T(8,128)S(1)} %add.63), channel_id=1, source_target_pairs={{0,2},{1,3},{2,0},{3,1},{4,6},{5,7},{6,4},{7,5},{8,10},{9,11},{10,... | collective-permute-start | bytes 49160 | tf_op jit(solution)/shard_map/ppermute | solution.py:289
  24.9 3.7 %collective-permute-start.9 = (f32[16,256]{1,0:T(8,128)S(1)}, f32[16,256]{1,0:T(8,128)S(1)}, u32[]{:S(2)}, u32[]{:S(2)}) collective-permute-start(f32[16,256]{1,0:T(8,128)S(1)} %add.63), channel_id=1, source_target_pairs={{0,4},{1,5},{2,6},{3,7},{4,0},{5,1},{6,2},{7,3},{8,12},{9,13},{10,... | collective-permute-start | bytes 49160 | tf_op jit(solution)/shard_map/ppermute | solution.py:289
  29.0 1.3 %collective-permute-start.11 = (f32[16,1024]{1,0:T(8,128)S(1)}, f32[16,1024]{1,0:T(8,128)S(1)}, u32[]{:S(2)}, u32[]{:S(2)}) collective-permute-start(f32[16,1024]{1,0:T(8,128)S(1)} %right.3), channel_id=1, source_target_pairs={{0,1},{1,0},{2,3},{3,2},{4,5},{5,4},{6,7},{7,6},{8,9},{9,8},{10,11... | collective-permute-start | bytes 196616 | tf_op jit(solution)/shard_map/ppermute | solution.py:289
  30.3 5.1 %collective-permute-start.12 = (f32[16,1024]{1,0:T(8,128)S(1)}, f32[16,1024]{1,0:T(8,128)S(1)}, u32[]{:S(2)}, u32[]{:S(2)}) collective-permute-start(f32[16,1024]{1,0:T(8,128)S(1)} %add.67), channel_id=1, source_target_pairs={{0,2},{1,3},{2,0},{3,1},{4,6},{5,7},{6,4},{7,5},{8,10},{9,11},{10,... | collective-permute-start | bytes 196616 | tf_op jit(solution)/shard_map/ppermute | solution.py:289
  31.8 5.0 %collective-permute-start.13 = (f32[16,1024]{1,0:T(8,128)S(1)}, f32[16,1024]{1,0:T(8,128)S(1)}, u32[]{:S(2)}, u32[]{:S(2)}) collective-permute-start(f32[16,1024]{1,0:T(8,128)S(1)} %add.67), channel_id=1, source_target_pairs={{0,4},{1,5},{2,6},{3,7},{4,0},{5,1},{6,2},{7,3},{8,12},{9,13},{10,... | collective-permute-start | bytes 196616 | tf_op jit(solution)/shard_map/ppermute | solution.py:289
  32.5 5.2 %collective-permute-start.14 = (f32[16,1024]{1,0:T(8,128)S(1)}, f32[16,1024]{1,0:T(8,128)S(1)}, u32[]{:S(2)}, u32[]{:S(2)}) collective-permute-start(f32[16,1024]{1,0:T(8,128)S(1)} %add.67), channel_id=1, source_target_pairs={{0,6},{1,7},{2,4},{3,5},{4,2},{5,3},{6,0},{7,1},{8,14},{9,15},{10,... | collective-permute-start | bytes 196616 | tf_op jit(solution)/shard_map/ppermute | solution.py:289
  37.9 6.3 %collective-permute-start.15 = (f32[16,1280]{1,0:T(8,128)S(1)}, f32[16,1280]{1,0:T(8,128)S(1)}, u32[]{:S(2)}, u32[]{:S(2)}) collective-permute-start(f32[16,1280]{1,0:T(8,128)S(1)} %get-tuple-element.53.refs_9_), channel_id=1, source_target_pairs={{8,0},{16,8},{24,16},{9,1},{17,9},{25,17},{10,2},{18,10},{26,18},{... | collective-permute-start | bytes 245768 | tf_op jit(solution)/shard_map/ppermute | solution.py:446
  47.9 1.2 %collective-permute-start.16 = (f32[16,256]{1,0:T(8,128)S(1)}, f32[16,256]{1,0:T(8,128)S(1)}, u32[]{:S(2)}, u32[]{:S(2)}) collective-permute-start(f32[16,256]{1,0:T(8,128)S(1)} %get-tuple-element.56), channel_id=1, source_target_pairs={{0,1},{1,0},{2,3},{3,2},{4,5},{5,4},{6,7},{7,6},{8,9},{9,8},{10,11... | collective-permute-start | bytes 49160 | tf_op jit(solution)/shard_map/ppermute | solution.py:289
  49.2 5.9 %collective-permute-start.17 = (f32[16,256]{1,0:T(8,128)S(1)}, f32[16,256]{1,0:T(8,128)S(1)}, u32[]{:S(2)}, u32[]{:S(2)}) collective-permute-start(f32[16,256]{1,0:T(8,128)S(1)} %add.71), channel_id=1, source_target_pairs={{0,2},{1,3},{2,0},{3,1},{4,6},{5,7},{6,4},{7,5},{8,10},{9,11},{10,... | collective-permute-start | bytes 49160 | tf_op jit(solution)/shard_map/ppermute | solution.py:289
  49.7 5.3 %collective-permute-start.18 = (f32[16,256]{1,0:T(8,128)S(1)}, f32[16,256]{1,0:T(8,128)S(1)}, u32[]{:S(2)}, u32[]{:S(2)}) collective-permute-start(f32[16,256]{1,0:T(8,128)S(1)} %add.71), channel_id=1, source_target_pairs={{0,4},{1,5},{2,6},{3,7},{4,0},{5,1},{6,2},{7,3},{8,12},{9,13},{10,... | collective-permute-start | bytes 49160 | tf_op jit(solution)/shard_map/ppermute | solution.py:289
  51.0 4.6 %collective-permute-start.19 = (f32[16,256]{1,0:T(8,128)S(1)}, f32[16,256]{1,0:T(8,128)S(1)}, u32[]{:S(2)}, u32[]{:S(2)}) collective-permute-start(f32[16,256]{1,0:T(8,128)S(1)} %add.71), channel_id=1, source_target_pairs={{0,6},{1,7},{2,4},{3,5},{4,2},{5,3},{6,0},{7,1},{8,14},{9,15},{10,... | collective-permute-start | bytes 49160 | tf_op jit(solution)/shard_map/ppermute | solution.py:289
  56.0 1.3 %collective-permute-start.20 = (f32[16,1024]{1,0:T(8,128)S(1)}, f32[16,1024]{1,0:T(8,128)S(1)}, u32[]{:S(2)}, u32[]{:S(2)}) collective-permute-start(f32[16,1024]{1,0:T(8,128)S(1)} %right.4), channel_id=1, source_target_pairs={{0,1},{1,0},{2,3},{3,2},{4,5},{5,4},{6,7},{7,6},{8,9},{9,8},{10,11... | collective-permute-start | bytes 196616 | tf_op jit(solution)/shard_map/ppermute | solution.py:289
  57.3 5.1 %collective-permute-start.21 = (f32[16,1024]{1,0:T(8,128)S(1)}, f32[16,1024]{1,0:T(8,128)S(1)}, u32[]{:S(2)}, u32[]{:S(2)}) collective-permute-start(f32[16,1024]{1,0:T(8,128)S(1)} %add.75), channel_id=1, source_target_pairs={{0,2},{1,3},{2,0},{3,1},{4,6},{5,7},{6,4},{7,5},{8,10},{9,11},{10,... | collective-permute-start | bytes 196616 | tf_op jit(solution)/shard_map/ppermute | solution.py:289
  58.8 5.0 %collective-permute-start.22 = (f32[16,1024]{1,0:T(8,128)S(1)}, f32[16,1024]{1,0:T(8,128)S(1)}, u32[]{:S(2)}, u32[]{:S(2)}) collective-permute-start(f32[16,1024]{1,0:T(8,128)S(1)} %add.75), channel_id=1, source_target_pairs={{0,4},{1,5},{2,6},{3,7},{4,0},{5,1},{6,2},{7,3},{8,12},{9,13},{10,... | collective-permute-start | bytes 196616 | tf_op jit(solution)/shard_map/ppermute | solution.py:289
  59.5 5.2 %collective-permute-start.23 = (f32[16,1024]{1,0:T(8,128)S(1)}, f32[16,1024]{1,0:T(8,128)S(1)}, u32[]{:S(2)}, u32[]{:S(2)}) collective-permute-start(f32[16,1024]{1,0:T(8,128)S(1)} %add.75), channel_id=1, source_target_pairs={{0,6},{1,7},{2,4},{3,5},{4,2},{5,3},{6,0},{7,1},{8,14},{9,15},{10,... | collective-permute-start | bytes 196616 | tf_op jit(solution)/shard_map/ppermute | solution.py:289
  64.9 6.3 %collective-permute-start.24 = (f32[16,1280]{1,0:T(8,128)S(1)}, f32[16,1280]{1,0:T(8,128)S(1)}, u32[]{:S(2)}, u32[]{:S(2)}) collective-permute-start(f32[16,1280]{1,0:T(8,128)S(1)} %get-tuple-element.61.refs_9_), channel_id=1, source_target_pairs={{8,0},{16,8},{24,16},{9,1},{17,9},{25,17},{10,2},{18,10},{26,18},{... | collective-permute-start | bytes 245768 | tf_op jit(solution)/shard_map/ppermute | solution.py:446
  74.9 1.2 %collective-permute-start.25 = (f32[16,256]{1,0:T(8,128)S(1)}, f32[16,256]{1,0:T(8,128)S(1)}, u32[]{:S(2)}, u32[]{:S(2)}) collective-permute-start(f32[16,256]{1,0:T(8,128)S(1)} %get-tuple-element.63), channel_id=1, source_target_pairs={{0,1},{1,0},{2,3},{3,2},{4,5},{5,4},{6,7},{7,6},{8,9},{9,8},{10,11... | collective-permute-start | bytes 49160 | tf_op jit(solution)/shard_map/ppermute | solution.py:289
  76.2 6.0 %collective-permute-start.26 = (f32[16,256]{1,0:T(8,128)S(1)}, f32[16,256]{1,0:T(8,128)S(1)}, u32[]{:S(2)}, u32[]{:S(2)}) collective-permute-start(f32[16,256]{1,0:T(8,128)S(1)} %add.79), channel_id=1, source_target_pairs={{0,2},{1,3},{2,0},{3,1},{4,6},{5,7},{6,4},{7,5},{8,10},{9,11},{10,... | collective-permute-start | bytes 49160 | tf_op jit(solution)/shard_map/ppermute | solution.py:289
  76.7 5.4 %collective-permute-start.27 = (f32[16,256]{1,0:T(8,128)S(1)}, f32[16,256]{1,0:T(8,128)S(1)}, u32[]{:S(2)}, u32[]{:S(2)}) collective-permute-start(f32[16,256]{1,0:T(8,128)S(1)} %add.79), channel_id=1, source_target_pairs={{0,4},{1,5},{2,6},{3,7},{4,0},{5,1},{6,2},{7,3},{8,12},{9,13},{10,... | collective-permute-start | bytes 49160 | tf_op jit(solution)/shard_map/ppermute | solution.py:289
  78.0 4.6 %collective-permute-start.28 = (f32[16,256]{1,0:T(8,128)S(1)}, f32[16,256]{1,0:T(8,128)S(1)}, u32[]{:S(2)}, u32[]{:S(2)}) collective-permute-start(f32[16,256]{1,0:T(8,128)S(1)} %add.79), channel_id=1, source_target_pairs={{0,6},{1,7},{2,4},{3,5},{4,2},{5,3},{6,0},{7,1},{8,14},{9,15},{10,... | collective-permute-start | bytes 49160 | tf_op jit(solution)/shard_map/ppermute | solution.py:289
  82.1 2.2 %collective-permute-start.29 = (bf16[4,32,1024]{2,1,0:T(8,128)(2,1)S(1)}, bf16[4,32,1024]{2,1,0:T(8,128)(2,1)S(1)}, u32[]{:S(2)}, u32[]{:S(2)}) collective-permute-start(bf16[4,32,1024]{2,1,0:T(8,128)(2,1)S(1)} %outgoing.1), channel_id=1, source_target_pairs={{0,1},{1,0},{2,3},{3,2},{4,5},{5,4},{6,7},{7,6},{8,9},{9,8},{10,11... | collective-permute-start | bytes 786440 | tf_op jit(solution)/shard_map/ppermute | solution.py:289
  83.0 1.3 %collective-permute-start.30 = (f32[16,1024]{1,0:T(8,128)S(1)}, f32[16,1024]{1,0:T(8,128)S(1)}, u32[]{:S(2)}, u32[]{:S(2)}) collective-permute-start(f32[16,1024]{1,0:T(8,128)S(1)} %right.5.right_ref), channel_id=1, source_target_pairs={{0,1},{1,0},{2,3},{3,2},{4,5},{5,4},{6,7},{7,6},{8,9},{9,8},{10,11... | collective-permute-start | bytes 196616 | tf_op jit(solution)/shard_map/ppermute | solution.py:289
  84.3 6.0 %collective-permute-start.31 = (bf16[64,1024]{1,0:T(8,128)(2,1)S(1)}, bf16[64,1024]{1,0:T(8,128)(2,1)S(1)}, u32[]{:S(2)}, u32[]{:S(2)}) collective-permute-start(bf16[64,1024]{1,0:T(8,128)(2,1)S(1)} %get-tuple-element.69), channel_id=1, source_target_pairs={{0,2},{1,3},{2,0},{3,1},{4,6},{5,7},{6,4},{7,5},{8,10},{9,11},{10,... | collective-permute-start | bytes 393224 | tf_op jit(solution)/shard_map/ppermute | solution.py:289
  85.9 8.1 %collective-permute-start.32 = (bf16[64,1024]{1,0:T(8,128)(2,1)S(1)}, bf16[64,1024]{1,0:T(8,128)(2,1)S(1)}, u32[]{:S(2)}, u32[]{:S(2)}) collective-permute-start(bf16[64,1024]{1,0:T(8,128)(2,1)S(1)} %get-tuple-element.70), channel_id=1, source_target_pairs={{0,4},{1,5},{2,6},{3,7},{4,0},{5,1},{6,2},{7,3},{8,12},{9,13},{10,... | collective-permute-start | bytes 393224 | tf_op jit(solution)/shard_map/ppermute | solution.py:289
  86.6 7.4 %collective-permute-start.33 = (bf16[64,1024]{1,0:T(8,128)(2,1)S(1)}, bf16[64,1024]{1,0:T(8,128)(2,1)S(1)}, u32[]{:S(2)}, u32[]{:S(2)}) collective-permute-start(bf16[64,1024]{1,0:T(8,128)(2,1)S(1)} %get-tuple-element.71), channel_id=1, source_target_pairs={{0,6},{1,7},{2,4},{3,5},{4,2},{5,3},{6,0},{7,1},{8,14},{9,15},{10,... | collective-permute-start | bytes 393224 | tf_op jit(solution)/shard_map/ppermute | solution.py:289

commit v3 on v2

--- a/solution.py
+++ b/solution.py
@@ -85,26 +85,18 @@
     return result if many else result[0]
 
 
-def fetch(pairs, sems):
-    copies = [pltpu.make_async_copy(source, target, sems.at[k]) for k, (source, target) in enumerate(pairs)]
-    for copy in copies:
-        copy.start()
-    return copies
-
-
-def up_kernel(
-    in_left, in_right, pend_left, pend_right, warm_ref, w_out,
-    up_ref, block_ref, proj_ref, w_out_ref, right_ref, sems,
-):
-    parts = chunks(w_out_ref.shape[0], 1024)
-    arrivals = fetch([(w_out.at[pl.ds(*part)], w_out_ref.at[pl.ds(*part)]) for part in parts], sems)
+def begin_kernel(rows_ref, first_ref, later_ref):
+    first_ref[...] = rows_ref[0]
+    later_ref[...] = rows_ref[1:]
+
+
+def up_kernel(in_left, in_right, pend_left, pend_right, warm_ref, w_out_ref, up_ref, block_ref, proj_ref, right_ref):
     left = chosen(in_left[0], pend_left[...])
     right_ref[...] = chosen(in_right[0], pend_right[...])
     lefts = left_parts(left)
     own_share(lefts, right_ref, warm_ref, block_ref, proj_ref)
     cotangent_low = cotangent_of(lefts, right_ref[...]).astype(BF16)
-    for part, (start, size) in enumerate(parts):
-        arrivals[part].wait()
+    for start, size in chunks(w_out_ref.shape[0]):
         up_ref[:, start : start + size] = dot(cotangent_low, w_out_ref[start : start + size, :], 1, 1).astype(BF16)
 
 
@@ -131,15 +123,6 @@
         warm_into(stacked, w_in_ref, out_ref, start, size)
 
 
-def enter_kernel(warm_ref, w_in, out_ref, w_in_ref, sems):
-    parts = chunks(w_in_ref.shape[1])
-    arrivals = fetch([(w_in.at[:, pl.ds(*part)], w_in_ref.at[:, pl.ds(*part)]) for part in parts], sems)
-    stacked = split(warm_ref[...])
-    for part, (start, size) in enumerate(parts):
-        arrivals[part].wait()
-        warm_into(stacked, w_in_ref, out_ref, start, size)
-
-
 def place_rows(offsets, pieces, rows_ref):
     block = pieces[0].shape[0]
     for offset, piece in zip(offsets, pieces):
@@ -163,7 +146,7 @@
 def first_kernel(offsets, *refs):
     pieces, rest = refs[: len(offsets)], refs[len(offsets) :]
     w_in_ref, up_ref, warm_in_ref, share_ref, hidden_ref, proj_ref, rows_ref = rest
-    place_rows(offsets, [piece.at[0] for piece in pieces], rows_ref)
+    place_rows(offsets, pieces, rows_ref)
     total = None
     for start, size in chunks(w_in_ref.shape[1]):
         preact = dot(rows_ref[...], w_in_ref[:, start : start + size], 1, 0)
@@ -339,36 +322,29 @@
     plan = stages(count)
     by_rows = rows_own % 16 == 0
     if by_rows:
-        blocks = gather_pieces({0: inputs}, plan[1:])
+        rows_first, rows_later = on_device(
+            begin_kernel,
+            [(inputs.shape[1:], BF16), ((ticks - 1, rows_own, depth), BF16)],
+            (inputs,),
+            8 * full,
+            "begin",
+        )
+        blocks = gather_pieces({0: rows_first}, plan[1:] + plan[:1])
+        later = gather_pieces({0: rows_later}, plan[1:] + plan[:1])
+        offsets, pieces, later = list(blocks), list(blocks.values()), list(later.values())
     else:
-        blocks = {0: lax.all_gather(inputs, "hid", axis=1, tiled=True)}
+        everything = lax.all_gather(inputs, "hid", axis=1, tiled=True)
+        offsets, pieces, later = [0], [everything[0]], [everything[1:]]
     block_form = ((rows, own_width(depth)), F32)
-    sems = [pltpu.SemaphoreType.DMA((len(chunks(hidden_units)),))]
-    warm_in, w_in = on_device(
-        enter_kernel,
-        [((2 * rank, hidden_units), BF16), (w_in.shape, BF16)],
-        (warm, w_in),
-        full,
-        "enter",
-        sems,
-        1,
-        43,
-    )
-    early = lax.optimization_barrier((warm, warm_in))[0]
-    up, block, share, w_out = on_device(
+    warm_in = on_device(warm_kernel, ((2 * rank, hidden_units), BF16), (warm, w_in), full // 2, "warm")
+    up, block, share = on_device(
         up_kernel,
-        [wide, block_form, left_form, (w_out.shape, BF16)],
-        (*incoming, turned(pending_left[0]), turned(pending_right[0]), early, w_out),
+        [wide, block_form, left_form],
+        (*incoming, turned(pending_left[0]), turned(pending_right[0]), warm, w_out),
         full,
         "up",
-        [pltpu.VMEM(*right_form)] + sems,
-        1,
-        38,
+        [pltpu.VMEM(*right_form)],
     )
-    if by_rows:
-        held = lax.optimization_barrier((list(blocks.values()), share))[0]
-        blocks = gather_pieces(zip(blocks, held), plan[:1])
-    offsets, pieces = list(blocks), list(blocks.values())
 
     for tick in range(ticks):
         last = tick + 1 == ticks
@@ -387,9 +363,9 @@
                 warm_kernel, ((2 * rank, hidden_units), BF16), (warm, w_in), full // 2, "warm"
             )
             mask = on_device(
-                functools.partial(mask_kernel, offsets, tick),
+                functools.partial(mask_kernel, offsets, tick - 1),
                 wide,
-                (*pieces, w_in, leaving),
+                (*later, w_in, leaving),
                 full,
                 "mask",
                 scratch,

time: 95 us -> 92.9 us (0.978)
  Pallas kernels: 40.8 us -> 36.5 us
  starting transfers between devices: 30.3 us -> 33.8 us
  waiting for transfers between devices: 21.2 us -> 19.8 us
    pallas_call x23 -> x24, Pallas kernels: 40.8 us -> 36.5 us  [on_device(): pl.pallas_call(kernel, out_shape=shapes, in_specs=[VMEM] * (len(operands)...]
    ppermute x32 -> x39, starting transfers between devices: 27.3 us -> 30.8 us  [flip(): lax.ppermute(value, axis, [(source, source ^ bits) for source in range(co...]
    ppermute x32 -> x39, waiting for transfers between devices: 19.2 us -> 17.4 us  [flip(): lax.ppermute(value, axis, [(source, source ^ bits) for source in range(co...]
  transfers between devices with their start and end apart: 34 -> 41, of which waited for: 22 -> 17; matrix products, arithmetic and copies ran while one was open for 1% -> 1% of each run, Pallas kernels for 30% -> 26%
where the time goes in v3:
time: 92.9 us; the launch traced here: 92.7 us
  Pallas kernels  36.5 us (39%)
  starting transfers between devices  33.8 us (36%)
  waiting for transfers between devices  19.8 us (21%)
  local copies, waits for them, and re-layouts  1.65 us (2%)
  between operations  0.99 us (1%)
    pallas_call x24, Pallas kernels, on_device(): pl.pallas_call(kernel, out_shape=shapes, in_specs=[VMEM] * (len(operands)...  36.5 us
    ppermute x39, starting transfers between devices, flip(): lax.ppermute(value, axis, [(source, source ^ bits) for source in range(co...  30.8 us
    ppermute x39, waiting for transfers between devices, flip(): lax.ppermute(value, axis, [(source, source ^ bits) for source in range(co...  17.4 us
    ppermute x2, starting transfers between devices, body(): lax.ppermute(leaving, 'pipe', [(source, source - 1) for source in range(1...  3 us
    ppermute x2, waiting for transfers between devices, body(): lax.ppermute(leaving, 'pipe', [(source, source - 1) for source in range(1...  2.38 us
  transfers between devices with their start and end apart: 41, of which 17 were waited for; matrix products, arithmetic and copies ran while one was open for 1% of the time, Pallas kernels for 26%

profile of v3, /device:TPU:0, one launch (start us, length us, event | category | flops | bytes accessed | tf_op | source)
XLA Modules:
  0.0 92.7 jit_solution(1746627495953422868)
XLA Ops:
  0.6 0.9 copy-done.7
  1.6 3.0 %collective-permute-start = (bf16[32,1024]{1,0:T(8,128)(2,1)S(1)}, bf16[32,1024]{1,0:T(8,128)(2,1)S(1)}, u32[]{:S(2)}, u32[]{:S(2)}) collective-permute-start(bf16[32,1024]{1,0:T(8,128)(2,1)S(1)} %get-tuple-element.33.refs_0_), channel_id=1, source_target_pairs={{0,2},{1,3},{2,0},{3,1},{4,6},{5,7},{6,4},{7,5},{8,10},{9,11},{10,... | collective-permute-start | bytes 196616 | tf_op jit(solution)/shard_map/ppermute | solution.py:272
  4.6 1.5 %collective-permute-start.1 = (bf16[32,1024]{1,0:T(8,128)(2,1)S(1)}, bf16[32,1024]{1,0:T(8,128)(2,1)S(1)}, u32[]{:S(2)}, u32[]{:S(2)}) collective-permute-start(bf16[32,1024]{1,0:T(8,128)(2,1)S(1)} %get-tuple-element.33.refs_0_), channel_id=1, source_target_pairs={{0,4},{1,5},{2,6},{3,7},{4,0},{5,1},{6,2},{7,3},{8,12},{9,13},{10,... | collective-permute-start | bytes 196616 | tf_op jit(solution)/shard_map/ppermute | solution.py:272
  6.2 2.8 %up.1 = (bf16[256,4096]{1,0:T(8,128)(2,1)S(1)}, f32[256,128]{1,0:T(8,128)S(1)}, f32[16,256]{1,0:T(8,128)S(1)}) custom-call(f32[3,16,256]{2,1,0:T(8,128)S(1)} %bitcast.37, f32[3,16,1024]{2,1,0:T(8,128)S(1)} %bitcast.34, f32[16,256]{1,0:T(8,128)S(1)} %bitcast.43, f32[16,1024]{1,0:T(8,128)S(1)} %bitcast.42, f32[16,1024]{1,0:T(8,128)S(1)} %bitcast.40, ...), custom_call_target="tpu_custom_call" | custom-call | flops 2147483648 | bytes 1048576 | tf_op jit(solution)/shard_map/up/pallas_call | solution.py:75
  9.0 0.6 collective-permute-start.4
  9.7 1.6 %collective-permute-done.2.refs_3_ = bf16[32,1024]{1,0:T(8,128)(2,1)S(1)} collective-permute-done((bf16[32,1024]{1,0:T(8,128)(2,1)S(1)}, bf16[32,1024]{1,0:T(8,128)(2,1)S(1)}, u32[]{:S(2)}, u32[]{:S(2)}) %collective-permute-start.2) | collective-permute-done | bytes 65568 | tf_op jit(solution)/shard_map/ppermute | solution.py:272
  11.3 1.4 %warm.3.refs_10_ = bf16[32,4096]{1,0:T(8,128)(2,1)S(1)} custom-call(f32[16,1024]{1,0:T(8,128)S(1)} %bitcast.41, bf16[1024,4096]{1,0:T(8,128)(2,1)S(1)} %bitcast.22), custom_call_target="tpu_custom_call" | custom-call | flops 1073741824 | bytes 1048576 | tf_op jit(solution)/shard_map/warm/pallas_call | solution.py:75
  12.8 3.2 %first.1 = (bf16[256,4096]{1,0:T(8,128)(2,1)S(1)}, f32[16,256]{1,0:T(8,128)S(1)}) custom-call(bf16[32,1024]{1,0:T(8,128)(2,1)S(1)} %get-tuple-element.33.refs_0_, bf16[32,1024]{1,0:T(8,128)(2,1)S(1)} %collective-permute-done.refs_1_, bf16[32,1024]{1,0:T(8,128)(2,1)S(1)} %collective-permute-done.1.refs_2_, ...), custom_call_target="tpu_custom_call" | custom-call | flops 2147483648 | bytes 1048576 | tf_op jit(solution)/shard_map/first/pallas_call | solution.py:75
  16.0 0.6 collective-permute-start.7
  16.5 0.5 collective-permute-start.16
  17.4 1.5 %collective-permute-start.10 = (f32[16,256]{1,0:T(8,128)S(1)}, f32[16,256]{1,0:T(8,128)S(1)}, u32[]{:S(2)}, u32[]{:S(2)}) collective-permute-start(f32[16,256]{1,0:T(8,128)S(1)} %add.63), channel_id=1, source_target_pairs={{0,6},{1,7},{2,4},{3,5},{4,2},{5,3},{6,0},{7,1},{8,14},{9,15},{10,... | collective-permute-start | bytes 49160 | tf_op jit(solution)/shard_map/ppermute | solution.py:272
  18.9 1.0 %collective-permute-start.8 = (f32[16,256]{1,0:T(8,128)S(1)}, f32[16,256]{1,0:T(8,128)S(1)}, u32[]{:S(2)}, u32[]{:S(2)}) collective-permute-start(f32[16,256]{1,0:T(8,128)S(1)} %add.63), channel_id=1, source_target_pairs={{0,2},{1,3},{2,0},{3,1},{4,6},{5,7},{6,4},{7,5},{8,10},{9,11},{10,... | collective-permute-start | bytes 49160 | tf_op jit(solution)/shard_map/ppermute | solution.py:272
  19.9 1.0 %collective-permute-start.9 = (f32[16,256]{1,0:T(8,128)S(1)}, f32[16,256]{1,0:T(8,128)S(1)}, u32[]{:S(2)}, u32[]{:S(2)}) collective-permute-start(f32[16,256]{1,0:T(8,128)S(1)} %add.63), channel_id=1, source_target_pairs={{0,4},{1,5},{2,6},{3,7},{4,0},{5,1},{6,2},{7,3},{8,12},{9,13},{10,... | collective-permute-start | bytes 49160 | tf_op jit(solution)/shard_map/ppermute | solution.py:272
  20.9 2.4 %merged.3.merged_ref = f32[256,1024]{1,0:T(8,128)S(1)} custom-call(f32[256,128]{1,0:T(8,128)S(1)} %get-tuple-element.39.block_ref, bf16[256,4096]{1,0:T(8,128)(2,1)S(1)} %get-tuple-element.40.hidden_ref, bf16[1024,4096]{1,0:T(8,128)(2,1)S(1)} %bitcast.24), custom_call_target="tpu_custom_call" | custom-call | flops 2147483648 | bytes 1048576 | tf_op jit(solution)/shard_map/merged/pallas_call | solution.py:75
  23.3 0.4 collective-permute-done.9
  23.7 0.3 right.3
  24.0 1.0 %collective-permute-start.17 = (bf16[2,32,1024]{2,1,0:T(8,128)(2,1)S(1)}, bf16[2,32,1024]{2,1,0:T(8,128)(2,1)S(1)}, u32[]{:S(2)}, u32[]{:S(2)}) collective-permute-start(bf16[2,32,1024]{2,1,0:T(8,128)(2,1)S(1)} %get-tuple-element.43.refs_0_), channel_id=1, source_target_pairs={{0,4},{1,5},{2,6},{3,7},{4,0},{5,1},{6,2},{7,3},{8,12},{9,13},{10,... | collective-permute-start | bytes 393224 | tf_op jit(solution)/shard_map/ppermute | solution.py:272
  25.0 1.5 %collective-permute-start.18 = (bf16[2,32,1024]{2,1,0:T(8,128)(2,1)S(1)}, bf16[2,32,1024]{2,1,0:T(8,128)(2,1)S(1)}, u32[]{:S(2)}, u32[]{:S(2)}) collective-permute-start(bf16[2,32,1024]{2,1,0:T(8,128)(2,1)S(1)} %get-tuple-element.43.refs_0_), channel_id=1, source_target_pairs={{0,6},{1,7},{2,4},{3,5},{4,2},{5,3},{6,0},{7,1},{8,14},{9,15},{10,... | collective-permute-start | bytes 393224 | tf_op jit(solution)/shard_map/ppermute | solution.py:272
  26.5 1.1 %collective-permute-start.12 = (f32[16,1024]{1,0:T(8,128)S(1)}, f32[16,1024]{1,0:T(8,128)S(1)}, u32[]{:S(2)}, u32[]{:S(2)}) collective-permute-start(f32[16,1024]{1,0:T(8,128)S(1)} %add.67), channel_id=1, source_target_pairs={{0,2},{1,3},{2,0},{3,1},{4,6},{5,7},{6,4},{7,5},{8,10},{9,11},{10,... | collective-permute-start | bytes 196616 | tf_op jit(solution)/shard_map/ppermute | solution.py:272
  27.6 1.0 %collective-permute-start.13 = (f32[16,1024]{1,0:T(8,128)S(1)}, f32[16,1024]{1,0:T(8,128)S(1)}, u32[]{:S(2)}, u32[]{:S(2)}) collective-permute-start(f32[16,1024]{1,0:T(8,128)S(1)} %add.67), channel_id=1, source_target_pairs={{0,4},{1,5},{2,6},{3,7},{4,0},{5,1},{6,2},{7,3},{8,12},{9,13},{10,... | collective-permute-start | bytes 196616 | tf_op jit(solution)/shard_map/ppermute | solution.py:272
  28.6 1.5 %collective-permute-start.14 = (f32[16,1024]{1,0:T(8,128)S(1)}, f32[16,1024]{1,0:T(8,128)S(1)}, u32[]{:S(2)}, u32[]{:S(2)}) collective-permute-start(f32[16,1024]{1,0:T(8,128)S(1)} %add.67), channel_id=1, source_target_pairs={{0,6},{1,7},{2,4},{3,5},{4,2},{5,3},{6,0},{7,1},{8,14},{9,15},{10,... | collective-permute-start | bytes 196616 | tf_op jit(solution)/shard_map/ppermute | solution.py:272
  30.1 1.6 %factor.3 = (f32[16,256]{1,0:T(8,128)S(1)}, f32[16,16]{1,0:T(8,128)S(1)}) custom-call(f32[16,256]{1,0:T(8,128)S(1)} %add_add_fusion.4.proj_ref), custom_call_target="tpu_custom_call" | custom-call | flops 1073741824 | bytes 1048576 | tf_op jit(solution)/shard_map/factor/pallas_call | solution.py:75
  31.6 2.9 %collective-permute-done.17.refs_2_ = bf16[2,32,1024]{2,1,0:T(8,128)(2,1)S(1)} collective-permute-done((bf16[2,32,1024]{2,1,0:T(8,128)(2,1)S(1)}, bf16[2,32,1024]{2,1,0:T(8,128)(2,1)S(1)}, u32[]{:S(2)}, u32[]{:S(2)}) %collective-permute-start.17) | collective-permute-done | bytes 131104 | tf_op jit(solution)/shard_map/ppermute | solution.py:272
  34.5 0.5 collective-permute-start.20
  35.1 0.4 collective-permute-done.13
  35.8 1.5 %collective-permute-start.15 = (f32[16,1280]{1,0:T(8,128)S(1)}, f32[16,1280]{1,0:T(8,128)S(1)}, u32[]{:S(2)}, u32[]{:S(2)}) collective-permute-start(f32[16,1280]{1,0:T(8,128)S(1)} %get-tuple-element.41.refs_9_), channel_id=1, source_target_pairs={{8,0},{16,8},{24,16},{9,1},{17,9},{25,17},{10,2},{18,10},{26,18},{... | collective-permute-start | bytes 245768 | tf_op jit(solution)/shard_map/ppermute | solution.py:422
  37.3 2.4 %mask.2.mask_ref = bf16[256,4096]{1,0:T(8,128)(2,1)S(1)} custom-call(bf16[2,32,1024]{2,1,0:T(8,128)(2,1)S(1)} %get-tuple-element.43.refs_0_, bf16[2,32,1024]{2,1,0:T(8,128)(2,1)S(1)} %collective-permute-done.16.refs_1_, bf16[2,32,1024]{2,1,0:T(8,128)(2,1)S(1)} %collective-permute-done.17.refs_2_, bf16[2,32,1024]{2,1,0:T(8,128)(2,1)S(1)} %collective-permute-done.18.refs_3_, ...), custom_call_target="tpu_custom_call" | custom-call | flops 2147483648 | bytes 1048576 | tf_op jit(solution)/shard_map/mask/pallas_call | solution.py:75
  39.7 1.4 %warm.4.warm_in_ref = bf16[32,4096]{1,0:T(8,128)(2,1)S(1)} custom-call(f32[16,1024]{1,0:T(8,128)S(1)} %get-tuple-element.42.warm_ref, bf16[1024,4096]{1,0:T(8,128)(2,1)S(1)} %bitcast.26), custom_call_target="tpu_custom_call" | custom-call | flops 1073741824 | bytes 1048576 | tf_op jit(solution)/shard_map/warm/pallas_call | solution.py:75
  41.1 1.4 %collective-permute-done.15.both_ref = f32[16,1280]{1,0:T(8,128)S(1)} collective-permute-done((f32[16,1280]{1,0:T(8,128)S(1)}, f32[16,1280]{1,0:T(8,128)S(1)}, u32[]{:S(2)}, u32[]{:S(2)}) %collective-permute-start.15) | collective-permute-done | bytes 81952 | tf_op jit(solution)/shard_map/ppermute | solution.py:422
  42.5 3.7 %hidden.2 = (bf16[256,4096]{1,0:T(8,128)(2,1)S(1)}, f32[16,256]{1,0:T(8,128)S(1)}, f32[256,128]{1,0:T(8,128)S(1)}) custom-call(f32[3,16,256]{2,1,0:T(8,128)S(1)} %bitcast.38, f32[3,16,1024]{2,1,0:T(8,128)S(1)} %bitcast.35, f32[16,1280]{1,0:T(8,128)S(1)} %collective-permute-done.15.both_ref, f32[16,1024]{1,0:T(8,128)S(1)} %get-tuple-element.42.warm_ref, ...), custom_call_target="tpu_custom_call" | custom-call | flops 2147483648 | bytes 1048576 | tf_op jit(solution)/shard_map/hidden/pallas_call | solution.py:75
  46.3 1.2 %collective-permute-done.23 = f32[16,256]{1,0:T(8,128)S(1)} collective-permute-done((f32[16,256]{1,0:T(8,128)S(1)}, f32[16,256]{1,0:T(8,128)S(1)}, u32[]{:S(2)}, u32[]{:S(2)}) %collective-permute-start.23) | collective-permute-done | bytes 16416 | tf_op jit(solution)/shard_map/ppermute | solution.py:272
  47.4 1.0 %collective-permute-start.24 = (f32[16,256]{1,0:T(8,128)S(1)}, f32[16,256]{1,0:T(8,128)S(1)}, u32[]{:S(2)}, u32[]{:S(2)}) collective-permute-start(f32[16,256]{1,0:T(8,128)S(1)} %add.71), channel_id=1, source_target_pairs={{0,2},{1,3},{2,0},{3,1},{4,6},{5,7},{6,4},{7,5},{8,10},{9,11},{10,... | collective-permute-start | bytes 49160 | tf_op jit(solution)/shard_map/ppermute | solution.py:272
  48.5 1.2 %collective-permute-start.25 = (f32[16,256]{1,0:T(8,128)S(1)}, f32[16,256]{1,0:T(8,128)S(1)}, u32[]{:S(2)}, u32[]{:S(2)}) collective-permute-start(f32[16,256]{1,0:T(8,128)S(1)} %add.71), channel_id=1, source_target_pairs={{0,4},{1,5},{2,6},{3,7},{4,0},{5,1},{6,2},{7,3},{8,12},{9,13},{10,... | collective-permute-start | bytes 49160 | tf_op jit(solution)/shard_map/ppermute | solution.py:272
  49.6 1.3 %collective-permute-start.26 = (f32[16,256]{1,0:T(8,128)S(1)}, f32[16,256]{1,0:T(8,128)S(1)}, u32[]{:S(2)}, u32[]{:S(2)}) collective-permute-start(f32[16,256]{1,0:T(8,128)S(1)} %add.71), channel_id=1, source_target_pairs={{0,6},{1,7},{2,4},{3,5},{4,2},{5,3},{6,0},{7,1},{8,14},{9,15},{10,... | collective-permute-start | bytes 49160 | tf_op jit(solution)/shard_map/ppermute | solution.py:272
  50.9 2.4 %merged.4.merged_ref = f32[256,1024]{1,0:T(8,128)S(1)} custom-call(f32[256,128]{1,0:T(8,128)S(1)} %get-tuple-element.47.block_ref, bf16[256,4096]{1,0:T(8,128)(2,1)S(1)} %get-tuple-element.48.hidden_ref, bf16[1024,4096]{1,0:T(8,128)(2,1)S(1)} %bitcast.27), custom_call_target="tpu_custom_call" | custom-call | flops 2147483648 | bytes 1048576 | tf_op jit(solution)/shard_map/merged/pallas_call | solution.py:75
  53.3 0.9 %collective-permute-done.26 = f32[16,256]{1,0:T(8,128)S(1)} collective-permute-done((f32[16,256]{1,0:T(8,128)S(1)}, f32[16,256]{1,0:T(8,128)S(1)}, u32[]{:S(2)}, u32[]{:S(2)}) %collective-permute-start.26) | collective-permute-done | bytes 16416 | tf_op jit(solution)/shard_map/ppermute | solution.py:272
  54.3 0.3 right.4
  54.6 1.3 %collective-permute-done.27 = f32[16,1024]{1,0:T(8,128)S(1)} collective-permute-done((f32[16,1024]{1,0:T(8,128)S(1)}, f32[16,1024]{1,0:T(8,128)S(1)}, u32[]{:S(2)}, u32[]{:S(2)}) %collective-permute-start.27) | collective-permute-done | bytes 65568 | tf_op jit(solution)/shard_map/ppermute | solution.py:272
  55.9 0.8 collective-permute-start.28
  56.7 1.1 %collective-permute-start.29 = (f32[16,1024]{1,0:T(8,128)S(1)}, f32[16,1024]{1,0:T(8,128)S(1)}, u32[]{:S(2)}, u32[]{:S(2)}) collective-permute-start(f32[16,1024]{1,0:T(8,128)S(1)} %add.75), channel_id=1, source_target_pairs={{0,4},{1,5},{2,6},{3,7},{4,0},{5,1},{6,2},{7,3},{8,12},{9,13},{10,... | collective-permute-start | bytes 196616 | tf_op jit(solution)/shard_map/ppermute | solution.py:272
  57.8 1.6 %collective-permute-start.30 = (f32[16,1024]{1,0:T(8,128)S(1)}, f32[16,1024]{1,0:T(8,128)S(1)}, u32[]{:S(2)}, u32[]{:S(2)}) collective-permute-start(f32[16,1024]{1,0:T(8,128)S(1)} %add.75), channel_id=1, source_target_pairs={{0,6},{1,7},{2,4},{3,5},{4,2},{5,3},{6,0},{7,1},{8,14},{9,15},{10,... | collective-permute-start | bytes 196616 | tf_op jit(solution)/shard_map/ppermute | solution.py:272
  59.4 1.6 %factor.4 = (f32[16,256]{1,0:T(8,128)S(1)}, f32[16,16]{1,0:T(8,128)S(1)}) custom-call(f32[16,256]{1,0:T(8,128)S(1)} %add_add_fusion.3.proj_ref), custom_call_target="tpu_custom_call" | custom-call | flops 1073741824 | bytes 1048576 | tf_op jit(solution)/shard_map/factor/pallas_call | solution.py:75
  61.0 0.7 collective-permute-done.29
  61.7 1.3 %collective-permute-done.30 = f32[16,1024]{1,0:T(8,128)S(1)} collective-permute-done((f32[16,1024]{1,0:T(8,128)S(1)}, f32[16,1024]{1,0:T(8,128)S(1)}, u32[]{:S(2)}, u32[]{:S(2)}) %collective-permute-start.30) | collective-permute-done | bytes 65568 | tf_op jit(solution)/shard_map/ppermute | solution.py:272
  63.2 1.5 %collective-permute-start.31 = (f32[16,1280]{1,0:T(8,128)S(1)}, f32[16,1280]{1,0:T(8,128)S(1)}, u32[]{:S(2)}, u32[]{:S(2)}) collective-permute-start(f32[16,1280]{1,0:T(8,128)S(1)} %get-tuple-element.49.refs_9_), channel_id=1, source_target_pairs={{8,0},{16,8},{24,16},{9,1},{17,9},{25,17},{10,2},{18,10},{26,18},{... | collective-permute-start | bytes 245768 | tf_op jit(solution)/shard_map/ppermute | solution.py:422
  64.7 2.4 %mask.3.mask_ref = bf16[256,4096]{1,0:T(8,128)(2,1)S(1)} custom-call(bf16[2,32,1024]{2,1,0:T(8,128)(2,1)S(1)} %get-tuple-element.43.refs_0_, bf16[2,32,1024]{2,1,0:T(8,128)(2,1)S(1)} %collective-permute-done.16.refs_1_, bf16[2,32,1024]{2,1,0:T(8,128)(2,1)S(1)} %collective-permute-done.17.refs_2_, bf16[2,32,1024]{2,1,0:T(8,128)(2,1)S(1)} %collective-permute-done.18.refs_3_, ...), custom_call_target="tpu_custom_call" | custom-call | flops 2147483648 | bytes 1048576 | tf_op jit(solution)/shard_map/mask/pallas_call | solution.py:75
  67.0 1.4 %warm.5.warm_in_ref = bf16[32,4096]{1,0:T(8,128)(2,1)S(1)} custom-call(f32[16,1024]{1,0:T(8,128)S(1)} %get-tuple-element.50.warm_ref, bf16[1024,4096]{1,0:T(8,128)(2,1)S(1)} %bitcast.29), custom_call_target="tpu_custom_call" | custom-call | flops 1073741824 | bytes 1048576 | tf_op jit(solution)/shard_map/warm/pallas_call | solution.py:75
  68.5 1.0 %collective-permute-done.31.both_ref = f32[16,1280]{1,0:T(8,128)S(1)} collective-permute-done((f32[16,1280]{1,0:T(8,128)S(1)}, f32[16,1280]{1,0:T(8,128)S(1)}, u32[]{:S(2)}, u32[]{:S(2)}) %collective-permute-start.31) | collective-permute-done | bytes 81952 | tf_op jit(solution)/shard_map/ppermute | solution.py:422
  69.5 3.7 %hidden.3 = (bf16[256,4096]{1,0:T(8,128)(2,1)S(1)}, f32[16,256]{1,0:T(8,128)S(1)}, f32[256,128]{1,0:T(8,128)S(1)}) custom-call(f32[3,16,256]{2,1,0:T(8,128)S(1)} %bitcast.39, f32[3,16,1024]{2,1,0:T(8,128)S(1)} %bitcast.36, f32[16,1280]{1,0:T(8,128)S(1)} %collective-permute-done.31.both_ref, f32[16,1024]{1,0:T(8,128)S(1)} %get-tuple-element.50.warm_ref, ...), custom_call_target="tpu_custom_call" | custom-call | flops 2147483648 | bytes 1048576 | tf_op jit(solution)/shard_map/hidden/pallas_call | solution.py:75
  73.3 1.2 %collective-permute-done.32 = f32[16,256]{1,0:T(8,128)S(1)} collective-permute-done((f32[16,256]{1,0:T(8,128)S(1)}, f32[16,256]{1,0:T(8,128)S(1)}, u32[]{:S(2)}, u32[]{:S(2)}) %collective-permute-start.32) | collective-permute-done | bytes 16416 | tf_op jit(solution)/shard_map/ppermute | solution.py:272
  74.4 1.0 %collective-permute-start.33 = (f32[16,256]{1,0:T(8,128)S(1)}, f32[16,256]{1,0:T(8,128)S(1)}, u32[]{:S(2)}, u32[]{:S(2)}) collective-permute-start(f32[16,256]{1,0:T(8,128)S(1)} %add.79), channel_id=1, source_target_pairs={{0,2},{1,3},{2,0},{3,1},{4,6},{5,7},{6,4},{7,5},{8,10},{9,11},{10,... | collective-permute-start | bytes 49160 | tf_op jit(solution)/shard_map/ppermute | solution.py:272
  75.5 1.2 %collective-permute-start.34 = (f32[16,256]{1,0:T(8,128)S(1)}, f32[16,256]{1,0:T(8,128)S(1)}, u32[]{:S(2)}, u32[]{:S(2)}) collective-permute-start(f32[16,256]{1,0:T(8,128)S(1)} %add.79), channel_id=1, source_target_pairs={{0,4},{1,5},{2,6},{3,7},{4,0},{5,1},{6,2},{7,3},{8,12},{9,13},{10,... | collective-permute-start | bytes 49160 | tf_op jit(solution)/shard_map/ppermute | solution.py:272
  76.6 1.3 %collective-permute-start.35 = (f32[16,256]{1,0:T(8,128)S(1)}, f32[16,256]{1,0:T(8,128)S(1)}, u32[]{:S(2)}, u32[]{:S(2)}) collective-permute-start(f32[16,256]{1,0:T(8,128)S(1)} %add.79), channel_id=1, source_target_pairs={{0,6},{1,7},{2,4},{3,5},{4,2},{5,3},{6,0},{7,1},{8,14},{9,15},{10,... | collective-permute-start | bytes 49160 | tf_op jit(solution)/shard_map/ppermute | solution.py:272
  77.9 2.4 %merged.5.merged_ref = f32[256,1024]{1,0:T(8,128)S(1)} custom-call(f32[256,128]{1,0:T(8,128)S(1)} %get-tuple-element.53.block_ref, bf16[256,4096]{1,0:T(8,128)(2,1)S(1)} %get-tuple-element.54.hidden_ref, bf16[1024,4096]{1,0:T(8,128)(2,1)S(1)} %bitcast.30), custom_call_target="tpu_custom_call" | custom-call | flops 2147483648 | bytes 1048576 | tf_op jit(solution)/shard_map/merged/pallas_call | solution.py:75
  80.5 0.8 collective-permute-done.35
  81.6 1.3 %collective-permute-done.37.right_arrived_ref = f32[16,1024]{1,0:T(8,128)S(1)} collective-permute-done((f32[16,1024]{1,0:T(8,128)S(1)}, f32[16,1024]{1,0:T(8,128)S(1)}, u32[]{:S(2)}, u32[]{:S(2)}) %collective-permute-start.37) | collective-permute-done | bytes 65568 | tf_op jit(solution)/shard_map/ppermute | solution.py:272
  82.9 0.8 collective-permute-start.38
  83.8 1.1 %collective-permute-start.39 = (bf16[64,1024]{1,0:T(8,128)(2,1)S(1)}, bf16[64,1024]{1,0:T(8,128)(2,1)S(1)}, u32[]{:S(2)}, u32[]{:S(2)}) collective-permute-start(bf16[64,1024]{1,0:T(8,128)(2,1)S(1)} %get-tuple-element.58), channel_id=1, source_target_pairs={{0,4},{1,5},{2,6},{3,7},{4,0},{5,1},{6,2},{7,3},{8,12},{9,13},{10,... | collective-permute-start | bytes 393224 | tf_op jit(solution)/shard_map/ppermute | solution.py:272
  84.8 1.6 %collective-permute-start.40 = (bf16[64,1024]{1,0:T(8,128)(2,1)S(1)}, bf16[64,1024]{1,0:T(8,128)(2,1)S(1)}, u32[]{:S(2)}, u32[]{:S(2)}) collective-permute-start(bf16[64,1024]{1,0:T(8,128)(2,1)S(1)} %get-tuple-element.59), channel_id=1, source_target_pairs={{0,6},{1,7},{2,4},{3,5},{4,2},{5,3},{6,0},{7,1},{8,14},{9,15},{10,... | collective-permute-start | bytes 393224 | tf_op jit(solution)/shard_map/ppermute | solution.py:272
  86.5 1.6 %factor.5 = (f32[16,256]{1,0:T(8,128)S(1)}, f32[16,16]{1,0:T(8,128)S(1)}) custom-call(f32[16,256]{1,0:T(8,128)S(1)} %add_add_fusion.2.proj_ref), custom_call_target="tpu_custom_call" | custom-call | flops 1073741824 | bytes 1048576 | tf_op jit(solution)/shard_map/factor/pallas_call | solution.py:75
  88.0 0.7 dynamic-slice_bitcast_fusion
  88.7 0.6 collective-permute-done.38.refs_0_
  89.3 2.5 %collective-permute-done.39.refs_1_ = bf16[64,1024]{1,0:T(8,128)(2,1)S(1)} collective-permute-done((bf16[64,1024]{1,0:T(8,128)(2,1)S(1)}, bf16[64,1024]{1,0:T(8,128)(2,1)S(1)}, u32[]{:S(2)}, u32[]{:S(2)}) %collective-permute-start.39) | collective-permute-done | bytes 131104 | tf_op jit(solution)/shard_map/ppermute | solution.py:272
  91.9 0.9 last.1
  (69 shorter events, 1.7 us)
Async XLA Ops:
  0.6 0.9 %copy-start.7 = (bf16[1,3,32,1024]{3,2,1,0:T(8,128)(2,1)S(1)}, bf16[1,3,32,1024]{3,2,1,0:T(8,128)(2,1)}, u32[]{:S(2)}) copy-start(bf16[1,3,32,1024]{3,2,1,0:T(8,128)(2,1)} %param.8) | copy-start | bytes 589828
  1.6 4.6 %copy-start.1 = (bf16[1,4096,1024]{2,1,0:T(8,128)(2,1)S(1)}, bf16[1,4096,1024]{2,1,0:T(8,128)(2,1)}, u32[]{:S(2)}) copy-start(bf16[1,4096,1024]{2,1,0:T(8,128)(2,1)} %param.10) | copy-start | bytes 25165828
  1.6 4.6 %copy-start.2 = (f32[3,1024,16]{1,2,0:T(8,128)S(1)}, f32[3,1024,16]{1,2,0:T(8,128)}, u32[]{:S(2)}) copy-start(f32[3,1024,16]{1,2,0:T(8,128)} %param.15) | copy-start | bytes 589828
  1.6 4.6 %copy-start.3 = (f32[3,256,16]{1,2,0:T(8,128)S(1)}, f32[3,256,16]{1,2,0:T(8,128)}, u32[]{:S(2)}) copy-start(f32[3,256,16]{1,2,0:T(8,128)} %param.14) | copy-start | bytes 147460
  1.6 4.6 %copy-start.4 = (f32[1,1024,16]{1,2,0:T(8,128)S(1)}, f32[1,1024,16]{1,2,0:T(8,128)}, u32[]{:S(2)}) copy-start(f32[1,1024,16]{1,2,0:T(8,128)} %param.11) | copy-start | bytes 196612
  1.6 4.6 %copy-start.5 = (f32[1,1024,16]{1,2,0:T(8,128)S(1)}, f32[1,1024,16]{1,2,0:T(8,128)}, u32[]{:S(2)}) copy-start(f32[1,1024,16]{1,2,0:T(8,128)} %param.13) | copy-start | bytes 196612
  1.6 4.6 %copy-start.6 = (f32[1,256,16]{1,2,0:T(8,128)S(1)}, f32[1,256,16]{1,2,0:T(8,128)}, u32[]{:S(2)}) copy-start(f32[1,256,16]{1,2,0:T(8,128)} %param.12) | copy-start | bytes 49156
  1.6 7.4 %collective-permute-start = (bf16[32,1024]{1,0:T(8,128)(2,1)S(1)}, bf16[32,1024]{1,0:T(8,128)(2,1)S(1)}, u32[]{:S(2)}, u32[]{:S(2)}) collective-permute-start(bf16[32,1024]{1,0:T(8,128)(2,1)S(1)} %get-tuple-element.33.refs_0_), channel_id=1, source_target_pairs={{0,2},{1,3},{2,0},{3,1},{4,6},{5,7},{6,4},{7,5},{8,10},{9,11},{10,... | collective-permute-start | bytes 196616 | tf_op jit(solution)/shard_map/ppermute | solution.py:272
  4.6 5.0 %collective-permute-start.1 = (bf16[32,1024]{1,0:T(8,128)(2,1)S(1)}, bf16[32,1024]{1,0:T(8,128)(2,1)S(1)}, u32[]{:S(2)}, u32[]{:S(2)}) collective-permute-start(bf16[32,1024]{1,0:T(8,128)(2,1)S(1)} %get-tuple-element.33.refs_0_), channel_id=1, source_target_pairs={{0,4},{1,5},{2,6},{3,7},{4,0},{5,1},{6,2},{7,3},{8,12},{9,13},{10,... | collective-permute-start | bytes 196616 | tf_op jit(solution)/shard_map/ppermute | solution.py:272
  6.1 5.2 %collective-permute-start.2 = (bf16[32,1024]{1,0:T(8,128)(2,1)S(1)}, bf16[32,1024]{1,0:T(8,128)(2,1)S(1)}, u32[]{:S(2)}, u32[]{:S(2)}) collective-permute-start(bf16[32,1024]{1,0:T(8,128)(2,1)S(1)} %get-tuple-element.33.refs_0_), channel_id=1, source_target_pairs={{0,6},{1,7},{2,4},{3,5},{4,2},{5,3},{6,0},{7,1},{8,14},{9,15},{10,... | collective-permute-start | bytes 196616 | tf_op jit(solution)/shard_map/ppermute | solution.py:272
  6.2 6.6 %collective-permute-start.3 = (bf16[32,1024]{1,0:T(8,128)(2,1)S(1)}, bf16[32,1024]{1,0:T(8,128)(2,1)S(1)}, u32[]{:S(2)}, u32[]{:S(2)}) collective-permute-start(bf16[32,1024]{1,0:T(8,128)(2,1)S(1)} %get-tuple-element.33.refs_0_), channel_id=1, source_target_pairs={{0,1},{1,0},{2,3},{3,2},{4,5},{5,4},{6,7},{7,6},{8,9},{9,8},{10,11... | collective-permute-start | bytes 196616 | tf_op jit(solution)/shard_map/ppermute | solution.py:272
  6.2 5.1 %copy-start = (bf16[1,1024,4096]{2,1,0:T(8,128)(2,1)S(1)}, bf16[1,1024,4096]{2,1,0:T(8,128)(2,1)}, u32[]{:S(2)}) copy-start(bf16[1,1024,4096]{2,1,0:T(8,128)(2,1)} %param.9) | copy-start | bytes 25165828
  9.0 3.7 %collective-permute-start.4 = (bf16[32,1024]{1,0:T(8,128)(2,1)S(1)}, bf16[32,1024]{1,0:T(8,128)(2,1)S(1)}, u32[]{:S(2)}, u32[]{:S(2)}) collective-permute-start(bf16[32,1024]{1,0:T(8,128)(2,1)S(1)} %collective-permute-done.refs_1_), channel_id=1, source_target_pairs={{0,1},{1,0},{2,3},{3,2},{4,5},{5,4},{6,7},{7,6},{8,9},{9,8},{10,11... | collective-permute-start | bytes 196616 | tf_op jit(solution)/shard_map/ppermute | solution.py:272
  9.6 3.2 %collective-permute-start.5 = (bf16[32,1024]{1,0:T(8,128)(2,1)S(1)}, bf16[32,1024]{1,0:T(8,128)(2,1)S(1)}, u32[]{:S(2)}, u32[]{:S(2)}) collective-permute-start(bf16[32,1024]{1,0:T(8,128)(2,1)S(1)} %collective-permute-done.1.refs_2_), channel_id=1, source_target_pairs={{0,1},{1,0},{2,3},{3,2},{4,5},{5,4},{6,7},{7,6},{8,9},{9,8},{10,11... | collective-permute-start | bytes 196616 | tf_op jit(solution)/shard_map/ppermute | solution.py:272
  11.3 1.5 %collective-permute-start.6 = (bf16[32,1024]{1,0:T(8,128)(2,1)S(1)}, bf16[32,1024]{1,0:T(8,128)(2,1)S(1)}, u32[]{:S(2)}, u32[]{:S(2)}) collective-permute-start(bf16[32,1024]{1,0:T(8,128)(2,1)S(1)} %collective-permute-done.2.refs_3_), channel_id=1, source_target_pairs={{0,1},{1,0},{2,3},{3,2},{4,5},{5,4},{6,7},{7,6},{8,9},{9,8},{10,11... | collective-permute-start | bytes 196616 | tf_op jit(solution)/shard_map/ppermute | solution.py:272
  16.0 1.4 %collective-permute-start.7 = (f32[16,256]{1,0:T(8,128)S(1)}, f32[16,256]{1,0:T(8,128)S(1)}, u32[]{:S(2)}, u32[]{:S(2)}) collective-permute-start(f32[16,256]{1,0:T(8,128)S(1)} %get-tuple-element.36), channel_id=1, source_target_pairs={{0,1},{1,0},{2,3},{3,2},{4,5},{5,4},{6,7},{7,6},{8,9},{9,8},{10,11... | collective-permute-start | bytes 49160 | tf_op jit(solution)/shard_map/ppermute | solution.py:272
  16.5 12.0 %collective-permute-start.16 = (bf16[2,32,1024]{2,1,0:T(8,128)(2,1)S(1)}, bf16[2,32,1024]{2,1,0:T(8,128)(2,1)S(1)}, u32[]{:S(2)}, u32[]{:S(2)}) collective-permute-start(bf16[2,32,1024]{2,1,0:T(8,128)(2,1)S(1)} %get-tuple-element.43.refs_0_), channel_id=1, source_target_pairs={{0,2},{1,3},{2,0},{3,1},{4,6},{5,7},{6,4},{7,5},{8,10},{9,11},{10,... | collective-permute-start | bytes 393224 | tf_op jit(solution)/shard_map/ppermute | solution.py:272
  17.4 5.9 %collective-permute-start.10 = (f32[16,256]{1,0:T(8,128)S(1)}, f32[16,256]{1,0:T(8,128)S(1)}, u32[]{:S(2)}, u32[]{:S(2)}) collective-permute-start(f32[16,256]{1,0:T(8,128)S(1)} %add.63), channel_id=1, source_target_pairs={{0,6},{1,7},{2,4},{3,5},{4,2},{5,3},{6,0},{7,1},{8,14},{9,15},{10,... | collective-permute-start | bytes 49160 | tf_op jit(solution)/shard_map/ppermute | solution.py:272
  18.9 4.3 %collective-permute-start.8 = (f32[16,256]{1,0:T(8,128)S(1)}, f32[16,256]{1,0:T(8,128)S(1)}, u32[]{:S(2)}, u32[]{:S(2)}) collective-permute-start(f32[16,256]{1,0:T(8,128)S(1)} %add.63), channel_id=1, source_target_pairs={{0,2},{1,3},{2,0},{3,1},{4,6},{5,7},{6,4},{7,5},{8,10},{9,11},{10,... | collective-permute-start | bytes 49160 | tf_op jit(solution)/shard_map/ppermute | solution.py:272
  19.9 3.7 %collective-permute-start.9 = (f32[16,256]{1,0:T(8,128)S(1)}, f32[16,256]{1,0:T(8,128)S(1)}, u32[]{:S(2)}, u32[]{:S(2)}) collective-permute-start(f32[16,256]{1,0:T(8,128)S(1)} %add.63), channel_id=1, source_target_pairs={{0,4},{1,5},{2,6},{3,7},{4,0},{5,1},{6,2},{7,3},{8,12},{9,13},{10,... | collective-permute-start | bytes 49160 | tf_op jit(solution)/shard_map/ppermute | solution.py:272
  24.0 2.6 %collective-permute-start.11 = (f32[16,1024]{1,0:T(8,128)S(1)}, f32[16,1024]{1,0:T(8,128)S(1)}, u32[]{:S(2)}, u32[]{:S(2)}) collective-permute-start(f32[16,1024]{1,0:T(8,128)S(1)} %right.3), channel_id=1, source_target_pairs={{0,1},{1,0},{2,3},{3,2},{4,5},{5,4},{6,7},{7,6},{8,9},{9,8},{10,11... | collective-permute-start | bytes 196616 | tf_op jit(solution)/shard_map/ppermute | solution.py:272
  24.0 10.6 %collective-permute-start.17 = (bf16[2,32,1024]{2,1,0:T(8,128)(2,1)S(1)}, bf16[2,32,1024]{2,1,0:T(8,128)(2,1)S(1)}, u32[]{:S(2)}, u32[]{:S(2)}) collective-permute-start(bf16[2,32,1024]{2,1,0:T(8,128)(2,1)S(1)} %get-tuple-element.43.refs_0_), channel_id=1, source_target_pairs={{0,4},{1,5},{2,6},{3,7},{4,0},{5,1},{6,2},{7,3},{8,12},{9,13},{10,... | collective-permute-start | bytes 393224 | tf_op jit(solution)/shard_map/ppermute | solution.py:272
  25.0 9.6 %collective-permute-start.18 = (bf16[2,32,1024]{2,1,0:T(8,128)(2,1)S(1)}, bf16[2,32,1024]{2,1,0:T(8,128)(2,1)S(1)}, u32[]{:S(2)}, u32[]{:S(2)}) collective-permute-start(bf16[2,32,1024]{2,1,0:T(8,128)(2,1)S(1)} %get-tuple-element.43.refs_0_), channel_id=1, source_target_pairs={{0,6},{1,7},{2,4},{3,5},{4,2},{5,3},{6,0},{7,1},{8,14},{9,15},{10,... | collective-permute-start | bytes 393224 | tf_op jit(solution)/shard_map/ppermute | solution.py:272
  26.5 8.5 %collective-permute-start.12 = (f32[16,1024]{1,0:T(8,128)S(1)}, f32[16,1024]{1,0:T(8,128)S(1)}, u32[]{:S(2)}, u32[]{:S(2)}) collective-permute-start(f32[16,1024]{1,0:T(8,128)S(1)} %add.67), channel_id=1, source_target_pairs={{0,2},{1,3},{2,0},{3,1},{4,6},{5,7},{6,4},{7,5},{8,10},{9,11},{10,... | collective-permute-start | bytes 196616 | tf_op jit(solution)/shard_map/ppermute | solution.py:272
  27.6 7.9 %collective-permute-start.13 = (f32[16,1024]{1,0:T(8,128)S(1)}, f32[16,1024]{1,0:T(8,128)S(1)}, u32[]{:S(2)}, u32[]{:S(2)}) collective-permute-start(f32[16,1024]{1,0:T(8,128)S(1)} %add.67), channel_id=1, source_target_pairs={{0,4},{1,5},{2,6},{3,7},{4,0},{5,1},{6,2},{7,3},{8,12},{9,13},{10,... | collective-permute-start | bytes 196616 | tf_op jit(solution)/shard_map/ppermute | solution.py:272
  28.6 7.0 %collective-permute-start.14 = (f32[16,1024]{1,0:T(8,128)S(1)}, f32[16,1024]{1,0:T(8,128)S(1)}, u32[]{:S(2)}, u32[]{:S(2)}) collective-permute-start(f32[16,1024]{1,0:T(8,128)S(1)} %add.67), channel_id=1, source_target_pairs={{0,6},{1,7},{2,4},{3,5},{4,2},{5,3},{6,0},{7,1},{8,14},{9,15},{10,... | collective-permute-start | bytes 196616 | tf_op jit(solution)/shard_map/ppermute | solution.py:272
  34.5 2.7 %collective-permute-start.19 = (bf16[2,32,1024]{2,1,0:T(8,128)(2,1)S(1)}, bf16[2,32,1024]{2,1,0:T(8,128)(2,1)S(1)}, u32[]{:S(2)}, u32[]{:S(2)}) collective-permute-start(bf16[2,32,1024]{2,1,0:T(8,128)(2,1)S(1)} %get-tuple-element.43.refs_0_), channel_id=1, source_target_pairs={{0,1},{1,0},{2,3},{3,2},{4,5},{5,4},{6,7},{7,6},{8,9},{9,8},{10,11... | collective-permute-start | bytes 393224 | tf_op jit(solution)/shard_map/ppermute | solution.py:272
  34.5 2.7 %collective-permute-start.20 = (bf16[2,32,1024]{2,1,0:T(8,128)(2,1)S(1)}, bf16[2,32,1024]{2,1,0:T(8,128)(2,1)S(1)}, u32[]{:S(2)}, u32[]{:S(2)}) collective-permute-start(bf16[2,32,1024]{2,1,0:T(8,128)(2,1)S(1)} %collective-permute-done.16.refs_1_), channel_id=1, source_target_pairs={{0,1},{1,0},{2,3},{3,2},{4,5},{5,4},{6,7},{7,6},{8,9},{9,8},{10,11... | collective-permute-start | bytes 393224 | tf_op jit(solution)/shard_map/ppermute | solution.py:272
  35.0 2.2 %collective-permute-start.21 = (bf16[2,32,1024]{2,1,0:T(8,128)(2,1)S(1)}, bf16[2,32,1024]{2,1,0:T(8,128)(2,1)S(1)}, u32[]{:S(2)}, u32[]{:S(2)}) collective-permute-start(bf16[2,32,1024]{2,1,0:T(8,128)(2,1)S(1)} %collective-permute-done.17.refs_2_), channel_id=1, source_target_pairs={{0,1},{1,0},{2,3},{3,2},{4,5},{5,4},{6,7},{7,6},{8,9},{9,8},{10,11... | collective-permute-start | bytes 393224 | tf_op jit(solution)/shard_map/ppermute | solution.py:272
  35.5 1.8 %collective-permute-start.22 = (bf16[2,32,1024]{2,1,0:T(8,128)(2,1)S(1)}, bf16[2,32,1024]{2,1,0:T(8,128)(2,1)S(1)}, u32[]{:S(2)}, u32[]{:S(2)}) collective-permute-start(bf16[2,32,1024]{2,1,0:T(8,128)(2,1)S(1)} %collective-permute-done.18.refs_3_), channel_id=1, source_target_pairs={{0,1},{1,0},{2,3},{3,2},{4,5},{5,4},{6,7},{7,6},{8,9},{9,8},{10,11... | collective-permute-start | bytes 393224 | tf_op jit(solution)/shard_map/ppermute | solution.py:272
  35.8 6.7 %collective-permute-start.15 = (f32[16,1280]{1,0:T(8,128)S(1)}, f32[16,1280]{1,0:T(8,128)S(1)}, u32[]{:S(2)}, u32[]{:S(2)}) collective-permute-start(f32[16,1280]{1,0:T(8,128)S(1)} %get-tuple-element.41.refs_9_), channel_id=1, source_target_pairs={{8,0},{16,8},{24,16},{9,1},{17,9},{25,17},{10,2},{18,10},{26,18},{... | collective-permute-start | bytes 245768 | tf_op jit(solution)/shard_map/ppermute | solution.py:422
  46.2 1.2 %collective-permute-start.23 = (f32[16,256]{1,0:T(8,128)S(1)}, f32[16,256]{1,0:T(8,128)S(1)}, u32[]{:S(2)}, u32[]{:S(2)}) collective-permute-start(f32[16,256]{1,0:T(8,128)S(1)} %get-tuple-element.44), channel_id=1, source_target_pairs={{0,1},{1,0},{2,3},{3,2},{4,5},{5,4},{6,7},{7,6},{8,9},{9,8},{10,11... | collective-permute-start | bytes 49160 | tf_op jit(solution)/shard_map/ppermute | solution.py:272
  47.4 5.9 %collective-permute-start.24 = (f32[16,256]{1,0:T(8,128)S(1)}, f32[16,256]{1,0:T(8,128)S(1)}, u32[]{:S(2)}, u32[]{:S(2)}) collective-permute-start(f32[16,256]{1,0:T(8,128)S(1)} %add.71), channel_id=1, source_target_pairs={{0,2},{1,3},{2,0},{3,1},{4,6},{5,7},{6,4},{7,5},{8,10},{9,11},{10,... | collective-permute-start | bytes 49160 | tf_op jit(solution)/shard_map/ppermute | solution.py:272
  48.5 4.9 %collective-permute-start.25 = (f32[16,256]{1,0:T(8,128)S(1)}, f32[16,256]{1,0:T(8,128)S(1)}, u32[]{:S(2)}, u32[]{:S(2)}) collective-permute-start(f32[16,256]{1,0:T(8,128)S(1)} %add.71), channel_id=1, source_target_pairs={{0,4},{1,5},{2,6},{3,7},{4,0},{5,1},{6,2},{7,3},{8,12},{9,13},{10,... | collective-permute-start | bytes 49160 | tf_op jit(solution)/shard_map/ppermute | solution.py:272
  49.6 4.6 %collective-permute-start.26 = (f32[16,256]{1,0:T(8,128)S(1)}, f32[16,256]{1,0:T(8,128)S(1)}, u32[]{:S(2)}, u32[]{:S(2)}) collective-permute-start(f32[16,256]{1,0:T(8,128)S(1)} %add.71), channel_id=1, source_target_pairs={{0,6},{1,7},{2,4},{3,5},{4,2},{5,3},{6,0},{7,1},{8,14},{9,15},{10,... | collective-permute-start | bytes 49160 | tf_op jit(solution)/shard_map/ppermute | solution.py:272
  54.6 1.3 %collective-permute-start.27 = (f32[16,1024]{1,0:T(8,128)S(1)}, f32[16,1024]{1,0:T(8,128)S(1)}, u32[]{:S(2)}, u32[]{:S(2)}) collective-permute-start(f32[16,1024]{1,0:T(8,128)S(1)} %right.4), channel_id=1, source_target_pairs={{0,1},{1,0},{2,3},{3,2},{4,5},{5,4},{6,7},{7,6},{8,9},{9,8},{10,11... | collective-permute-start | bytes 196616 | tf_op jit(solution)/shard_map/ppermute | solution.py:272
  55.9 5.1 %collective-permute-start.28 = (f32[16,1024]{1,0:T(8,128)S(1)}, f32[16,1024]{1,0:T(8,128)S(1)}, u32[]{:S(2)}, u32[]{:S(2)}) collective-permute-start(f32[16,1024]{1,0:T(8,128)S(1)} %add.75), channel_id=1, source_target_pairs={{0,2},{1,3},{2,0},{3,1},{4,6},{5,7},{6,4},{7,5},{8,10},{9,11},{10,... | collective-permute-start | bytes 196616 | tf_op jit(solution)/shard_map/ppermute | solution.py:272
  56.7 5.0 %collective-permute-start.29 = (f32[16,1024]{1,0:T(8,128)S(1)}, f32[16,1024]{1,0:T(8,128)S(1)}, u32[]{:S(2)}, u32[]{:S(2)}) collective-permute-start(f32[16,1024]{1,0:T(8,128)S(1)} %add.75), channel_id=1, source_target_pairs={{0,4},{1,5},{2,6},{3,7},{4,0},{5,1},{6,2},{7,3},{8,12},{9,13},{10,... | collective-permute-start | bytes 196616 | tf_op jit(solution)/shard_map/ppermute | solution.py:272
  57.8 5.2 %collective-permute-start.30 = (f32[16,1024]{1,0:T(8,128)S(1)}, f32[16,1024]{1,0:T(8,128)S(1)}, u32[]{:S(2)}, u32[]{:S(2)}) collective-permute-start(f32[16,1024]{1,0:T(8,128)S(1)} %add.75), channel_id=1, source_target_pairs={{0,6},{1,7},{2,4},{3,5},{4,2},{5,3},{6,0},{7,1},{8,14},{9,15},{10,... | collective-permute-start | bytes 196616 | tf_op jit(solution)/shard_map/ppermute | solution.py:272
  63.2 6.3 %collective-permute-start.31 = (f32[16,1280]{1,0:T(8,128)S(1)}, f32[16,1280]{1,0:T(8,128)S(1)}, u32[]{:S(2)}, u32[]{:S(2)}) collective-permute-start(f32[16,1280]{1,0:T(8,128)S(1)} %get-tuple-element.49.refs_9_), channel_id=1, source_target_pairs={{8,0},{16,8},{24,16},{9,1},{17,9},{25,17},{10,2},{18,10},{26,18},{... | collective-permute-start | bytes 245768 | tf_op jit(solution)/shard_map/ppermute | solution.py:422
  73.2 1.2 %collective-permute-start.32 = (f32[16,256]{1,0:T(8,128)S(1)}, f32[16,256]{1,0:T(8,128)S(1)}, u32[]{:S(2)}, u32[]{:S(2)}) collective-permute-start(f32[16,256]{1,0:T(8,128)S(1)} %get-tuple-element.51), channel_id=1, source_target_pairs={{0,1},{1,0},{2,3},{3,2},{4,5},{5,4},{6,7},{7,6},{8,9},{9,8},{10,11... | collective-permute-start | bytes 49160 | tf_op jit(solution)/shard_map/ppermute | solution.py:272
  74.4 6.0 %collective-permute-start.33 = (f32[16,256]{1,0:T(8,128)S(1)}, f32[16,256]{1,0:T(8,128)S(1)}, u32[]{:S(2)}, u32[]{:S(2)}) collective-permute-start(f32[16,256]{1,0:T(8,128)S(1)} %add.79), channel_id=1, source_target_pairs={{0,2},{1,3},{2,0},{3,1},{4,6},{5,7},{6,4},{7,5},{8,10},{9,11},{10,... | collective-permute-start | bytes 49160 | tf_op jit(solution)/shard_map/ppermute | solution.py:272
  75.5 5.0 %collective-permute-start.34 = (f32[16,256]{1,0:T(8,128)S(1)}, f32[16,256]{1,0:T(8,128)S(1)}, u32[]{:S(2)}, u32[]{:S(2)}) collective-permute-start(f32[16,256]{1,0:T(8,128)S(1)} %add.79), channel_id=1, source_target_pairs={{0,4},{1,5},{2,6},{3,7},{4,0},{5,1},{6,2},{7,3},{8,12},{9,13},{10,... | collective-permute-start | bytes 49160 | tf_op jit(solution)/shard_map/ppermute | solution.py:272
  76.6 4.6 %collective-permute-start.35 = (f32[16,256]{1,0:T(8,128)S(1)}, f32[16,256]{1,0:T(8,128)S(1)}, u32[]{:S(2)}, u32[]{:S(2)}) collective-permute-start(f32[16,256]{1,0:T(8,128)S(1)} %add.79), channel_id=1, source_target_pairs={{0,6},{1,7},{2,4},{3,5},{4,2},{5,3},{6,0},{7,1},{8,14},{9,15},{10,... | collective-permute-start | bytes 49160 | tf_op jit(solution)/shard_map/ppermute | solution.py:272
  80.4 2.5 %collective-permute-start.36 = (bf16[4,32,1024]{2,1,0:T(8,128)(2,1)S(1)}, bf16[4,32,1024]{2,1,0:T(8,128)(2,1)S(1)}, u32[]{:S(2)}, u32[]{:S(2)}) collective-permute-start(bf16[4,32,1024]{2,1,0:T(8,128)(2,1)S(1)} %outgoing.1), channel_id=1, source_target_pairs={{0,1},{1,0},{2,3},{3,2},{4,5},{5,4},{6,7},{7,6},{8,9},{9,8},{10,11... | collective-permute-start | bytes 786440 | tf_op jit(solution)/shard_map/ppermute | solution.py:272
  81.6 1.3 %collective-permute-start.37 = (f32[16,1024]{1,0:T(8,128)S(1)}, f32[16,1024]{1,0:T(8,128)S(1)}, u32[]{:S(2)}, u32[]{:S(2)}) collective-permute-start(f32[16,1024]{1,0:T(8,128)S(1)} %right.5.right_ref), channel_id=1, source_target_pairs={{0,1},{1,0},{2,3},{3,2},{4,5},{5,4},{6,7},{7,6},{8,9},{9,8},{10,11... | collective-permute-start | bytes 196616 | tf_op jit(solution)/shard_map/ppermute | solution.py:272
  82.9 6.4 %collective-permute-start.38 = (bf16[64,1024]{1,0:T(8,128)(2,1)S(1)}, bf16[64,1024]{1,0:T(8,128)(2,1)S(1)}, u32[]{:S(2)}, u32[]{:S(2)}) collective-permute-start(bf16[64,1024]{1,0:T(8,128)(2,1)S(1)} %get-tuple-element.57), channel_id=1, source_target_pairs={{0,2},{1,3},{2,0},{3,1},{4,6},{5,7},{6,4},{7,5},{8,10},{9,11},{10,... | collective-permute-start | bytes 393224 | tf_op jit(solution)/shard_map/ppermute | solution.py:272
  83.8 8.1 %collective-permute-start.39 = (bf16[64,1024]{1,0:T(8,128)(2,1)S(1)}, bf16[64,1024]{1,0:T(8,128)(2,1)S(1)}, u32[]{:S(2)}, u32[]{:S(2)}) collective-permute-start(bf16[64,1024]{1,0:T(8,128)(2,1)S(1)} %get-tuple-element.58), channel_id=1, source_target_pairs={{0,4},{1,5},{2,6},{3,7},{4,0},{5,1},{6,2},{7,3},{8,12},{9,13},{10,... | collective-permute-start | bytes 393224 | tf_op jit(solution)/shard_map/ppermute | solution.py:272
  84.8 7.0 %collective-permute-start.40 = (bf16[64,1024]{1,0:T(8,128)(2,1)S(1)}, bf16[64,1024]{1,0:T(8,128)(2,1)S(1)}, u32[]{:S(2)}, u32[]{:S(2)}) collective-permute-start(bf16[64,1024]{1,0:T(8,128)(2,1)S(1)} %get-tuple-element.59), channel_id=1, source_target_pairs={{0,6},{1,7},{2,4},{3,5},{4,2},{5,3},{6,0},{7,1},{8,14},{9,15},{10,... | collective-permute-start | bytes 393224 | tf_op jit(solution)/shard_map/ppermute | solution.py:272

commit v4 on v3

--- a/solution.py
+++ b/solution.py
@@ -289,7 +289,8 @@
 
 def all_sum(value):
     for stride, members in stages(lax.axis_size("hid")):
-        value = tree_sum([value] + [flip(value, "hid", stride * k) for k in range(1, members)])
+        arrived = [flip(value, "hid", stride * k) for k in reversed(range(1, members))]
+        value = tree_sum([value] + arrived[:1] + arrived[:0:-1])
     return value
 
 
@@ -297,7 +298,7 @@
     pieces = dict(pieces)
     for stride, members in plan:
         for offset in list(pieces):
-            for k in range(1, members):
+            for k in reversed(range(1, members)):
                 pieces[offset ^ (stride * k)] = flip(pieces[offset], "hid", stride * k)
     return pieces
 
@@ -400,11 +401,11 @@
                 full // 16,
                 "pack",
             )
-            packs = [flip(pack, "hid", 2 * k) for k, pack in enumerate(packs, 1)]
+            packs = [flip(pack, "hid", 2 * k) for k, pack in reversed(list(enumerate(packs, 1)))][::-1]
             grads, warm = on_device(
                 last_kernel,
                 [((rows_own, depth), F32), right_form],
-                (inverse, own_rows, own_right, *packs),
+                (inverse, own_rows, own_right, *packs[-1:], *packs[:-1]),
                 full // 16,
                 "last",
             )

time: 92.9 us -> 90 us (0.969)
  waiting for transfers between devices: 19.8 us -> 15.1 us
  starting transfers between devices: 33.8 us -> 35.5 us
    ppermute x39, waiting for transfers between devices: 17.4 us -> 13.1 us  [flip(): lax.ppermute(value, axis, [(source, source ^ bits) for source in range(co...]
    ppermute x39, starting transfers between devices: 30.8 us -> 32.5 us  [flip(): lax.ppermute(value, axis, [(source, source ^ bits) for source in range(co...]
  transfers between devices with their start and end apart: 41 -> 41, of which waited for: 17 -> 19; matrix products, arithmetic and copies ran while one was open for 1% -> 1% of each run, Pallas kernels for 26% -> 27%
where the time goes in v4:
time: 90 us; the launch traced here: 89.8 us
  Pallas kernels  36.5 us (41%)
  starting transfers between devices  35.5 us (39%)
  waiting for transfers between devices  15.1 us (17%)
  local copies, waits for them, and re-layouts  1.65 us (2%)
  between operations  1.01 us (1%)
    pallas_call x24, Pallas kernels, on_device(): pl.pallas_call(kernel, out_shape=shapes, in_specs=[VMEM] * (len(operands)...  36.5 us
    ppermute x39, starting transfers between devices, flip(): lax.ppermute(value, axis, [(source, source ^ bits) for source in range(co...  32.5 us
    ppermute x39, waiting for transfers between devices, flip(): lax.ppermute(value, axis, [(source, source ^ bits) for source in range(co...  13.1 us
    ppermute x2, starting transfers between devices, body(): lax.ppermute(leaving, 'pipe', [(source, source - 1) for source in range(1...  3 us
    ppermute x2, waiting for transfers between devices, body(): lax.ppermute(leaving, 'pipe', [(source, source - 1) for source in range(1...  2.02 us
  transfers between devices with their start and end apart: 41, of which 19 were waited for; matrix products, arithmetic and copies ran while one was open for 1% of the time, Pallas kernels for 27%

profile of v4, /device:TPU:0, one launch (start us, length us, event | category | flops | bytes accessed | tf_op | source)
XLA Modules:
  0.0 89.8 jit_solution(11187298542182130282)
XLA Ops:
  0.6 0.9 %copy-done.7 = bf16[1,3,32,1024]{3,2,1,0:T(8,128)(2,1)S(1)} copy-done((bf16[1,3,32,1024]{3,2,1,0:T(8,128)(2,1)S(1)}, bf16[1,3,32,1024]{3,2,1,0:T(8,128)(2,1)}, u32[]{:S(2)}) %copy-start.7) | copy-done | bytes 196632
  1.6 4.0 %collective-permute-start = (bf16[32,1024]{1,0:T(8,128)(2,1)S(1)}, bf16[32,1024]{1,0:T(8,128)(2,1)S(1)}, u32[]{:S(2)}, u32[]{:S(2)}) collective-permute-start(bf16[32,1024]{1,0:T(8,128)(2,1)S(1)} %get-tuple-element.33.refs_0_), channel_id=1, source_target_pairs={{0,6},{1,7},{2,4},{3,5},{4,2},{5,3},{6,0},{7,1},{8,14},{9,15},{10,... | collective-permute-start | bytes 196616 | tf_op jit(solution)/shard_map/ppermute | solution.py:272
  5.6 0.5 collective-permute-start.1
  6.3 2.8 %up.1 = (bf16[256,4096]{1,0:T(8,128)(2,1)S(1)}, f32[256,128]{1,0:T(8,128)S(1)}, f32[16,256]{1,0:T(8,128)S(1)}) custom-call(f32[3,16,256]{2,1,0:T(8,128)S(1)} %bitcast.37, f32[3,16,1024]{2,1,0:T(8,128)S(1)} %bitcast.34, f32[16,256]{1,0:T(8,128)S(1)} %bitcast.43, f32[16,1024]{1,0:T(8,128)S(1)} %bitcast.42, f32[16,1024]{1,0:T(8,128)S(1)} %bitcast.40, ...), custom_call_target="tpu_custom_call" | custom-call | flops 2147483648 | bytes 1048576 | tf_op jit(solution)/shard_map/up/pallas_call | solution.py:75
  9.1 0.6 collective-permute-start.4
  9.8 0.5 collective-permute-done.2.refs_3_
  10.4 1.4 %warm.3.refs_10_ = bf16[32,4096]{1,0:T(8,128)(2,1)S(1)} custom-call(f32[16,1024]{1,0:T(8,128)S(1)} %bitcast.41, bf16[1024,4096]{1,0:T(8,128)(2,1)S(1)} %bitcast.22), custom_call_target="tpu_custom_call" | custom-call | flops 1073741824 | bytes 1048576 | tf_op jit(solution)/shard_map/warm/pallas_call | solution.py:75
  11.9 3.2 %first.1 = (bf16[256,4096]{1,0:T(8,128)(2,1)S(1)}, f32[16,256]{1,0:T(8,128)S(1)}) custom-call(bf16[32,1024]{1,0:T(8,128)(2,1)S(1)} %get-tuple-element.33.refs_0_, bf16[32,1024]{1,0:T(8,128)(2,1)S(1)} %collective-permute-done.refs_1_, bf16[32,1024]{1,0:T(8,128)(2,1)S(1)} %collective-permute-done.1.refs_2_, ...), custom_call_target="tpu_custom_call" | custom-call | flops 2147483648 | bytes 1048576 | tf_op jit(solution)/shard_map/first/pallas_call | solution.py:75
  15.0 0.6 collective-permute-start.7
  15.6 2.2 %collective-permute-start.16 = (bf16[2,32,1024]{2,1,0:T(8,128)(2,1)S(1)}, bf16[2,32,1024]{2,1,0:T(8,128)(2,1)S(1)}, u32[]{:S(2)}, u32[]{:S(2)}) collective-permute-start(bf16[2,32,1024]{2,1,0:T(8,128)(2,1)S(1)} %get-tuple-element.43.refs_0_), channel_id=1, source_target_pairs={{0,6},{1,7},{2,4},{3,5},{4,2},{5,3},{6,0},{7,1},{8,14},{9,15},{10,... | collective-permute-start | bytes 393224 | tf_op jit(solution)/shard_map/ppermute | solution.py:272
  17.8 0.6 collective-permute-start.10
  18.4 1.7 %collective-permute-start.8 = (f32[16,256]{1,0:T(8,128)S(1)}, f32[16,256]{1,0:T(8,128)S(1)}, u32[]{:S(2)}, u32[]{:S(2)}) collective-permute-start(f32[16,256]{1,0:T(8,128)S(1)} %add.63), channel_id=1, source_target_pairs={{0,6},{1,7},{2,4},{3,5},{4,2},{5,3},{6,0},{7,1},{8,14},{9,15},{10,... | collective-permute-start | bytes 49160 | tf_op jit(solution)/shard_map/ppermute | solution.py:272
  20.1 1.3 %collective-permute-start.9 = (f32[16,256]{1,0:T(8,128)S(1)}, f32[16,256]{1,0:T(8,128)S(1)}, u32[]{:S(2)}, u32[]{:S(2)}) collective-permute-start(f32[16,256]{1,0:T(8,128)S(1)} %add.63), channel_id=1, source_target_pairs={{0,2},{1,3},{2,0},{3,1},{4,6},{5,7},{6,4},{7,5},{8,10},{9,11},{10,... | collective-permute-start | bytes 49160 | tf_op jit(solution)/shard_map/ppermute | solution.py:272
  21.4 2.4 %merged.3.merged_ref = f32[256,1024]{1,0:T(8,128)S(1)} custom-call(f32[256,128]{1,0:T(8,128)S(1)} %get-tuple-element.39.block_ref, bf16[256,4096]{1,0:T(8,128)(2,1)S(1)} %get-tuple-element.40.hidden_ref, bf16[1024,4096]{1,0:T(8,128)(2,1)S(1)} %bitcast.24), custom_call_target="tpu_custom_call" | custom-call | flops 2147483648 | bytes 1048576 | tf_op jit(solution)/shard_map/merged/pallas_call | solution.py:75
  23.9 0.3 right.3
  24.2 0.9 collective-permute-start.17
  25.1 1.1 %collective-permute-start.18 = (bf16[2,32,1024]{2,1,0:T(8,128)(2,1)S(1)}, bf16[2,32,1024]{2,1,0:T(8,128)(2,1)S(1)}, u32[]{:S(2)}, u32[]{:S(2)}) collective-permute-start(bf16[2,32,1024]{2,1,0:T(8,128)(2,1)S(1)} %get-tuple-element.43.refs_0_), channel_id=1, source_target_pairs={{0,2},{1,3},{2,0},{3,1},{4,6},{5,7},{6,4},{7,5},{8,10},{9,11},{10,... | collective-permute-start | bytes 393224 | tf_op jit(solution)/shard_map/ppermute | solution.py:272
  26.2 1.6 %collective-permute-start.12 = (f32[16,1024]{1,0:T(8,128)S(1)}, f32[16,1024]{1,0:T(8,128)S(1)}, u32[]{:S(2)}, u32[]{:S(2)}) collective-permute-start(f32[16,1024]{1,0:T(8,128)S(1)} %add.67), channel_id=1, source_target_pairs={{0,6},{1,7},{2,4},{3,5},{4,2},{5,3},{6,0},{7,1},{8,14},{9,15},{10,... | collective-permute-start | bytes 196616 | tf_op jit(solution)/shard_map/ppermute | solution.py:272
  27.8 1.3 %collective-permute-start.13 = (f32[16,1024]{1,0:T(8,128)S(1)}, f32[16,1024]{1,0:T(8,128)S(1)}, u32[]{:S(2)}, u32[]{:S(2)}) collective-permute-start(f32[16,1024]{1,0:T(8,128)S(1)} %add.67), channel_id=1, source_target_pairs={{0,2},{1,3},{2,0},{3,1},{4,6},{5,7},{6,4},{7,5},{8,10},{9,11},{10,... | collective-permute-start | bytes 196616 | tf_op jit(solution)/shard_map/ppermute | solution.py:272
  29.1 0.7 collective-permute-start.14
  29.7 1.6 %factor.3 = (f32[16,256]{1,0:T(8,128)S(1)}, f32[16,16]{1,0:T(8,128)S(1)}) custom-call(f32[16,256]{1,0:T(8,128)S(1)} %add_add_fusion.4.proj_ref), custom_call_target="tpu_custom_call" | custom-call | flops 1073741824 | bytes 1048576 | tf_op jit(solution)/shard_map/factor/pallas_call | solution.py:75
  31.4 0.4 collective-permute-start.20
  31.8 1.7 %collective-permute-done.12 = f32[16,1024]{1,0:T(8,128)S(1)} collective-permute-done((f32[16,1024]{1,0:T(8,128)S(1)}, f32[16,1024]{1,0:T(8,128)S(1)}, u32[]{:S(2)}, u32[]{:S(2)}) %collective-permute-start.12) | collective-permute-done | bytes 65568 | tf_op jit(solution)/shard_map/ppermute | solution.py:272
  33.5 0.5 collective-permute-start.22
  34.2 1.5 %collective-permute-start.15 = (f32[16,1280]{1,0:T(8,128)S(1)}, f32[16,1280]{1,0:T(8,128)S(1)}, u32[]{:S(2)}, u32[]{:S(2)}) collective-permute-start(f32[16,1280]{1,0:T(8,128)S(1)} %get-tuple-element.41.refs_9_), channel_id=1, source_target_pairs={{8,0},{16,8},{24,16},{9,1},{17,9},{25,17},{10,2},{18,10},{26,18},{... | collective-permute-start | bytes 245768 | tf_op jit(solution)/shard_map/ppermute | solution.py:423
  35.7 2.4 %mask.2.mask_ref = bf16[256,4096]{1,0:T(8,128)(2,1)S(1)} custom-call(bf16[2,32,1024]{2,1,0:T(8,128)(2,1)S(1)} %get-tuple-element.43.refs_0_, bf16[2,32,1024]{2,1,0:T(8,128)(2,1)S(1)} %collective-permute-done.16.refs_1_, bf16[2,32,1024]{2,1,0:T(8,128)(2,1)S(1)} %collective-permute-done.17.refs_2_, bf16[2,32,1024]{2,1,0:T(8,128)(2,1)S(1)} %collective-permute-done.18.refs_3_, ...), custom_call_target="tpu_custom_call" | custom-call | flops 2147483648 | bytes 1048576 | tf_op jit(solution)/shard_map/mask/pallas_call | solution.py:75
  38.1 1.4 %warm.4.warm_in_ref = bf16[32,4096]{1,0:T(8,128)(2,1)S(1)} custom-call(f32[16,1024]{1,0:T(8,128)S(1)} %get-tuple-element.42.warm_ref, bf16[1024,4096]{1,0:T(8,128)(2,1)S(1)} %bitcast.26), custom_call_target="tpu_custom_call" | custom-call | flops 1073741824 | bytes 1048576 | tf_op jit(solution)/shard_map/warm/pallas_call | solution.py:75
  39.5 1.0 %collective-permute-done.15.both_ref = f32[16,1280]{1,0:T(8,128)S(1)} collective-permute-done((f32[16,1280]{1,0:T(8,128)S(1)}, f32[16,1280]{1,0:T(8,128)S(1)}, u32[]{:S(2)}, u32[]{:S(2)}) %collective-permute-start.15) | collective-permute-done | bytes 81952 | tf_op jit(solution)/shard_map/ppermute | solution.py:423
  40.5 3.7 %hidden.2 = (bf16[256,4096]{1,0:T(8,128)(2,1)S(1)}, f32[16,256]{1,0:T(8,128)S(1)}, f32[256,128]{1,0:T(8,128)S(1)}) custom-call(f32[3,16,256]{2,1,0:T(8,128)S(1)} %bitcast.38, f32[3,16,1024]{2,1,0:T(8,128)S(1)} %bitcast.35, f32[16,1280]{1,0:T(8,128)S(1)} %collective-permute-done.15.both_ref, f32[16,1024]{1,0:T(8,128)S(1)} %get-tuple-element.42.warm_ref, ...), custom_call_target="tpu_custom_call" | custom-call | flops 2147483648 | bytes 1048576 | tf_op jit(solution)/shard_map/hidden/pallas_call | solution.py:75
  44.3 1.2 %collective-permute-done.23 = f32[16,256]{1,0:T(8,128)S(1)} collective-permute-done((f32[16,256]{1,0:T(8,128)S(1)}, f32[16,256]{1,0:T(8,128)S(1)}, u32[]{:S(2)}, u32[]{:S(2)}) %collective-permute-start.23) | collective-permute-done | bytes 16416 | tf_op jit(solution)/shard_map/ppermute | solution.py:272
  45.5 1.8 %collective-permute-start.24 = (f32[16,256]{1,0:T(8,128)S(1)}, f32[16,256]{1,0:T(8,128)S(1)}, u32[]{:S(2)}, u32[]{:S(2)}) collective-permute-start(f32[16,256]{1,0:T(8,128)S(1)} %add.71), channel_id=1, source_target_pairs={{0,6},{1,7},{2,4},{3,5},{4,2},{5,3},{6,0},{7,1},{8,14},{9,15},{10,... | collective-permute-start | bytes 49160 | tf_op jit(solution)/shard_map/ppermute | solution.py:272
  47.3 0.7 collective-permute-start.25
  48.0 1.0 %collective-permute-start.26 = (f32[16,256]{1,0:T(8,128)S(1)}, f32[16,256]{1,0:T(8,128)S(1)}, u32[]{:S(2)}, u32[]{:S(2)}) collective-permute-start(f32[16,256]{1,0:T(8,128)S(1)} %add.71), channel_id=1, source_target_pairs={{0,4},{1,5},{2,6},{3,7},{4,0},{5,1},{6,2},{7,3},{8,12},{9,13},{10,... | collective-permute-start | bytes 49160 | tf_op jit(solution)/shard_map/ppermute | solution.py:272
  49.0 2.4 %merged.4.merged_ref = f32[256,1024]{1,0:T(8,128)S(1)} custom-call(f32[256,128]{1,0:T(8,128)S(1)} %get-tuple-element.47.block_ref, bf16[256,4096]{1,0:T(8,128)(2,1)S(1)} %get-tuple-element.48.hidden_ref, bf16[1024,4096]{1,0:T(8,128)(2,1)S(1)} %bitcast.27), custom_call_target="tpu_custom_call" | custom-call | flops 2147483648 | bytes 1048576 | tf_op jit(solution)/shard_map/merged/pallas_call | solution.py:75
  51.4 0.4 collective-permute-done.26
  51.8 0.3 right.4
  52.1 1.3 %collective-permute-done.27 = f32[16,1024]{1,0:T(8,128)S(1)} collective-permute-done((f32[16,1024]{1,0:T(8,128)S(1)}, f32[16,1024]{1,0:T(8,128)S(1)}, u32[]{:S(2)}, u32[]{:S(2)}) %collective-permute-start.27) | collective-permute-done | bytes 65568 | tf_op jit(solution)/shard_map/ppermute | solution.py:272
  53.3 1.7 %collective-permute-start.28 = (f32[16,1024]{1,0:T(8,128)S(1)}, f32[16,1024]{1,0:T(8,128)S(1)}, u32[]{:S(2)}, u32[]{:S(2)}) collective-permute-start(f32[16,1024]{1,0:T(8,128)S(1)} %add.75), channel_id=1, source_target_pairs={{0,6},{1,7},{2,4},{3,5},{4,2},{5,3},{6,0},{7,1},{8,14},{9,15},{10,... | collective-permute-start | bytes 196616 | tf_op jit(solution)/shard_map/ppermute | solution.py:272
  55.1 0.8 collective-permute-start.29
  55.8 1.1 %collective-permute-start.30 = (f32[16,1024]{1,0:T(8,128)S(1)}, f32[16,1024]{1,0:T(8,128)S(1)}, u32[]{:S(2)}, u32[]{:S(2)}) collective-permute-start(f32[16,1024]{1,0:T(8,128)S(1)} %add.75), channel_id=1, source_target_pairs={{0,4},{1,5},{2,6},{3,7},{4,0},{5,1},{6,2},{7,3},{8,12},{9,13},{10,... | collective-permute-start | bytes 196616 | tf_op jit(solution)/shard_map/ppermute | solution.py:272
  56.9 1.6 %factor.4 = (f32[16,256]{1,0:T(8,128)S(1)}, f32[16,16]{1,0:T(8,128)S(1)}) custom-call(f32[16,256]{1,0:T(8,128)S(1)} %add_add_fusion.3.proj_ref), custom_call_target="tpu_custom_call" | custom-call | flops 1073741824 | bytes 1048576 | tf_op jit(solution)/shard_map/factor/pallas_call | solution.py:75
  58.5 0.6 collective-permute-done.28
  59.1 0.4 collective-permute-done.29
  59.5 0.6 collective-permute-done.30
  60.3 1.5 %collective-permute-start.31 = (f32[16,1280]{1,0:T(8,128)S(1)}, f32[16,1280]{1,0:T(8,128)S(1)}, u32[]{:S(2)}, u32[]{:S(2)}) collective-permute-start(f32[16,1280]{1,0:T(8,128)S(1)} %get-tuple-element.49.refs_9_), channel_id=1, source_target_pairs={{8,0},{16,8},{24,16},{9,1},{17,9},{25,17},{10,2},{18,10},{26,18},{... | collective-permute-start | bytes 245768 | tf_op jit(solution)/shard_map/ppermute | solution.py:423
  61.8 2.4 %mask.3.mask_ref = bf16[256,4096]{1,0:T(8,128)(2,1)S(1)} custom-call(bf16[2,32,1024]{2,1,0:T(8,128)(2,1)S(1)} %get-tuple-element.43.refs_0_, bf16[2,32,1024]{2,1,0:T(8,128)(2,1)S(1)} %collective-permute-done.16.refs_1_, bf16[2,32,1024]{2,1,0:T(8,128)(2,1)S(1)} %collective-permute-done.17.refs_2_, bf16[2,32,1024]{2,1,0:T(8,128)(2,1)S(1)} %collective-permute-done.18.refs_3_, ...), custom_call_target="tpu_custom_call" | custom-call | flops 2147483648 | bytes 1048576 | tf_op jit(solution)/shard_map/mask/pallas_call | solution.py:75
  64.2 1.4 %warm.5.warm_in_ref = bf16[32,4096]{1,0:T(8,128)(2,1)S(1)} custom-call(f32[16,1024]{1,0:T(8,128)S(1)} %get-tuple-element.50.warm_ref, bf16[1024,4096]{1,0:T(8,128)(2,1)S(1)} %bitcast.29), custom_call_target="tpu_custom_call" | custom-call | flops 1073741824 | bytes 1048576 | tf_op jit(solution)/shard_map/warm/pallas_call | solution.py:75
  65.6 1.0 %collective-permute-done.31.both_ref = f32[16,1280]{1,0:T(8,128)S(1)} collective-permute-done((f32[16,1280]{1,0:T(8,128)S(1)}, f32[16,1280]{1,0:T(8,128)S(1)}, u32[]{:S(2)}, u32[]{:S(2)}) %collective-permute-start.31) | collective-permute-done | bytes 81952 | tf_op jit(solution)/shard_map/ppermute | solution.py:423
  66.7 3.7 %hidden.3 = (bf16[256,4096]{1,0:T(8,128)(2,1)S(1)}, f32[16,256]{1,0:T(8,128)S(1)}, f32[256,128]{1,0:T(8,128)S(1)}) custom-call(f32[3,16,256]{2,1,0:T(8,128)S(1)} %bitcast.39, f32[3,16,1024]{2,1,0:T(8,128)S(1)} %bitcast.36, f32[16,1280]{1,0:T(8,128)S(1)} %collective-permute-done.31.both_ref, f32[16,1024]{1,0:T(8,128)S(1)} %get-tuple-element.50.warm_ref, ...), custom_call_target="tpu_custom_call" | custom-call | flops 2147483648 | bytes 1048576 | tf_op jit(solution)/shard_map/hidden/pallas_call | solution.py:75
  70.4 1.2 %collective-permute-done.32 = f32[16,256]{1,0:T(8,128)S(1)} collective-permute-done((f32[16,256]{1,0:T(8,128)S(1)}, f32[16,256]{1,0:T(8,128)S(1)}, u32[]{:S(2)}, u32[]{:S(2)}) %collective-permute-start.32) | collective-permute-done | bytes 16416 | tf_op jit(solution)/shard_map/ppermute | solution.py:272
  71.6 1.8 %collective-permute-start.33 = (f32[16,256]{1,0:T(8,128)S(1)}, f32[16,256]{1,0:T(8,128)S(1)}, u32[]{:S(2)}, u32[]{:S(2)}) collective-permute-start(f32[16,256]{1,0:T(8,128)S(1)} %add.79), channel_id=1, source_target_pairs={{0,6},{1,7},{2,4},{3,5},{4,2},{5,3},{6,0},{7,1},{8,14},{9,15},{10,... | collective-permute-start | bytes 49160 | tf_op jit(solution)/shard_map/ppermute | solution.py:272
  73.4 0.7 collective-permute-start.34
  74.1 1.0 %collective-permute-start.35 = (f32[16,256]{1,0:T(8,128)S(1)}, f32[16,256]{1,0:T(8,128)S(1)}, u32[]{:S(2)}, u32[]{:S(2)}) collective-permute-start(f32[16,256]{1,0:T(8,128)S(1)} %add.79), channel_id=1, source_target_pairs={{0,4},{1,5},{2,6},{3,7},{4,0},{5,1},{6,2},{7,3},{8,12},{9,13},{10,... | collective-permute-start | bytes 49160 | tf_op jit(solution)/shard_map/ppermute | solution.py:272
  75.1 2.4 %merged.5.merged_ref = f32[256,1024]{1,0:T(8,128)S(1)} custom-call(f32[256,128]{1,0:T(8,128)S(1)} %get-tuple-element.53.block_ref, bf16[256,4096]{1,0:T(8,128)(2,1)S(1)} %get-tuple-element.54.hidden_ref, bf16[1024,4096]{1,0:T(8,128)(2,1)S(1)} %bitcast.30), custom_call_target="tpu_custom_call" | custom-call | flops 2147483648 | bytes 1048576 | tf_op jit(solution)/shard_map/merged/pallas_call | solution.py:75
  78.4 1.0 %collective-permute-done.37.right_arrived_ref = f32[16,1024]{1,0:T(8,128)S(1)} collective-permute-done((f32[16,1024]{1,0:T(8,128)S(1)}, f32[16,1024]{1,0:T(8,128)S(1)}, u32[]{:S(2)}, u32[]{:S(2)}) %collective-permute-start.37) | collective-permute-done | bytes 65568 | tf_op jit(solution)/shard_map/ppermute | solution.py:272
  79.5 1.7 %collective-permute-start.38 = (bf16[64,1024]{1,0:T(8,128)(2,1)S(1)}, bf16[64,1024]{1,0:T(8,128)(2,1)S(1)}, u32[]{:S(2)}, u32[]{:S(2)}) collective-permute-start(bf16[64,1024]{1,0:T(8,128)(2,1)S(1)} %get-tuple-element.57), channel_id=1, source_target_pairs={{0,6},{1,7},{2,4},{3,5},{4,2},{5,3},{6,0},{7,1},{8,14},{9,15},{10,... | collective-permute-start | bytes 393224 | tf_op jit(solution)/shard_map/ppermute | solution.py:272
  81.3 0.7 collective-permute-start.39
  82.0 1.1 %collective-permute-start.40 = (bf16[64,1024]{1,0:T(8,128)(2,1)S(1)}, bf16[64,1024]{1,0:T(8,128)(2,1)S(1)}, u32[]{:S(2)}, u32[]{:S(2)}) collective-permute-start(bf16[64,1024]{1,0:T(8,128)(2,1)S(1)} %get-tuple-element.59), channel_id=1, source_target_pairs={{0,4},{1,5},{2,6},{3,7},{4,0},{5,1},{6,2},{7,3},{8,12},{9,13},{10,... | collective-permute-start | bytes 393224 | tf_op jit(solution)/shard_map/ppermute | solution.py:272
  83.1 1.6 %factor.5 = (f32[16,256]{1,0:T(8,128)S(1)}, f32[16,16]{1,0:T(8,128)S(1)}) custom-call(f32[16,256]{1,0:T(8,128)S(1)} %add_add_fusion.2.proj_ref), custom_call_target="tpu_custom_call" | custom-call | flops 1073741824 | bytes 1048576 | tf_op jit(solution)/shard_map/factor/pallas_call | solution.py:75
  84.6 0.7 dynamic-slice_bitcast_fusion
  85.3 1.5 %collective-permute-done.38.refs_0_ = bf16[64,1024]{1,0:T(8,128)(2,1)S(1)} collective-permute-done((bf16[64,1024]{1,0:T(8,128)(2,1)S(1)}, bf16[64,1024]{1,0:T(8,128)(2,1)S(1)}, u32[]{:S(2)}, u32[]{:S(2)}) %collective-permute-start.38) | collective-permute-done | bytes 131104 | tf_op jit(solution)/shard_map/ppermute | solution.py:272
  86.8 1.7 %collective-permute-done.39.refs_1_ = bf16[64,1024]{1,0:T(8,128)(2,1)S(1)} collective-permute-done((bf16[64,1024]{1,0:T(8,128)(2,1)S(1)}, bf16[64,1024]{1,0:T(8,128)(2,1)S(1)}, u32[]{:S(2)}, u32[]{:S(2)}) %collective-permute-start.39) | collective-permute-done | bytes 131104 | tf_op jit(solution)/shard_map/ppermute | solution.py:272
  88.5 0.4 collective-permute-done.40.refs_2_
  88.9 0.9 last.1
  (69 shorter events, 2.2 us)
Async XLA Ops:
  0.6 0.9 %copy-start.7 = (bf16[1,3,32,1024]{3,2,1,0:T(8,128)(2,1)S(1)}, bf16[1,3,32,1024]{3,2,1,0:T(8,128)(2,1)}, u32[]{:S(2)}) copy-start(bf16[1,3,32,1024]{3,2,1,0:T(8,128)(2,1)} %param.8) | copy-start | bytes 589828
  1.6 4.7 %copy-start.1 = (bf16[1,4096,1024]{2,1,0:T(8,128)(2,1)S(1)}, bf16[1,4096,1024]{2,1,0:T(8,128)(2,1)}, u32[]{:S(2)}) copy-start(bf16[1,4096,1024]{2,1,0:T(8,128)(2,1)} %param.10) | copy-start | bytes 25165828
  1.6 4.7 %copy-start.2 = (f32[3,1024,16]{1,2,0:T(8,128)S(1)}, f32[3,1024,16]{1,2,0:T(8,128)}, u32[]{:S(2)}) copy-start(f32[3,1024,16]{1,2,0:T(8,128)} %param.15) | copy-start | bytes 589828
  1.6 4.7 %copy-start.3 = (f32[3,256,16]{1,2,0:T(8,128)S(1)}, f32[3,256,16]{1,2,0:T(8,128)}, u32[]{:S(2)}) copy-start(f32[3,256,16]{1,2,0:T(8,128)} %param.14) | copy-start | bytes 147460
  1.6 4.7 %copy-start.4 = (f32[1,1024,16]{1,2,0:T(8,128)S(1)}, f32[1,1024,16]{1,2,0:T(8,128)}, u32[]{:S(2)}) copy-start(f32[1,1024,16]{1,2,0:T(8,128)} %param.11) | copy-start | bytes 196612
  1.6 4.7 %copy-start.5 = (f32[1,1024,16]{1,2,0:T(8,128)S(1)}, f32[1,1024,16]{1,2,0:T(8,128)}, u32[]{:S(2)}) copy-start(f32[1,1024,16]{1,2,0:T(8,128)} %param.13) | copy-start | bytes 196612
  1.6 4.7 %copy-start.6 = (f32[1,256,16]{1,2,0:T(8,128)S(1)}, f32[1,256,16]{1,2,0:T(8,128)}, u32[]{:S(2)}) copy-start(f32[1,256,16]{1,2,0:T(8,128)} %param.12) | copy-start | bytes 49156
  1.6 7.5 %collective-permute-start = (bf16[32,1024]{1,0:T(8,128)(2,1)S(1)}, bf16[32,1024]{1,0:T(8,128)(2,1)S(1)}, u32[]{:S(2)}, u32[]{:S(2)}) collective-permute-start(bf16[32,1024]{1,0:T(8,128)(2,1)S(1)} %get-tuple-element.33.refs_0_), channel_id=1, source_target_pairs={{0,6},{1,7},{2,4},{3,5},{4,2},{5,3},{6,0},{7,1},{8,14},{9,15},{10,... | collective-permute-start | bytes 196616 | tf_op jit(solution)/shard_map/ppermute | solution.py:272
  5.6 4.3 %collective-permute-start.1 = (bf16[32,1024]{1,0:T(8,128)(2,1)S(1)}, bf16[32,1024]{1,0:T(8,128)(2,1)S(1)}, u32[]{:S(2)}, u32[]{:S(2)}) collective-permute-start(bf16[32,1024]{1,0:T(8,128)(2,1)S(1)} %get-tuple-element.33.refs_0_), channel_id=1, source_target_pairs={{0,4},{1,5},{2,6},{3,7},{4,0},{5,1},{6,2},{7,3},{8,12},{9,13},{10,... | collective-permute-start | bytes 196616 | tf_op jit(solution)/shard_map/ppermute | solution.py:272
  6.1 4.3 %collective-permute-start.2 = (bf16[32,1024]{1,0:T(8,128)(2,1)S(1)}, bf16[32,1024]{1,0:T(8,128)(2,1)S(1)}, u32[]{:S(2)}, u32[]{:S(2)}) collective-permute-start(bf16[32,1024]{1,0:T(8,128)(2,1)S(1)} %get-tuple-element.33.refs_0_), channel_id=1, source_target_pairs={{0,2},{1,3},{2,0},{3,1},{4,6},{5,7},{6,4},{7,5},{8,10},{9,11},{10,... | collective-permute-start | bytes 196616 | tf_op jit(solution)/shard_map/ppermute | solution.py:272
  6.2 5.6 %collective-permute-start.3 = (bf16[32,1024]{1,0:T(8,128)(2,1)S(1)}, bf16[32,1024]{1,0:T(8,128)(2,1)S(1)}, u32[]{:S(2)}, u32[]{:S(2)}) collective-permute-start(bf16[32,1024]{1,0:T(8,128)(2,1)S(1)} %get-tuple-element.33.refs_0_), channel_id=1, source_target_pairs={{0,1},{1,0},{2,3},{3,2},{4,5},{5,4},{6,7},{7,6},{8,9},{9,8},{10,11... | collective-permute-start | bytes 196616 | tf_op jit(solution)/shard_map/ppermute | solution.py:272
  6.3 4.1 %copy-start = (bf16[1,1024,4096]{2,1,0:T(8,128)(2,1)S(1)}, bf16[1,1024,4096]{2,1,0:T(8,128)(2,1)}, u32[]{:S(2)}) copy-start(bf16[1,1024,4096]{2,1,0:T(8,128)(2,1)} %param.9) | copy-start | bytes 25165828
  9.1 2.7 %collective-permute-start.4 = (bf16[32,1024]{1,0:T(8,128)(2,1)S(1)}, bf16[32,1024]{1,0:T(8,128)(2,1)S(1)}, u32[]{:S(2)}, u32[]{:S(2)}) collective-permute-start(bf16[32,1024]{1,0:T(8,128)(2,1)S(1)} %collective-permute-done.refs_1_), channel_id=1, source_target_pairs={{0,1},{1,0},{2,3},{3,2},{4,5},{5,4},{6,7},{7,6},{8,9},{9,8},{10,11... | collective-permute-start | bytes 196616 | tf_op jit(solution)/shard_map/ppermute | solution.py:272
  9.8 2.0 %collective-permute-start.5 = (bf16[32,1024]{1,0:T(8,128)(2,1)S(1)}, bf16[32,1024]{1,0:T(8,128)(2,1)S(1)}, u32[]{:S(2)}, u32[]{:S(2)}) collective-permute-start(bf16[32,1024]{1,0:T(8,128)(2,1)S(1)} %collective-permute-done.1.refs_2_), channel_id=1, source_target_pairs={{0,1},{1,0},{2,3},{3,2},{4,5},{5,4},{6,7},{7,6},{8,9},{9,8},{10,11... | collective-permute-start | bytes 196616 | tf_op jit(solution)/shard_map/ppermute | solution.py:272
  10.3 1.5 %collective-permute-start.6 = (bf16[32,1024]{1,0:T(8,128)(2,1)S(1)}, bf16[32,1024]{1,0:T(8,128)(2,1)S(1)}, u32[]{:S(2)}, u32[]{:S(2)}) collective-permute-start(bf16[32,1024]{1,0:T(8,128)(2,1)S(1)} %collective-permute-done.2.refs_3_), channel_id=1, source_target_pairs={{0,1},{1,0},{2,3},{3,2},{4,5},{5,4},{6,7},{7,6},{8,9},{9,8},{10,11... | collective-permute-start | bytes 196616 | tf_op jit(solution)/shard_map/ppermute | solution.py:272
  15.0 2.8 %collective-permute-start.7 = (f32[16,256]{1,0:T(8,128)S(1)}, f32[16,256]{1,0:T(8,128)S(1)}, u32[]{:S(2)}, u32[]{:S(2)}) collective-permute-start(f32[16,256]{1,0:T(8,128)S(1)} %get-tuple-element.36), channel_id=1, source_target_pairs={{0,1},{1,0},{2,3},{3,2},{4,5},{5,4},{6,7},{7,6},{8,9},{9,8},{10,11... | collective-permute-start | bytes 49160 | tf_op jit(solution)/shard_map/ppermute | solution.py:272
  15.6 13.5 %collective-permute-start.16 = (bf16[2,32,1024]{2,1,0:T(8,128)(2,1)S(1)}, bf16[2,32,1024]{2,1,0:T(8,128)(2,1)S(1)}, u32[]{:S(2)}, u32[]{:S(2)}) collective-permute-start(bf16[2,32,1024]{2,1,0:T(8,128)(2,1)S(1)} %get-tuple-element.43.refs_0_), channel_id=1, source_target_pairs={{0,6},{1,7},{2,4},{3,5},{4,2},{5,3},{6,0},{7,1},{8,14},{9,15},{10,... | collective-permute-start | bytes 393224 | tf_op jit(solution)/shard_map/ppermute | solution.py:272
  17.8 5.9 %collective-permute-start.10 = (f32[16,256]{1,0:T(8,128)S(1)}, f32[16,256]{1,0:T(8,128)S(1)}, u32[]{:S(2)}, u32[]{:S(2)}) collective-permute-start(f32[16,256]{1,0:T(8,128)S(1)} %add.63), channel_id=1, source_target_pairs={{0,4},{1,5},{2,6},{3,7},{4,0},{5,1},{6,2},{7,3},{8,12},{9,13},{10,... | collective-permute-start | bytes 49160 | tf_op jit(solution)/shard_map/ppermute | solution.py:272
  18.4 5.4 %collective-permute-start.8 = (f32[16,256]{1,0:T(8,128)S(1)}, f32[16,256]{1,0:T(8,128)S(1)}, u32[]{:S(2)}, u32[]{:S(2)}) collective-permute-start(f32[16,256]{1,0:T(8,128)S(1)} %add.63), channel_id=1, source_target_pairs={{0,6},{1,7},{2,4},{3,5},{4,2},{5,3},{6,0},{7,1},{8,14},{9,15},{10,... | collective-permute-start | bytes 49160 | tf_op jit(solution)/shard_map/ppermute | solution.py:272
  20.1 3.7 %collective-permute-start.9 = (f32[16,256]{1,0:T(8,128)S(1)}, f32[16,256]{1,0:T(8,128)S(1)}, u32[]{:S(2)}, u32[]{:S(2)}) collective-permute-start(f32[16,256]{1,0:T(8,128)S(1)} %add.63), channel_id=1, source_target_pairs={{0,2},{1,3},{2,0},{3,1},{4,6},{5,7},{6,4},{7,5},{8,10},{9,11},{10,... | collective-permute-start | bytes 49160 | tf_op jit(solution)/shard_map/ppermute | solution.py:272
  24.2 2.0 %collective-permute-start.11 = (f32[16,1024]{1,0:T(8,128)S(1)}, f32[16,1024]{1,0:T(8,128)S(1)}, u32[]{:S(2)}, u32[]{:S(2)}) collective-permute-start(f32[16,1024]{1,0:T(8,128)S(1)} %right.3), channel_id=1, source_target_pairs={{0,1},{1,0},{2,3},{3,2},{4,5},{5,4},{6,7},{7,6},{8,9},{9,8},{10,11... | collective-permute-start | bytes 196616 | tf_op jit(solution)/shard_map/ppermute | solution.py:272
  24.2 7.1 %collective-permute-start.17 = (bf16[2,32,1024]{2,1,0:T(8,128)(2,1)S(1)}, bf16[2,32,1024]{2,1,0:T(8,128)(2,1)S(1)}, u32[]{:S(2)}, u32[]{:S(2)}) collective-permute-start(bf16[2,32,1024]{2,1,0:T(8,128)(2,1)S(1)} %get-tuple-element.43.refs_0_), channel_id=1, source_target_pairs={{0,4},{1,5},{2,6},{3,7},{4,0},{5,1},{6,2},{7,3},{8,12},{9,13},{10,... | collective-permute-start | bytes 393224 | tf_op jit(solution)/shard_map/ppermute | solution.py:272
  25.1 6.3 %collective-permute-start.18 = (bf16[2,32,1024]{2,1,0:T(8,128)(2,1)S(1)}, bf16[2,32,1024]{2,1,0:T(8,128)(2,1)S(1)}, u32[]{:S(2)}, u32[]{:S(2)}) collective-permute-start(bf16[2,32,1024]{2,1,0:T(8,128)(2,1)S(1)} %get-tuple-element.43.refs_0_), channel_id=1, source_target_pairs={{0,2},{1,3},{2,0},{3,1},{4,6},{5,7},{6,4},{7,5},{8,10},{9,11},{10,... | collective-permute-start | bytes 393224 | tf_op jit(solution)/shard_map/ppermute | solution.py:272
  26.2 7.3 %collective-permute-start.12 = (f32[16,1024]{1,0:T(8,128)S(1)}, f32[16,1024]{1,0:T(8,128)S(1)}, u32[]{:S(2)}, u32[]{:S(2)}) collective-permute-start(f32[16,1024]{1,0:T(8,128)S(1)} %add.67), channel_id=1, source_target_pairs={{0,6},{1,7},{2,4},{3,5},{4,2},{5,3},{6,0},{7,1},{8,14},{9,15},{10,... | collective-permute-start | bytes 196616 | tf_op jit(solution)/shard_map/ppermute | solution.py:272
  27.8 5.7 %collective-permute-start.13 = (f32[16,1024]{1,0:T(8,128)S(1)}, f32[16,1024]{1,0:T(8,128)S(1)}, u32[]{:S(2)}, u32[]{:S(2)}) collective-permute-start(f32[16,1024]{1,0:T(8,128)S(1)} %add.67), channel_id=1, source_target_pairs={{0,2},{1,3},{2,0},{3,1},{4,6},{5,7},{6,4},{7,5},{8,10},{9,11},{10,... | collective-permute-start | bytes 196616 | tf_op jit(solution)/shard_map/ppermute | solution.py:272
  29.1 4.9 %collective-permute-start.14 = (f32[16,1024]{1,0:T(8,128)S(1)}, f32[16,1024]{1,0:T(8,128)S(1)}, u32[]{:S(2)}, u32[]{:S(2)}) collective-permute-start(f32[16,1024]{1,0:T(8,128)S(1)} %add.67), channel_id=1, source_target_pairs={{0,4},{1,5},{2,6},{3,7},{4,0},{5,1},{6,2},{7,3},{8,12},{9,13},{10,... | collective-permute-start | bytes 196616 | tf_op jit(solution)/shard_map/ppermute | solution.py:272
  31.3 4.4 %collective-permute-start.19 = (bf16[2,32,1024]{2,1,0:T(8,128)(2,1)S(1)}, bf16[2,32,1024]{2,1,0:T(8,128)(2,1)S(1)}, u32[]{:S(2)}, u32[]{:S(2)}) collective-permute-start(bf16[2,32,1024]{2,1,0:T(8,128)(2,1)S(1)} %get-tuple-element.43.refs_0_), channel_id=1, source_target_pairs={{0,1},{1,0},{2,3},{3,2},{4,5},{5,4},{6,7},{7,6},{8,9},{9,8},{10,11... | collective-permute-start | bytes 393224 | tf_op jit(solution)/shard_map/ppermute | solution.py:272
  31.4 4.3 %collective-permute-start.20 = (bf16[2,32,1024]{2,1,0:T(8,128)(2,1)S(1)}, bf16[2,32,1024]{2,1,0:T(8,128)(2,1)S(1)}, u32[]{:S(2)}, u32[]{:S(2)}) collective-permute-start(bf16[2,32,1024]{2,1,0:T(8,128)(2,1)S(1)} %collective-permute-done.16.refs_1_), channel_id=1, source_target_pairs={{0,1},{1,0},{2,3},{3,2},{4,5},{5,4},{6,7},{7,6},{8,9},{9,8},{10,11... | collective-permute-start | bytes 393224 | tf_op jit(solution)/shard_map/ppermute | solution.py:272
  33.5 2.2 %collective-permute-start.21 = (bf16[2,32,1024]{2,1,0:T(8,128)(2,1)S(1)}, bf16[2,32,1024]{2,1,0:T(8,128)(2,1)S(1)}, u32[]{:S(2)}, u32[]{:S(2)}) collective-permute-start(bf16[2,32,1024]{2,1,0:T(8,128)(2,1)S(1)} %collective-permute-done.17.refs_2_), channel_id=1, source_target_pairs={{0,1},{1,0},{2,3},{3,2},{4,5},{5,4},{6,7},{7,6},{8,9},{9,8},{10,11... | collective-permute-start | bytes 393224 | tf_op jit(solution)/shard_map/ppermute | solution.py:272
  33.5 2.2 %collective-permute-start.22 = (bf16[2,32,1024]{2,1,0:T(8,128)(2,1)S(1)}, bf16[2,32,1024]{2,1,0:T(8,128)(2,1)S(1)}, u32[]{:S(2)}, u32[]{:S(2)}) collective-permute-start(bf16[2,32,1024]{2,1,0:T(8,128)(2,1)S(1)} %collective-permute-done.18.refs_3_), channel_id=1, source_target_pairs={{0,1},{1,0},{2,3},{3,2},{4,5},{5,4},{6,7},{7,6},{8,9},{9,8},{10,11... | collective-permute-start | bytes 393224 | tf_op jit(solution)/shard_map/ppermute | solution.py:272
  34.2 6.3 %collective-permute-start.15 = (f32[16,1280]{1,0:T(8,128)S(1)}, f32[16,1280]{1,0:T(8,128)S(1)}, u32[]{:S(2)}, u32[]{:S(2)}) collective-permute-start(f32[16,1280]{1,0:T(8,128)S(1)} %get-tuple-element.41.refs_9_), channel_id=1, source_target_pairs={{8,0},{16,8},{24,16},{9,1},{17,9},{25,17},{10,2},{18,10},{26,18},{... | collective-permute-start | bytes 245768 | tf_op jit(solution)/shard_map/ppermute | solution.py:423
  44.2 1.2 %collective-permute-start.23 = (f32[16,256]{1,0:T(8,128)S(1)}, f32[16,256]{1,0:T(8,128)S(1)}, u32[]{:S(2)}, u32[]{:S(2)}) collective-permute-start(f32[16,256]{1,0:T(8,128)S(1)} %get-tuple-element.44), channel_id=1, source_target_pairs={{0,1},{1,0},{2,3},{3,2},{4,5},{5,4},{6,7},{7,6},{8,9},{9,8},{10,11... | collective-permute-start | bytes 49160 | tf_op jit(solution)/shard_map/ppermute | solution.py:272
  45.5 5.9 %collective-permute-start.24 = (f32[16,256]{1,0:T(8,128)S(1)}, f32[16,256]{1,0:T(8,128)S(1)}, u32[]{:S(2)}, u32[]{:S(2)}) collective-permute-start(f32[16,256]{1,0:T(8,128)S(1)} %add.71), channel_id=1, source_target_pairs={{0,6},{1,7},{2,4},{3,5},{4,2},{5,3},{6,0},{7,1},{8,14},{9,15},{10,... | collective-permute-start | bytes 49160 | tf_op jit(solution)/shard_map/ppermute | solution.py:272
  47.3 4.1 %collective-permute-start.25 = (f32[16,256]{1,0:T(8,128)S(1)}, f32[16,256]{1,0:T(8,128)S(1)}, u32[]{:S(2)}, u32[]{:S(2)}) collective-permute-start(f32[16,256]{1,0:T(8,128)S(1)} %add.71), channel_id=1, source_target_pairs={{0,2},{1,3},{2,0},{3,1},{4,6},{5,7},{6,4},{7,5},{8,10},{9,11},{10,... | collective-permute-start | bytes 49160 | tf_op jit(solution)/shard_map/ppermute | solution.py:272
  48.0 3.7 %collective-permute-start.26 = (f32[16,256]{1,0:T(8,128)S(1)}, f32[16,256]{1,0:T(8,128)S(1)}, u32[]{:S(2)}, u32[]{:S(2)}) collective-permute-start(f32[16,256]{1,0:T(8,128)S(1)} %add.71), channel_id=1, source_target_pairs={{0,4},{1,5},{2,6},{3,7},{4,0},{5,1},{6,2},{7,3},{8,12},{9,13},{10,... | collective-permute-start | bytes 49160 | tf_op jit(solution)/shard_map/ppermute | solution.py:272
  52.1 1.3 %collective-permute-start.27 = (f32[16,1024]{1,0:T(8,128)S(1)}, f32[16,1024]{1,0:T(8,128)S(1)}, u32[]{:S(2)}, u32[]{:S(2)}) collective-permute-start(f32[16,1024]{1,0:T(8,128)S(1)} %right.4), channel_id=1, source_target_pairs={{0,1},{1,0},{2,3},{3,2},{4,5},{5,4},{6,7},{7,6},{8,9},{9,8},{10,11... | collective-permute-start | bytes 196616 | tf_op jit(solution)/shard_map/ppermute | solution.py:272
  53.3 5.7 %collective-permute-start.28 = (f32[16,1024]{1,0:T(8,128)S(1)}, f32[16,1024]{1,0:T(8,128)S(1)}, u32[]{:S(2)}, u32[]{:S(2)}) collective-permute-start(f32[16,1024]{1,0:T(8,128)S(1)} %add.75), channel_id=1, source_target_pairs={{0,6},{1,7},{2,4},{3,5},{4,2},{5,3},{6,0},{7,1},{8,14},{9,15},{10,... | collective-permute-start | bytes 196616 | tf_op jit(solution)/shard_map/ppermute | solution.py:272
  55.1 4.4 %collective-permute-start.29 = (f32[16,1024]{1,0:T(8,128)S(1)}, f32[16,1024]{1,0:T(8,128)S(1)}, u32[]{:S(2)}, u32[]{:S(2)}) collective-permute-start(f32[16,1024]{1,0:T(8,128)S(1)} %add.75), channel_id=1, source_target_pairs={{0,2},{1,3},{2,0},{3,1},{4,6},{5,7},{6,4},{7,5},{8,10},{9,11},{10,... | collective-permute-start | bytes 196616 | tf_op jit(solution)/shard_map/ppermute | solution.py:272
  55.8 4.3 %collective-permute-start.30 = (f32[16,1024]{1,0:T(8,128)S(1)}, f32[16,1024]{1,0:T(8,128)S(1)}, u32[]{:S(2)}, u32[]{:S(2)}) collective-permute-start(f32[16,1024]{1,0:T(8,128)S(1)} %add.75), channel_id=1, source_target_pairs={{0,4},{1,5},{2,6},{3,7},{4,0},{5,1},{6,2},{7,3},{8,12},{9,13},{10,... | collective-permute-start | bytes 196616 | tf_op jit(solution)/shard_map/ppermute | solution.py:272
  60.3 6.3 %collective-permute-start.31 = (f32[16,1280]{1,0:T(8,128)S(1)}, f32[16,1280]{1,0:T(8,128)S(1)}, u32[]{:S(2)}, u32[]{:S(2)}) collective-permute-start(f32[16,1280]{1,0:T(8,128)S(1)} %get-tuple-element.49.refs_9_), channel_id=1, source_target_pairs={{8,0},{16,8},{24,16},{9,1},{17,9},{25,17},{10,2},{18,10},{26,18},{... | collective-permute-start | bytes 245768 | tf_op jit(solution)/shard_map/ppermute | solution.py:423
  70.4 1.2 %collective-permute-start.32 = (f32[16,256]{1,0:T(8,128)S(1)}, f32[16,256]{1,0:T(8,128)S(1)}, u32[]{:S(2)}, u32[]{:S(2)}) collective-permute-start(f32[16,256]{1,0:T(8,128)S(1)} %get-tuple-element.51), channel_id=1, source_target_pairs={{0,1},{1,0},{2,3},{3,2},{4,5},{5,4},{6,7},{7,6},{8,9},{9,8},{10,11... | collective-permute-start | bytes 49160 | tf_op jit(solution)/shard_map/ppermute | solution.py:272
  71.6 6.0 %collective-permute-start.33 = (f32[16,256]{1,0:T(8,128)S(1)}, f32[16,256]{1,0:T(8,128)S(1)}, u32[]{:S(2)}, u32[]{:S(2)}) collective-permute-start(f32[16,256]{1,0:T(8,128)S(1)} %add.79), channel_id=1, source_target_pairs={{0,6},{1,7},{2,4},{3,5},{4,2},{5,3},{6,0},{7,1},{8,14},{9,15},{10,... | collective-permute-start | bytes 49160 | tf_op jit(solution)/shard_map/ppermute | solution.py:272
  73.4 4.2 %collective-permute-start.34 = (f32[16,256]{1,0:T(8,128)S(1)}, f32[16,256]{1,0:T(8,128)S(1)}, u32[]{:S(2)}, u32[]{:S(2)}) collective-permute-start(f32[16,256]{1,0:T(8,128)S(1)} %add.79), channel_id=1, source_target_pairs={{0,2},{1,3},{2,0},{3,1},{4,6},{5,7},{6,4},{7,5},{8,10},{9,11},{10,... | collective-permute-start | bytes 49160 | tf_op jit(solution)/shard_map/ppermute | solution.py:272
  74.1 3.7 %collective-permute-start.35 = (f32[16,256]{1,0:T(8,128)S(1)}, f32[16,256]{1,0:T(8,128)S(1)}, u32[]{:S(2)}, u32[]{:S(2)}) collective-permute-start(f32[16,256]{1,0:T(8,128)S(1)} %add.79), channel_id=1, source_target_pairs={{0,4},{1,5},{2,6},{3,7},{4,0},{5,1},{6,2},{7,3},{8,12},{9,13},{10,... | collective-permute-start | bytes 49160 | tf_op jit(solution)/shard_map/ppermute | solution.py:272
  77.5 1.9 %collective-permute-start.36 = (bf16[4,32,1024]{2,1,0:T(8,128)(2,1)S(1)}, bf16[4,32,1024]{2,1,0:T(8,128)(2,1)S(1)}, u32[]{:S(2)}, u32[]{:S(2)}) collective-permute-start(bf16[4,32,1024]{2,1,0:T(8,128)(2,1)S(1)} %outgoing.1), channel_id=1, source_target_pairs={{0,1},{1,0},{2,3},{3,2},{4,5},{5,4},{6,7},{7,6},{8,9},{9,8},{10,11... | collective-permute-start | bytes 786440 | tf_op jit(solution)/shard_map/ppermute | solution.py:272
  78.2 1.3 %collective-permute-start.37 = (f32[16,1024]{1,0:T(8,128)S(1)}, f32[16,1024]{1,0:T(8,128)S(1)}, u32[]{:S(2)}, u32[]{:S(2)}) collective-permute-start(f32[16,1024]{1,0:T(8,128)S(1)} %right.5.right_ref), channel_id=1, source_target_pairs={{0,1},{1,0},{2,3},{3,2},{4,5},{5,4},{6,7},{7,6},{8,9},{9,8},{10,11... | collective-permute-start | bytes 196616 | tf_op jit(solution)/shard_map/ppermute | solution.py:272
  79.5 7.3 %collective-permute-start.38 = (bf16[64,1024]{1,0:T(8,128)(2,1)S(1)}, bf16[64,1024]{1,0:T(8,128)(2,1)S(1)}, u32[]{:S(2)}, u32[]{:S(2)}) collective-permute-start(bf16[64,1024]{1,0:T(8,128)(2,1)S(1)} %get-tuple-element.57), channel_id=1, source_target_pairs={{0,6},{1,7},{2,4},{3,5},{4,2},{5,3},{6,0},{7,1},{8,14},{9,15},{10,... | collective-permute-start | bytes 393224 | tf_op jit(solution)/shard_map/ppermute | solution.py:272
  81.3 7.3 %collective-permute-start.39 = (bf16[64,1024]{1,0:T(8,128)(2,1)S(1)}, bf16[64,1024]{1,0:T(8,128)(2,1)S(1)}, u32[]{:S(2)}, u32[]{:S(2)}) collective-permute-start(bf16[64,1024]{1,0:T(8,128)(2,1)S(1)} %get-tuple-element.58), channel_id=1, source_target_pairs={{0,2},{1,3},{2,0},{3,1},{4,6},{5,7},{6,4},{7,5},{8,10},{9,11},{10,... | collective-permute-start | bytes 393224 | tf_op jit(solution)/shard_map/ppermute | solution.py:272
  82.0 6.9 %collective-permute-start.40 = (bf16[64,1024]{1,0:T(8,128)(2,1)S(1)}, bf16[64,1024]{1,0:T(8,128)(2,1)S(1)}, u32[]{:S(2)}, u32[]{:S(2)}) collective-permute-start(bf16[64,1024]{1,0:T(8,128)(2,1)S(1)} %get-tuple-element.59), channel_id=1, source_target_pairs={{0,4},{1,5},{2,6},{3,7},{4,0},{5,1},{6,2},{7,3},{8,12},{9,13},{10,... | collective-permute-start | bytes 393224 | tf_op jit(solution)/shard_map/ppermute | solution.py:272

commit v5 on v4

--- a/solution.py
+++ b/solution.py
@@ -294,11 +294,11 @@
     return value
 
 
-def gather_pieces(pieces, plan):
+def gather_pieces(pieces, plan, order=reversed):
     pieces = dict(pieces)
     for stride, members in plan:
         for offset in list(pieces):
-            for k in reversed(range(1, members)):
+            for k in order(range(1, members)):
                 pieces[offset ^ (stride * k)] = flip(pieces[offset], "hid", stride * k)
     return pieces
 
@@ -331,8 +331,8 @@
             "begin",
         )
         blocks = gather_pieces({0: rows_first}, plan[1:] + plan[:1])
-        later = gather_pieces({0: rows_later}, plan[1:] + plan[:1])
-        offsets, pieces, later = list(blocks), list(blocks.values()), list(later.values())
+        later = gather_pieces({0: rows_later}, plan[1:] + plan[:1], list)
+        offsets, pieces, later = list(blocks), list(blocks.values()), [later[offset] for offset in blocks]
     else:
         everything = lax.all_gather(inputs, "hid", axis=1, tiled=True)
         offsets, pieces, later = [0], [everything[0]], [everything[1:]]

time: 90 us -> 90 us (level)
  no operation moved by 1% of the time
where the time goes in v5:
time: 90 us; the launch traced here: 89.8 us
  Pallas kernels  36.5 us (41%)
  starting transfers between devices  35.5 us (39%)
  waiting for transfers between devices  15.1 us (17%)
  local copies, waits for them, and re-layouts  1.65 us (2%)
  between operations  1.01 us (1%)
    pallas_call x24, Pallas kernels, on_device(): pl.pallas_call(kernel, out_shape=shapes, in_specs=[VMEM] * (len(operands)...  36.5 us
    ppermute x39, starting transfers between devices, flip(): lax.ppermute(value, axis, [(source, source ^ bits) for source in range(co...  32.5 us
    ppermute x39, waiting for transfers between devices, flip(): lax.ppermute(value, axis, [(source, source ^ bits) for source in range(co...  13.1 us
    ppermute x2, starting transfers between devices, body(): lax.ppermute(leaving, 'pipe', [(source, source - 1) for source in range(1...  3 us
    ppermute x2, waiting for transfers between devices, body(): lax.ppermute(leaving, 'pipe', [(source, source - 1) for source in range(1...  2.02 us
  transfers between devices with their start and end apart: 41, of which 19 were waited for; matrix products, arithmetic and copies ran while one was open for 1% of the time, Pallas kernels for 27%

profile of v5, /device:TPU:0, one launch (start us, length us, event | category | flops | bytes accessed | tf_op | source)
XLA Modules:
  0.0 89.8 jit_solution(11187298542182130282)
XLA Ops:
  0.6 0.9 %copy-done.7 = bf16[1,3,32,1024]{3,2,1,0:T(8,128)(2,1)S(1)} copy-done((bf16[1,3,32,1024]{3,2,1,0:T(8,128)(2,1)S(1)}, bf16[1,3,32,1024]{3,2,1,0:T(8,128)(2,1)}, u32[]{:S(2)}) %copy-start.7) | copy-done | bytes 196632
  1.6 4.0 %collective-permute-start = (bf16[32,1024]{1,0:T(8,128)(2,1)S(1)}, bf16[32,1024]{1,0:T(8,128)(2,1)S(1)}, u32[]{:S(2)}, u32[]{:S(2)}) collective-permute-start(bf16[32,1024]{1,0:T(8,128)(2,1)S(1)} %get-tuple-element.33.refs_0_), channel_id=1, source_target_pairs={{0,6},{1,7},{2,4},{3,5},{4,2},{5,3},{6,0},{7,1},{8,14},{9,15},{10,... | collective-permute-start | bytes 196616 | tf_op jit(solution)/shard_map/ppermute | solution.py:272
  5.6 0.5 collective-permute-start.1
  6.3 2.8 %up.1 = (bf16[256,4096]{1,0:T(8,128)(2,1)S(1)}, f32[256,128]{1,0:T(8,128)S(1)}, f32[16,256]{1,0:T(8,128)S(1)}) custom-call(f32[3,16,256]{2,1,0:T(8,128)S(1)} %bitcast.37, f32[3,16,1024]{2,1,0:T(8,128)S(1)} %bitcast.34, f32[16,256]{1,0:T(8,128)S(1)} %bitcast.43, f32[16,1024]{1,0:T(8,128)S(1)} %bitcast.42, f32[16,1024]{1,0:T(8,128)S(1)} %bitcast.40, ...), custom_call_target="tpu_custom_call" | custom-call | flops 2147483648 | bytes 1048576 | tf_op jit(solution)/shard_map/up/pallas_call | solution.py:75
  9.1 0.6 collective-permute-start.4
  9.8 0.5 collective-permute-done.2.refs_3_
  10.4 1.4 %warm.3.refs_10_ = bf16[32,4096]{1,0:T(8,128)(2,1)S(1)} custom-call(f32[16,1024]{1,0:T(8,128)S(1)} %bitcast.41, bf16[1024,4096]{1,0:T(8,128)(2,1)S(1)} %bitcast.22), custom_call_target="tpu_custom_call" | custom-call | flops 1073741824 | bytes 1048576 | tf_op jit(solution)/shard_map/warm/pallas_call | solution.py:75
  11.9 3.2 %first.1 = (bf16[256,4096]{1,0:T(8,128)(2,1)S(1)}, f32[16,256]{1,0:T(8,128)S(1)}) custom-call(bf16[32,1024]{1,0:T(8,128)(2,1)S(1)} %get-tuple-element.33.refs_0_, bf16[32,1024]{1,0:T(8,128)(2,1)S(1)} %collective-permute-done.refs_1_, bf16[32,1024]{1,0:T(8,128)(2,1)S(1)} %collective-permute-done.1.refs_2_, ...), custom_call_target="tpu_custom_call" | custom-call | flops 2147483648 | bytes 1048576 | tf_op jit(solution)/shard_map/first/pallas_call | solution.py:75
  15.0 0.6 collective-permute-start.7
  15.6 2.2 %collective-permute-start.16 = (bf16[2,32,1024]{2,1,0:T(8,128)(2,1)S(1)}, bf16[2,32,1024]{2,1,0:T(8,128)(2,1)S(1)}, u32[]{:S(2)}, u32[]{:S(2)}) collective-permute-start(bf16[2,32,1024]{2,1,0:T(8,128)(2,1)S(1)} %get-tuple-element.43.refs_0_), channel_id=1, source_target_pairs={{0,6},{1,7},{2,4},{3,5},{4,2},{5,3},{6,0},{7,1},{8,14},{9,15},{10,... | collective-permute-start | bytes 393224 | tf_op jit(solution)/shard_map/ppermute | solution.py:272
  17.8 0.6 collective-permute-start.10
  18.4 1.7 %collective-permute-start.8 = (f32[16,256]{1,0:T(8,128)S(1)}, f32[16,256]{1,0:T(8,128)S(1)}, u32[]{:S(2)}, u32[]{:S(2)}) collective-permute-start(f32[16,256]{1,0:T(8,128)S(1)} %add.63), channel_id=1, source_target_pairs={{0,6},{1,7},{2,4},{3,5},{4,2},{5,3},{6,0},{7,1},{8,14},{9,15},{10,... | collective-permute-start | bytes 49160 | tf_op jit(solution)/shard_map/ppermute | solution.py:272
  20.1 1.3 %collective-permute-start.9 = (f32[16,256]{1,0:T(8,128)S(1)}, f32[16,256]{1,0:T(8,128)S(1)}, u32[]{:S(2)}, u32[]{:S(2)}) collective-permute-start(f32[16,256]{1,0:T(8,128)S(1)} %add.63), channel_id=1, source_target_pairs={{0,2},{1,3},{2,0},{3,1},{4,6},{5,7},{6,4},{7,5},{8,10},{9,11},{10,... | collective-permute-start | bytes 49160 | tf_op jit(solution)/shard_map/ppermute | solution.py:272
  21.4 2.4 %merged.3.merged_ref = f32[256,1024]{1,0:T(8,128)S(1)} custom-call(f32[256,128]{1,0:T(8,128)S(1)} %get-tuple-element.39.block_ref, bf16[256,4096]{1,0:T(8,128)(2,1)S(1)} %get-tuple-element.40.hidden_ref, bf16[1024,4096]{1,0:T(8,128)(2,1)S(1)} %bitcast.24), custom_call_target="tpu_custom_call" | custom-call | flops 2147483648 | bytes 1048576 | tf_op jit(solution)/shard_map/merged/pallas_call | solution.py:75
  23.9 0.3 right.3
  24.2 0.9 collective-permute-start.17
  25.1 1.1 %collective-permute-start.18 = (bf16[2,32,1024]{2,1,0:T(8,128)(2,1)S(1)}, bf16[2,32,1024]{2,1,0:T(8,128)(2,1)S(1)}, u32[]{:S(2)}, u32[]{:S(2)}) collective-permute-start(bf16[2,32,1024]{2,1,0:T(8,128)(2,1)S(1)} %get-tuple-element.43.refs_0_), channel_id=1, source_target_pairs={{0,2},{1,3},{2,0},{3,1},{4,6},{5,7},{6,4},{7,5},{8,10},{9,11},{10,... | collective-permute-start | bytes 393224 | tf_op jit(solution)/shard_map/ppermute | solution.py:272
  26.2 1.6 %collective-permute-start.12 = (f32[16,1024]{1,0:T(8,128)S(1)}, f32[16,1024]{1,0:T(8,128)S(1)}, u32[]{:S(2)}, u32[]{:S(2)}) collective-permute-start(f32[16,1024]{1,0:T(8,128)S(1)} %add.67), channel_id=1, source_target_pairs={{0,6},{1,7},{2,4},{3,5},{4,2},{5,3},{6,0},{7,1},{8,14},{9,15},{10,... | collective-permute-start | bytes 196616 | tf_op jit(solution)/shard_map/ppermute | solution.py:272
  27.8 1.3 %collective-permute-start.13 = (f32[16,1024]{1,0:T(8,128)S(1)}, f32[16,1024]{1,0:T(8,128)S(1)}, u32[]{:S(2)}, u32[]{:S(2)}) collective-permute-start(f32[16,1024]{1,0:T(8,128)S(1)} %add.67), channel_id=1, source_target_pairs={{0,2},{1,3},{2,0},{3,1},{4,6},{5,7},{6,4},{7,5},{8,10},{9,11},{10,... | collective-permute-start | bytes 196616 | tf_op jit(solution)/shard_map/ppermute | solution.py:272
  29.1 0.7 collective-permute-start.14
  29.7 1.6 %factor.3 = (f32[16,256]{1,0:T(8,128)S(1)}, f32[16,16]{1,0:T(8,128)S(1)}) custom-call(f32[16,256]{1,0:T(8,128)S(1)} %add_add_fusion.4.proj_ref), custom_call_target="tpu_custom_call" | custom-call | flops 1073741824 | bytes 1048576 | tf_op jit(solution)/shard_map/factor/pallas_call | solution.py:75
  31.4 0.4 collective-permute-start.20
  31.8 1.7 %collective-permute-done.12 = f32[16,1024]{1,0:T(8,128)S(1)} collective-permute-done((f32[16,1024]{1,0:T(8,128)S(1)}, f32[16,1024]{1,0:T(8,128)S(1)}, u32[]{:S(2)}, u32[]{:S(2)}) %collective-permute-start.12) | collective-permute-done | bytes 65568 | tf_op jit(solution)/shard_map/ppermute | solution.py:272
  33.5 0.5 collective-permute-start.22
  34.2 1.5 %collective-permute-start.15 = (f32[16,1280]{1,0:T(8,128)S(1)}, f32[16,1280]{1,0:T(8,128)S(1)}, u32[]{:S(2)}, u32[]{:S(2)}) collective-permute-start(f32[16,1280]{1,0:T(8,128)S(1)} %get-tuple-element.41.refs_9_), channel_id=1, source_target_pairs={{8,0},{16,8},{24,16},{9,1},{17,9},{25,17},{10,2},{18,10},{26,18},{... | collective-permute-start | bytes 245768 | tf_op jit(solution)/shard_map/ppermute | solution.py:423
  35.7 2.4 %mask.2.mask_ref = bf16[256,4096]{1,0:T(8,128)(2,1)S(1)} custom-call(bf16[2,32,1024]{2,1,0:T(8,128)(2,1)S(1)} %get-tuple-element.43.refs_0_, bf16[2,32,1024]{2,1,0:T(8,128)(2,1)S(1)} %collective-permute-done.16.refs_1_, bf16[2,32,1024]{2,1,0:T(8,128)(2,1)S(1)} %collective-permute-done.17.refs_2_, bf16[2,32,1024]{2,1,0:T(8,128)(2,1)S(1)} %collective-permute-done.18.refs_3_, ...), custom_call_target="tpu_custom_call" | custom-call | flops 2147483648 | bytes 1048576 | tf_op jit(solution)/shard_map/mask/pallas_call | solution.py:75
  38.1 1.4 %warm.4.warm_in_ref = bf16[32,4096]{1,0:T(8,128)(2,1)S(1)} custom-call(f32[16,1024]{1,0:T(8,128)S(1)} %get-tuple-element.42.warm_ref, bf16[1024,4096]{1,0:T(8,128)(2,1)S(1)} %bitcast.26), custom_call_target="tpu_custom_call" | custom-call | flops 1073741824 | bytes 1048576 | tf_op jit(solution)/shard_map/warm/pallas_call | solution.py:75
  39.5 1.0 %collective-permute-done.15.both_ref = f32[16,1280]{1,0:T(8,128)S(1)} collective-permute-done((f32[16,1280]{1,0:T(8,128)S(1)}, f32[16,1280]{1,0:T(8,128)S(1)}, u32[]{:S(2)}, u32[]{:S(2)}) %collective-permute-start.15) | collective-permute-done | bytes 81952 | tf_op jit(solution)/shard_map/ppermute | solution.py:423
  40.5 3.7 %hidden.2 = (bf16[256,4096]{1,0:T(8,128)(2,1)S(1)}, f32[16,256]{1,0:T(8,128)S(1)}, f32[256,128]{1,0:T(8,128)S(1)}) custom-call(f32[3,16,256]{2,1,0:T(8,128)S(1)} %bitcast.38, f32[3,16,1024]{2,1,0:T(8,128)S(1)} %bitcast.35, f32[16,1280]{1,0:T(8,128)S(1)} %collective-permute-done.15.both_ref, f32[16,1024]{1,0:T(8,128)S(1)} %get-tuple-element.42.warm_ref, ...), custom_call_target="tpu_custom_call" | custom-call | flops 2147483648 | bytes 1048576 | tf_op jit(solution)/shard_map/hidden/pallas_call | solution.py:75
  44.3 1.2 %collective-permute-done.23 = f32[16,256]{1,0:T(8,128)S(1)} collective-permute-done((f32[16,256]{1,0:T(8,128)S(1)}, f32[16,256]{1,0:T(8,128)S(1)}, u32[]{:S(2)}, u32[]{:S(2)}) %collective-permute-start.23) | collective-permute-done | bytes 16416 | tf_op jit(solution)/shard_map/ppermute | solution.py:272
  45.5 1.8 %collective-permute-start.24 = (f32[16,256]{1,0:T(8,128)S(1)}, f32[16,256]{1,0:T(8,128)S(1)}, u32[]{:S(2)}, u32[]{:S(2)}) collective-permute-start(f32[16,256]{1,0:T(8,128)S(1)} %add.71), channel_id=1, source_target_pairs={{0,6},{1,7},{2,4},{3,5},{4,2},{5,3},{6,0},{7,1},{8,14},{9,15},{10,... | collective-permute-start | bytes 49160 | tf_op jit(solution)/shard_map/ppermute | solution.py:272
  47.3 0.7 collective-permute-start.25
  48.0 1.0 %collective-permute-start.26 = (f32[16,256]{1,0:T(8,128)S(1)}, f32[16,256]{1,0:T(8,128)S(1)}, u32[]{:S(2)}, u32[]{:S(2)}) collective-permute-start(f32[16,256]{1,0:T(8,128)S(1)} %add.71), channel_id=1, source_target_pairs={{0,4},{1,5},{2,6},{3,7},{4,0},{5,1},{6,2},{7,3},{8,12},{9,13},{10,... | collective-permute-start | bytes 49160 | tf_op jit(solution)/shard_map/ppermute | solution.py:272
  49.0 2.4 %merged.4.merged_ref = f32[256,1024]{1,0:T(8,128)S(1)} custom-call(f32[256,128]{1,0:T(8,128)S(1)} %get-tuple-element.47.block_ref, bf16[256,4096]{1,0:T(8,128)(2,1)S(1)} %get-tuple-element.48.hidden_ref, bf16[1024,4096]{1,0:T(8,128)(2,1)S(1)} %bitcast.27), custom_call_target="tpu_custom_call" | custom-call | flops 2147483648 | bytes 1048576 | tf_op jit(solution)/shard_map/merged/pallas_call | solution.py:75
  51.4 0.4 collective-permute-done.26
  51.8 0.3 right.4
  52.1 1.3 %collective-permute-done.27 = f32[16,1024]{1,0:T(8,128)S(1)} collective-permute-done((f32[16,1024]{1,0:T(8,128)S(1)}, f32[16,1024]{1,0:T(8,128)S(1)}, u32[]{:S(2)}, u32[]{:S(2)}) %collective-permute-start.27) | collective-permute-done | bytes 65568 | tf_op jit(solution)/shard_map/ppermute | solution.py:272
  53.3 1.7 %collective-permute-start.28 = (f32[16,1024]{1,0:T(8,128)S(1)}, f32[16,1024]{1,0:T(8,128)S(1)}, u32[]{:S(2)}, u32[]{:S(2)}) collective-permute-start(f32[16,1024]{1,0:T(8,128)S(1)} %add.75), channel_id=1, source_target_pairs={{0,6},{1,7},{2,4},{3,5},{4,2},{5,3},{6,0},{7,1},{8,14},{9,15},{10,... | collective-permute-start | bytes 196616 | tf_op jit(solution)/shard_map/ppermute | solution.py:272
  55.1 0.8 collective-permute-start.29
  55.8 1.1 %collective-permute-start.30 = (f32[16,1024]{1,0:T(8,128)S(1)}, f32[16,1024]{1,0:T(8,128)S(1)}, u32[]{:S(2)}, u32[]{:S(2)}) collective-permute-start(f32[16,1024]{1,0:T(8,128)S(1)} %add.75), channel_id=1, source_target_pairs={{0,4},{1,5},{2,6},{3,7},{4,0},{5,1},{6,2},{7,3},{8,12},{9,13},{10,... | collective-permute-start | bytes 196616 | tf_op jit(solution)/shard_map/ppermute | solution.py:272
  56.9 1.6 %factor.4 = (f32[16,256]{1,0:T(8,128)S(1)}, f32[16,16]{1,0:T(8,128)S(1)}) custom-call(f32[16,256]{1,0:T(8,128)S(1)} %add_add_fusion.3.proj_ref), custom_call_target="tpu_custom_call" | custom-call | flops 1073741824 | bytes 1048576 | tf_op jit(solution)/shard_map/factor/pallas_call | solution.py:75
  58.5 0.6 collective-permute-done.28
  59.1 0.4 collective-permute-done.29
  59.5 0.6 collective-permute-done.30
  60.3 1.5 %collective-permute-start.31 = (f32[16,1280]{1,0:T(8,128)S(1)}, f32[16,1280]{1,0:T(8,128)S(1)}, u32[]{:S(2)}, u32[]{:S(2)}) collective-permute-start(f32[16,1280]{1,0:T(8,128)S(1)} %get-tuple-element.49.refs_9_), channel_id=1, source_target_pairs={{8,0},{16,8},{24,16},{9,1},{17,9},{25,17},{10,2},{18,10},{26,18},{... | collective-permute-start | bytes 245768 | tf_op jit(solution)/shard_map/ppermute | solution.py:423
  61.8 2.4 %mask.3.mask_ref = bf16[256,4096]{1,0:T(8,128)(2,1)S(1)} custom-call(bf16[2,32,1024]{2,1,0:T(8,128)(2,1)S(1)} %get-tuple-element.43.refs_0_, bf16[2,32,1024]{2,1,0:T(8,128)(2,1)S(1)} %collective-permute-done.16.refs_1_, bf16[2,32,1024]{2,1,0:T(8,128)(2,1)S(1)} %collective-permute-done.17.refs_2_, bf16[2,32,1024]{2,1,0:T(8,128)(2,1)S(1)} %collective-permute-done.18.refs_3_, ...), custom_call_target="tpu_custom_call" | custom-call | flops 2147483648 | bytes 1048576 | tf_op jit(solution)/shard_map/mask/pallas_call | solution.py:75
  64.2 1.4 %warm.5.warm_in_ref = bf16[32,4096]{1,0:T(8,128)(2,1)S(1)} custom-call(f32[16,1024]{1,0:T(8,128)S(1)} %get-tuple-element.50.warm_ref, bf16[1024,4096]{1,0:T(8,128)(2,1)S(1)} %bitcast.29), custom_call_target="tpu_custom_call" | custom-call | flops 1073741824 | bytes 1048576 | tf_op jit(solution)/shard_map/warm/pallas_call | solution.py:75
  65.6 1.0 %collective-permute-done.31.both_ref = f32[16,1280]{1,0:T(8,128)S(1)} collective-permute-done((f32[16,1280]{1,0:T(8,128)S(1)}, f32[16,1280]{1,0:T(8,128)S(1)}, u32[]{:S(2)}, u32[]{:S(2)}) %collective-permute-start.31) | collective-permute-done | bytes 81952 | tf_op jit(solution)/shard_map/ppermute | solution.py:423
  66.7 3.7 %hidden.3 = (bf16[256,4096]{1,0:T(8,128)(2,1)S(1)}, f32[16,256]{1,0:T(8,128)S(1)}, f32[256,128]{1,0:T(8,128)S(1)}) custom-call(f32[3,16,256]{2,1,0:T(8,128)S(1)} %bitcast.39, f32[3,16,1024]{2,1,0:T(8,128)S(1)} %bitcast.36, f32[16,1280]{1,0:T(8,128)S(1)} %collective-permute-done.31.both_ref, f32[16,1024]{1,0:T(8,128)S(1)} %get-tuple-element.50.warm_ref, ...), custom_call_target="tpu_custom_call" | custom-call | flops 2147483648 | bytes 1048576 | tf_op jit(solution)/shard_map/hidden/pallas_call | solution.py:75
  70.4 1.2 %collective-permute-done.32 = f32[16,256]{1,0:T(8,128)S(1)} collective-permute-done((f32[16,256]{1,0:T(8,128)S(1)}, f32[16,256]{1,0:T(8,128)S(1)}, u32[]{:S(2)}, u32[]{:S(2)}) %collective-permute-start.32) | collective-permute-done | bytes 16416 | tf_op jit(solution)/shard_map/ppermute | solution.py:272
  71.6 1.8 %collective-permute-start.33 = (f32[16,256]{1,0:T(8,128)S(1)}, f32[16,256]{1,0:T(8,128)S(1)}, u32[]{:S(2)}, u32[]{:S(2)}) collective-permute-start(f32[16,256]{1,0:T(8,128)S(1)} %add.79), channel_id=1, source_target_pairs={{0,6},{1,7},{2,4},{3,5},{4,2},{5,3},{6,0},{7,1},{8,14},{9,15},{10,... | collective-permute-start | bytes 49160 | tf_op jit(solution)/shard_map/ppermute | solution.py:272
  73.4 0.7 collective-permute-start.34
  74.1 1.0 %collective-permute-start.35 = (f32[16,256]{1,0:T(8,128)S(1)}, f32[16,256]{1,0:T(8,128)S(1)}, u32[]{:S(2)}, u32[]{:S(2)}) collective-permute-start(f32[16,256]{1,0:T(8,128)S(1)} %add.79), channel_id=1, source_target_pairs={{0,4},{1,5},{2,6},{3,7},{4,0},{5,1},{6,2},{7,3},{8,12},{9,13},{10,... | collective-permute-start | bytes 49160 | tf_op jit(solution)/shard_map/ppermute | solution.py:272
  75.1 2.4 %merged.5.merged_ref = f32[256,1024]{1,0:T(8,128)S(1)} custom-call(f32[256,128]{1,0:T(8,128)S(1)} %get-tuple-element.53.block_ref, bf16[256,4096]{1,0:T(8,128)(2,1)S(1)} %get-tuple-element.54.hidden_ref, bf16[1024,4096]{1,0:T(8,128)(2,1)S(1)} %bitcast.30), custom_call_target="tpu_custom_call" | custom-call | flops 2147483648 | bytes 1048576 | tf_op jit(solution)/shard_map/merged/pallas_call | solution.py:75
  78.4 1.0 %collective-permute-done.37.right_arrived_ref = f32[16,1024]{1,0:T(8,128)S(1)} collective-permute-done((f32[16,1024]{1,0:T(8,128)S(1)}, f32[16,1024]{1,0:T(8,128)S(1)}, u32[]{:S(2)}, u32[]{:S(2)}) %collective-permute-start.37) | collective-permute-done | bytes 65568 | tf_op jit(solution)/shard_map/ppermute | solution.py:272
  79.5 1.7 %collective-permute-start.38 = (bf16[64,1024]{1,0:T(8,128)(2,1)S(1)}, bf16[64,1024]{1,0:T(8,128)(2,1)S(1)}, u32[]{:S(2)}, u32[]{:S(2)}) collective-permute-start(bf16[64,1024]{1,0:T(8,128)(2,1)S(1)} %get-tuple-element.57), channel_id=1, source_target_pairs={{0,6},{1,7},{2,4},{3,5},{4,2},{5,3},{6,0},{7,1},{8,14},{9,15},{10,... | collective-permute-start | bytes 393224 | tf_op jit(solution)/shard_map/ppermute | solution.py:272
  81.3 0.7 collective-permute-start.39
  82.0 1.1 %collective-permute-start.40 = (bf16[64,1024]{1,0:T(8,128)(2,1)S(1)}, bf16[64,1024]{1,0:T(8,128)(2,1)S(1)}, u32[]{:S(2)}, u32[]{:S(2)}) collective-permute-start(bf16[64,1024]{1,0:T(8,128)(2,1)S(1)} %get-tuple-element.59), channel_id=1, source_target_pairs={{0,4},{1,5},{2,6},{3,7},{4,0},{5,1},{6,2},{7,3},{8,12},{9,13},{10,... | collective-permute-start | bytes 393224 | tf_op jit(solution)/shard_map/ppermute | solution.py:272
  83.1 1.6 %factor.5 = (f32[16,256]{1,0:T(8,128)S(1)}, f32[16,16]{1,0:T(8,128)S(1)}) custom-call(f32[16,256]{1,0:T(8,128)S(1)} %add_add_fusion.2.proj_ref), custom_call_target="tpu_custom_call" | custom-call | flops 1073741824 | bytes 1048576 | tf_op jit(solution)/shard_map/factor/pallas_call | solution.py:75
  84.6 0.7 dynamic-slice_bitcast_fusion
  85.3 1.5 %collective-permute-done.38.refs_0_ = bf16[64,1024]{1,0:T(8,128)(2,1)S(1)} collective-permute-done((bf16[64,1024]{1,0:T(8,128)(2,1)S(1)}, bf16[64,1024]{1,0:T(8,128)(2,1)S(1)}, u32[]{:S(2)}, u32[]{:S(2)}) %collective-permute-start.38) | collective-permute-done | bytes 131104 | tf_op jit(solution)/shard_map/ppermute | solution.py:272
  86.8 1.7 %collective-permute-done.39.refs_1_ = bf16[64,1024]{1,0:T(8,128)(2,1)S(1)} collective-permute-done((bf16[64,1024]{1,0:T(8,128)(2,1)S(1)}, bf16[64,1024]{1,0:T(8,128)(2,1)S(1)}, u32[]{:S(2)}, u32[]{:S(2)}) %collective-permute-start.39) | collective-permute-done | bytes 131104 | tf_op jit(solution)/shard_map/ppermute | solution.py:272
  88.5 0.4 collective-permute-done.40.refs_2_
  88.9 0.9 last.1
  (69 shorter events, 2.2 us)
Async XLA Ops:
  0.6 0.9 %copy-start.7 = (bf16[1,3,32,1024]{3,2,1,0:T(8,128)(2,1)S(1)}, bf16[1,3,32,1024]{3,2,1,0:T(8,128)(2,1)}, u32[]{:S(2)}) copy-start(bf16[1,3,32,1024]{3,2,1,0:T(8,128)(2,1)} %param.8) | copy-start | bytes 589828
  1.6 4.7 %copy-start.1 = (bf16[1,4096,1024]{2,1,0:T(8,128)(2,1)S(1)}, bf16[1,4096,1024]{2,1,0:T(8,128)(2,1)}, u32[]{:S(2)}) copy-start(bf16[1,4096,1024]{2,1,0:T(8,128)(2,1)} %param.10) | copy-start | bytes 25165828
  1.6 4.7 %copy-start.2 = (f32[3,1024,16]{1,2,0:T(8,128)S(1)}, f32[3,1024,16]{1,2,0:T(8,128)}, u32[]{:S(2)}) copy-start(f32[3,1024,16]{1,2,0:T(8,128)} %param.15) | copy-start | bytes 589828
  1.6 4.7 %copy-start.3 = (f32[3,256,16]{1,2,0:T(8,128)S(1)}, f32[3,256,16]{1,2,0:T(8,128)}, u32[]{:S(2)}) copy-start(f32[3,256,16]{1,2,0:T(8,128)} %param.14) | copy-start | bytes 147460
  1.6 4.7 %copy-start.4 = (f32[1,1024,16]{1,2,0:T(8,128)S(1)}, f32[1,1024,16]{1,2,0:T(8,128)}, u32[]{:S(2)}) copy-start(f32[1,1024,16]{1,2,0:T(8,128)} %param.11) | copy-start | bytes 196612
  1.6 4.7 %copy-start.5 = (f32[1,1024,16]{1,2,0:T(8,128)S(1)}, f32[1,1024,16]{1,2,0:T(8,128)}, u32[]{:S(2)}) copy-start(f32[1,1024,16]{1,2,0:T(8,128)} %param.13) | copy-start | bytes 196612
  1.6 4.7 %copy-start.6 = (f32[1,256,16]{1,2,0:T(8,128)S(1)}, f32[1,256,16]{1,2,0:T(8,128)}, u32[]{:S(2)}) copy-start(f32[1,256,16]{1,2,0:T(8,128)} %param.12) | copy-start | bytes 49156
  1.6 7.5 %collective-permute-start = (bf16[32,1024]{1,0:T(8,128)(2,1)S(1)}, bf16[32,1024]{1,0:T(8,128)(2,1)S(1)}, u32[]{:S(2)}, u32[]{:S(2)}) collective-permute-start(bf16[32,1024]{1,0:T(8,128)(2,1)S(1)} %get-tuple-element.33.refs_0_), channel_id=1, source_target_pairs={{0,6},{1,7},{2,4},{3,5},{4,2},{5,3},{6,0},{7,1},{8,14},{9,15},{10,... | collective-permute-start | bytes 196616 | tf_op jit(solution)/shard_map/ppermute | solution.py:272
  5.6 4.3 %collective-permute-start.1 = (bf16[32,1024]{1,0:T(8,128)(2,1)S(1)}, bf16[32,1024]{1,0:T(8,128)(2,1)S(1)}, u32[]{:S(2)}, u32[]{:S(2)}) collective-permute-start(bf16[32,1024]{1,0:T(8,128)(2,1)S(1)} %get-tuple-element.33.refs_0_), channel_id=1, source_target_pairs={{0,4},{1,5},{2,6},{3,7},{4,0},{5,1},{6,2},{7,3},{8,12},{9,13},{10,... | collective-permute-start | bytes 196616 | tf_op jit(solution)/shard_map/ppermute | solution.py:272
  6.1 4.3 %collective-permute-start.2 = (bf16[32,1024]{1,0:T(8,128)(2,1)S(1)}, bf16[32,1024]{1,0:T(8,128)(2,1)S(1)}, u32[]{:S(2)}, u32[]{:S(2)}) collective-permute-start(bf16[32,1024]{1,0:T(8,128)(2,1)S(1)} %get-tuple-element.33.refs_0_), channel_id=1, source_target_pairs={{0,2},{1,3},{2,0},{3,1},{4,6},{5,7},{6,4},{7,5},{8,10},{9,11},{10,... | collective-permute-start | bytes 196616 | tf_op jit(solution)/shard_map/ppermute | solution.py:272
  6.2 5.6 %collective-permute-start.3 = (bf16[32,1024]{1,0:T(8,128)(2,1)S(1)}, bf16[32,1024]{1,0:T(8,128)(2,1)S(1)}, u32[]{:S(2)}, u32[]{:S(2)}) collective-permute-start(bf16[32,1024]{1,0:T(8,128)(2,1)S(1)} %get-tuple-element.33.refs_0_), channel_id=1, source_target_pairs={{0,1},{1,0},{2,3},{3,2},{4,5},{5,4},{6,7},{7,6},{8,9},{9,8},{10,11... | collective-permute-start | bytes 196616 | tf_op jit(solution)/shard_map/ppermute | solution.py:272
  6.3 4.1 %copy-start = (bf16[1,1024,4096]{2,1,0:T(8,128)(2,1)S(1)}, bf16[1,1024,4096]{2,1,0:T(8,128)(2,1)}, u32[]{:S(2)}) copy-start(bf16[1,1024,4096]{2,1,0:T(8,128)(2,1)} %param.9) | copy-start | bytes 25165828
  9.1 2.7 %collective-permute-start.4 = (bf16[32,1024]{1,0:T(8,128)(2,1)S(1)}, bf16[32,1024]{1,0:T(8,128)(2,1)S(1)}, u32[]{:S(2)}, u32[]{:S(2)}) collective-permute-start(bf16[32,1024]{1,0:T(8,128)(2,1)S(1)} %collective-permute-done.refs_1_), channel_id=1, source_target_pairs={{0,1},{1,0},{2,3},{3,2},{4,5},{5,4},{6,7},{7,6},{8,9},{9,8},{10,11... | collective-permute-start | bytes 196616 | tf_op jit(solution)/shard_map/ppermute | solution.py:272
  9.8 2.0 %collective-permute-start.5 = (bf16[32,1024]{1,0:T(8,128)(2,1)S(1)}, bf16[32,1024]{1,0:T(8,128)(2,1)S(1)}, u32[]{:S(2)}, u32[]{:S(2)}) collective-permute-start(bf16[32,1024]{1,0:T(8,128)(2,1)S(1)} %collective-permute-done.1.refs_2_), channel_id=1, source_target_pairs={{0,1},{1,0},{2,3},{3,2},{4,5},{5,4},{6,7},{7,6},{8,9},{9,8},{10,11... | collective-permute-start | bytes 196616 | tf_op jit(solution)/shard_map/ppermute | solution.py:272
  10.3 1.5 %collective-permute-start.6 = (bf16[32,1024]{1,0:T(8,128)(2,1)S(1)}, bf16[32,1024]{1,0:T(8,128)(2,1)S(1)}, u32[]{:S(2)}, u32[]{:S(2)}) collective-permute-start(bf16[32,1024]{1,0:T(8,128)(2,1)S(1)} %collective-permute-done.2.refs_3_), channel_id=1, source_target_pairs={{0,1},{1,0},{2,3},{3,2},{4,5},{5,4},{6,7},{7,6},{8,9},{9,8},{10,11... | collective-permute-start | bytes 196616 | tf_op jit(solution)/shard_map/ppermute | solution.py:272
  15.0 2.8 %collective-permute-start.7 = (f32[16,256]{1,0:T(8,128)S(1)}, f32[16,256]{1,0:T(8,128)S(1)}, u32[]{:S(2)}, u32[]{:S(2)}) collective-permute-start(f32[16,256]{1,0:T(8,128)S(1)} %get-tuple-element.36), channel_id=1, source_target_pairs={{0,1},{1,0},{2,3},{3,2},{4,5},{5,4},{6,7},{7,6},{8,9},{9,8},{10,11... | collective-permute-start | bytes 49160 | tf_op jit(solution)/shard_map/ppermute | solution.py:272
  15.6 13.5 %collective-permute-start.16 = (bf16[2,32,1024]{2,1,0:T(8,128)(2,1)S(1)}, bf16[2,32,1024]{2,1,0:T(8,128)(2,1)S(1)}, u32[]{:S(2)}, u32[]{:S(2)}) collective-permute-start(bf16[2,32,1024]{2,1,0:T(8,128)(2,1)S(1)} %get-tuple-element.43.refs_0_), channel_id=1, source_target_pairs={{0,6},{1,7},{2,4},{3,5},{4,2},{5,3},{6,0},{7,1},{8,14},{9,15},{10,... | collective-permute-start | bytes 393224 | tf_op jit(solution)/shard_map/ppermute | solution.py:272
  17.8 5.9 %collective-permute-start.10 = (f32[16,256]{1,0:T(8,128)S(1)}, f32[16,256]{1,0:T(8,128)S(1)}, u32[]{:S(2)}, u32[]{:S(2)}) collective-permute-start(f32[16,256]{1,0:T(8,128)S(1)} %add.63), channel_id=1, source_target_pairs={{0,4},{1,5},{2,6},{3,7},{4,0},{5,1},{6,2},{7,3},{8,12},{9,13},{10,... | collective-permute-start | bytes 49160 | tf_op jit(solution)/shard_map/ppermute | solution.py:272
  18.4 5.4 %collective-permute-start.8 = (f32[16,256]{1,0:T(8,128)S(1)}, f32[16,256]{1,0:T(8,128)S(1)}, u32[]{:S(2)}, u32[]{:S(2)}) collective-permute-start(f32[16,256]{1,0:T(8,128)S(1)} %add.63), channel_id=1, source_target_pairs={{0,6},{1,7},{2,4},{3,5},{4,2},{5,3},{6,0},{7,1},{8,14},{9,15},{10,... | collective-permute-start | bytes 49160 | tf_op jit(solution)/shard_map/ppermute | solution.py:272
  20.1 3.7 %collective-permute-start.9 = (f32[16,256]{1,0:T(8,128)S(1)}, f32[16,256]{1,0:T(8,128)S(1)}, u32[]{:S(2)}, u32[]{:S(2)}) collective-permute-start(f32[16,256]{1,0:T(8,128)S(1)} %add.63), channel_id=1, source_target_pairs={{0,2},{1,3},{2,0},{3,1},{4,6},{5,7},{6,4},{7,5},{8,10},{9,11},{10,... | collective-permute-start | bytes 49160 | tf_op jit(solution)/shard_map/ppermute | solution.py:272
  24.2 2.0 %collective-permute-start.11 = (f32[16,1024]{1,0:T(8,128)S(1)}, f32[16,1024]{1,0:T(8,128)S(1)}, u32[]{:S(2)}, u32[]{:S(2)}) collective-permute-start(f32[16,1024]{1,0:T(8,128)S(1)} %right.3), channel_id=1, source_target_pairs={{0,1},{1,0},{2,3},{3,2},{4,5},{5,4},{6,7},{7,6},{8,9},{9,8},{10,11... | collective-permute-start | bytes 196616 | tf_op jit(solution)/shard_map/ppermute | solution.py:272
  24.2 7.1 %collective-permute-start.17 = (bf16[2,32,1024]{2,1,0:T(8,128)(2,1)S(1)}, bf16[2,32,1024]{2,1,0:T(8,128)(2,1)S(1)}, u32[]{:S(2)}, u32[]{:S(2)}) collective-permute-start(bf16[2,32,1024]{2,1,0:T(8,128)(2,1)S(1)} %get-tuple-element.43.refs_0_), channel_id=1, source_target_pairs={{0,4},{1,5},{2,6},{3,7},{4,0},{5,1},{6,2},{7,3},{8,12},{9,13},{10,... | collective-permute-start | bytes 393224 | tf_op jit(solution)/shard_map/ppermute | solution.py:272
  25.1 6.3 %collective-permute-start.18 = (bf16[2,32,1024]{2,1,0:T(8,128)(2,1)S(1)}, bf16[2,32,1024]{2,1,0:T(8,128)(2,1)S(1)}, u32[]{:S(2)}, u32[]{:S(2)}) collective-permute-start(bf16[2,32,1024]{2,1,0:T(8,128)(2,1)S(1)} %get-tuple-element.43.refs_0_), channel_id=1, source_target_pairs={{0,2},{1,3},{2,0},{3,1},{4,6},{5,7},{6,4},{7,5},{8,10},{9,11},{10,... | collective-permute-start | bytes 393224 | tf_op jit(solution)/shard_map/ppermute | solution.py:272
  26.2 7.3 %collective-permute-start.12 = (f32[16,1024]{1,0:T(8,128)S(1)}, f32[16,1024]{1,0:T(8,128)S(1)}, u32[]{:S(2)}, u32[]{:S(2)}) collective-permute-start(f32[16,1024]{1,0:T(8,128)S(1)} %add.67), channel_id=1, source_target_pairs={{0,6},{1,7},{2,4},{3,5},{4,2},{5,3},{6,0},{7,1},{8,14},{9,15},{10,... | collective-permute-start | bytes 196616 | tf_op jit(solution)/shard_map/ppermute | solution.py:272
  27.8 5.7 %collective-permute-start.13 = (f32[16,1024]{1,0:T(8,128)S(1)}, f32[16,1024]{1,0:T(8,128)S(1)}, u32[]{:S(2)}, u32[]{:S(2)}) collective-permute-start(f32[16,1024]{1,0:T(8,128)S(1)} %add.67), channel_id=1, source_target_pairs={{0,2},{1,3},{2,0},{3,1},{4,6},{5,7},{6,4},{7,5},{8,10},{9,11},{10,... | collective-permute-start | bytes 196616 | tf_op jit(solution)/shard_map/ppermute | solution.py:272
  29.1 4.9 %collective-permute-start.14 = (f32[16,1024]{1,0:T(8,128)S(1)}, f32[16,1024]{1,0:T(8,128)S(1)}, u32[]{:S(2)}, u32[]{:S(2)}) collective-permute-start(f32[16,1024]{1,0:T(8,128)S(1)} %add.67), channel_id=1, source_target_pairs={{0,4},{1,5},{2,6},{3,7},{4,0},{5,1},{6,2},{7,3},{8,12},{9,13},{10,... | collective-permute-start | bytes 196616 | tf_op jit(solution)/shard_map/ppermute | solution.py:272
  31.3 4.4 %collective-permute-start.19 = (bf16[2,32,1024]{2,1,0:T(8,128)(2,1)S(1)}, bf16[2,32,1024]{2,1,0:T(8,128)(2,1)S(1)}, u32[]{:S(2)}, u32[]{:S(2)}) collective-permute-start(bf16[2,32,1024]{2,1,0:T(8,128)(2,1)S(1)} %get-tuple-element.43.refs_0_), channel_id=1, source_target_pairs={{0,1},{1,0},{2,3},{3,2},{4,5},{5,4},{6,7},{7,6},{8,9},{9,8},{10,11... | collective-permute-start | bytes 393224 | tf_op jit(solution)/shard_map/ppermute | solution.py:272
  31.4 4.3 %collective-permute-start.20 = (bf16[2,32,1024]{2,1,0:T(8,128)(2,1)S(1)}, bf16[2,32,1024]{2,1,0:T(8,128)(2,1)S(1)}, u32[]{:S(2)}, u32[]{:S(2)}) collective-permute-start(bf16[2,32,1024]{2,1,0:T(8,128)(2,1)S(1)} %collective-permute-done.16.refs_1_), channel_id=1, source_target_pairs={{0,1},{1,0},{2,3},{3,2},{4,5},{5,4},{6,7},{7,6},{8,9},{9,8},{10,11... | collective-permute-start | bytes 393224 | tf_op jit(solution)/shard_map/ppermute | solution.py:272
  33.5 2.2 %collective-permute-start.21 = (bf16[2,32,1024]{2,1,0:T(8,128)(2,1)S(1)}, bf16[2,32,1024]{2,1,0:T(8,128)(2,1)S(1)}, u32[]{:S(2)}, u32[]{:S(2)}) collective-permute-start(bf16[2,32,1024]{2,1,0:T(8,128)(2,1)S(1)} %collective-permute-done.17.refs_2_), channel_id=1, source_target_pairs={{0,1},{1,0},{2,3},{3,2},{4,5},{5,4},{6,7},{7,6},{8,9},{9,8},{10,11... | collective-permute-start | bytes 393224 | tf_op jit(solution)/shard_map/ppermute | solution.py:272
  33.5 2.2 %collective-permute-start.22 = (bf16[2,32,1024]{2,1,0:T(8,128)(2,1)S(1)}, bf16[2,32,1024]{2,1,0:T(8,128)(2,1)S(1)}, u32[]{:S(2)}, u32[]{:S(2)}) collective-permute-start(bf16[2,32,1024]{2,1,0:T(8,128)(2,1)S(1)} %collective-permute-done.18.refs_3_), channel_id=1, source_target_pairs={{0,1},{1,0},{2,3},{3,2},{4,5},{5,4},{6,7},{7,6},{8,9},{9,8},{10,11... | collective-permute-start | bytes 393224 | tf_op jit(solution)/shard_map/ppermute | solution.py:272
  34.2 6.3 %collective-permute-start.15 = (f32[16,1280]{1,0:T(8,128)S(1)}, f32[16,1280]{1,0:T(8,128)S(1)}, u32[]{:S(2)}, u32[]{:S(2)}) collective-permute-start(f32[16,1280]{1,0:T(8,128)S(1)} %get-tuple-element.41.refs_9_), channel_id=1, source_target_pairs={{8,0},{16,8},{24,16},{9,1},{17,9},{25,17},{10,2},{18,10},{26,18},{... | collective-permute-start | bytes 245768 | tf_op jit(solution)/shard_map/ppermute | solution.py:423
  44.2 1.2 %collective-permute-start.23 = (f32[16,256]{1,0:T(8,128)S(1)}, f32[16,256]{1,0:T(8,128)S(1)}, u32[]{:S(2)}, u32[]{:S(2)}) collective-permute-start(f32[16,256]{1,0:T(8,128)S(1)} %get-tuple-element.44), channel_id=1, source_target_pairs={{0,1},{1,0},{2,3},{3,2},{4,5},{5,4},{6,7},{7,6},{8,9},{9,8},{10,11... | collective-permute-start | bytes 49160 | tf_op jit(solution)/shard_map/ppermute | solution.py:272
  45.5 5.9 %collective-permute-start.24 = (f32[16,256]{1,0:T(8,128)S(1)}, f32[16,256]{1,0:T(8,128)S(1)}, u32[]{:S(2)}, u32[]{:S(2)}) collective-permute-start(f32[16,256]{1,0:T(8,128)S(1)} %add.71), channel_id=1, source_target_pairs={{0,6},{1,7},{2,4},{3,5},{4,2},{5,3},{6,0},{7,1},{8,14},{9,15},{10,... | collective-permute-start | bytes 49160 | tf_op jit(solution)/shard_map/ppermute | solution.py:272
  47.3 4.1 %collective-permute-start.25 = (f32[16,256]{1,0:T(8,128)S(1)}, f32[16,256]{1,0:T(8,128)S(1)}, u32[]{:S(2)}, u32[]{:S(2)}) collective-permute-start(f32[16,256]{1,0:T(8,128)S(1)} %add.71), channel_id=1, source_target_pairs={{0,2},{1,3},{2,0},{3,1},{4,6},{5,7},{6,4},{7,5},{8,10},{9,11},{10,... | collective-permute-start | bytes 49160 | tf_op jit(solution)/shard_map/ppermute | solution.py:272
  48.0 3.7 %collective-permute-start.26 = (f32[16,256]{1,0:T(8,128)S(1)}, f32[16,256]{1,0:T(8,128)S(1)}, u32[]{:S(2)}, u32[]{:S(2)}) collective-permute-start(f32[16,256]{1,0:T(8,128)S(1)} %add.71), channel_id=1, source_target_pairs={{0,4},{1,5},{2,6},{3,7},{4,0},{5,1},{6,2},{7,3},{8,12},{9,13},{10,... | collective-permute-start | bytes 49160 | tf_op jit(solution)/shard_map/ppermute | solution.py:272
  52.1 1.3 %collective-permute-start.27 = (f32[16,1024]{1,0:T(8,128)S(1)}, f32[16,1024]{1,0:T(8,128)S(1)}, u32[]{:S(2)}, u32[]{:S(2)}) collective-permute-start(f32[16,1024]{1,0:T(8,128)S(1)} %right.4), channel_id=1, source_target_pairs={{0,1},{1,0},{2,3},{3,2},{4,5},{5,4},{6,7},{7,6},{8,9},{9,8},{10,11... | collective-permute-start | bytes 196616 | tf_op jit(solution)/shard_map/ppermute | solution.py:272
  53.3 5.7 %collective-permute-start.28 = (f32[16,1024]{1,0:T(8,128)S(1)}, f32[16,1024]{1,0:T(8,128)S(1)}, u32[]{:S(2)}, u32[]{:S(2)}) collective-permute-start(f32[16,1024]{1,0:T(8,128)S(1)} %add.75), channel_id=1, source_target_pairs={{0,6},{1,7},{2,4},{3,5},{4,2},{5,3},{6,0},{7,1},{8,14},{9,15},{10,... | collective-permute-start | bytes 196616 | tf_op jit(solution)/shard_map/ppermute | solution.py:272
  55.1 4.4 %collective-permute-start.29 = (f32[16,1024]{1,0:T(8,128)S(1)}, f32[16,1024]{1,0:T(8,128)S(1)}, u32[]{:S(2)}, u32[]{:S(2)}) collective-permute-start(f32[16,1024]{1,0:T(8,128)S(1)} %add.75), channel_id=1, source_target_pairs={{0,2},{1,3},{2,0},{3,1},{4,6},{5,7},{6,4},{7,5},{8,10},{9,11},{10,... | collective-permute-start | bytes 196616 | tf_op jit(solution)/shard_map/ppermute | solution.py:272
  55.8 4.3 %collective-permute-start.30 = (f32[16,1024]{1,0:T(8,128)S(1)}, f32[16,1024]{1,0:T(8,128)S(1)}, u32[]{:S(2)}, u32[]{:S(2)}) collective-permute-start(f32[16,1024]{1,0:T(8,128)S(1)} %add.75), channel_id=1, source_target_pairs={{0,4},{1,5},{2,6},{3,7},{4,0},{5,1},{6,2},{7,3},{8,12},{9,13},{10,... | collective-permute-start | bytes 196616 | tf_op jit(solution)/shard_map/ppermute | solution.py:272
  60.3 6.3 %collective-permute-start.31 = (f32[16,1280]{1,0:T(8,128)S(1)}, f32[16,1280]{1,0:T(8,128)S(1)}, u32[]{:S(2)}, u32[]{:S(2)}) collective-permute-start(f32[16,1280]{1,0:T(8,128)S(1)} %get-tuple-element.49.refs_9_), channel_id=1, source_target_pairs={{8,0},{16,8},{24,16},{9,1},{17,9},{25,17},{10,2},{18,10},{26,18},{... | collective-permute-start | bytes 245768 | tf_op jit(solution)/shard_map/ppermute | solution.py:423
  70.4 1.2 %collective-permute-start.32 = (f32[16,256]{1,0:T(8,128)S(1)}, f32[16,256]{1,0:T(8,128)S(1)}, u32[]{:S(2)}, u32[]{:S(2)}) collective-permute-start(f32[16,256]{1,0:T(8,128)S(1)} %get-tuple-element.51), channel_id=1, source_target_pairs={{0,1},{1,0},{2,3},{3,2},{4,5},{5,4},{6,7},{7,6},{8,9},{9,8},{10,11... | collective-permute-start | bytes 49160 | tf_op jit(solution)/shard_map/ppermute | solution.py:272
  71.6 6.0 %collective-permute-start.33 = (f32[16,256]{1,0:T(8,128)S(1)}, f32[16,256]{1,0:T(8,128)S(1)}, u32[]{:S(2)}, u32[]{:S(2)}) collective-permute-start(f32[16,256]{1,0:T(8,128)S(1)} %add.79), channel_id=1, source_target_pairs={{0,6},{1,7},{2,4},{3,5},{4,2},{5,3},{6,0},{7,1},{8,14},{9,15},{10,... | collective-permute-start | bytes 49160 | tf_op jit(solution)/shard_map/ppermute | solution.py:272
  73.4 4.2 %collective-permute-start.34 = (f32[16,256]{1,0:T(8,128)S(1)}, f32[16,256]{1,0:T(8,128)S(1)}, u32[]{:S(2)}, u32[]{:S(2)}) collective-permute-start(f32[16,256]{1,0:T(8,128)S(1)} %add.79), channel_id=1, source_target_pairs={{0,2},{1,3},{2,0},{3,1},{4,6},{5,7},{6,4},{7,5},{8,10},{9,11},{10,... | collective-permute-start | bytes 49160 | tf_op jit(solution)/shard_map/ppermute | solution.py:272
  74.1 3.7 %collective-permute-start.35 = (f32[16,256]{1,0:T(8,128)S(1)}, f32[16,256]{1,0:T(8,128)S(1)}, u32[]{:S(2)}, u32[]{:S(2)}) collective-permute-start(f32[16,256]{1,0:T(8,128)S(1)} %add.79), channel_id=1, source_target_pairs={{0,4},{1,5},{2,6},{3,7},{4,0},{5,1},{6,2},{7,3},{8,12},{9,13},{10,... | collective-permute-start | bytes 49160 | tf_op jit(solution)/shard_map/ppermute | solution.py:272
  77.5 1.9 %collective-permute-start.36 = (bf16[4,32,1024]{2,1,0:T(8,128)(2,1)S(1)}, bf16[4,32,1024]{2,1,0:T(8,128)(2,1)S(1)}, u32[]{:S(2)}, u32[]{:S(2)}) collective-permute-start(bf16[4,32,1024]{2,1,0:T(8,128)(2,1)S(1)} %outgoing.1), channel_id=1, source_target_pairs={{0,1},{1,0},{2,3},{3,2},{4,5},{5,4},{6,7},{7,6},{8,9},{9,8},{10,11... | collective-permute-start | bytes 786440 | tf_op jit(solution)/shard_map/ppermute | solution.py:272
  78.2 1.3 %collective-permute-start.37 = (f32[16,1024]{1,0:T(8,128)S(1)}, f32[16,1024]{1,0:T(8,128)S(1)}, u32[]{:S(2)}, u32[]{:S(2)}) collective-permute-start(f32[16,1024]{1,0:T(8,128)S(1)} %right.5.right_ref), channel_id=1, source_target_pairs={{0,1},{1,0},{2,3},{3,2},{4,5},{5,4},{6,7},{7,6},{8,9},{9,8},{10,11... | collective-permute-start | bytes 196616 | tf_op jit(solution)/shard_map/ppermute | solution.py:272
  79.5 7.3 %collective-permute-start.38 = (bf16[64,1024]{1,0:T(8,128)(2,1)S(1)}, bf16[64,1024]{1,0:T(8,128)(2,1)S(1)}, u32[]{:S(2)}, u32[]{:S(2)}) collective-permute-start(bf16[64,1024]{1,0:T(8,128)(2,1)S(1)} %get-tuple-element.57), channel_id=1, source_target_pairs={{0,6},{1,7},{2,4},{3,5},{4,2},{5,3},{6,0},{7,1},{8,14},{9,15},{10,... | collective-permute-start | bytes 393224 | tf_op jit(solution)/shard_map/ppermute | solution.py:272
  81.3 7.3 %collective-permute-start.39 = (bf16[64,1024]{1,0:T(8,128)(2,1)S(1)}, bf16[64,1024]{1,0:T(8,128)(2,1)S(1)}, u32[]{:S(2)}, u32[]{:S(2)}) collective-permute-start(bf16[64,1024]{1,0:T(8,128)(2,1)S(1)} %get-tuple-element.58), channel_id=1, source_target_pairs={{0,2},{1,3},{2,0},{3,1},{4,6},{5,7},{6,4},{7,5},{8,10},{9,11},{10,... | collective-permute-start | bytes 393224 | tf_op jit(solution)/shard_map/ppermute | solution.py:272
  82.0 6.9 %collective-permute-start.40 = (bf16[64,1024]{1,0:T(8,128)(2,1)S(1)}, bf16[64,1024]{1,0:T(8,128)(2,1)S(1)}, u32[]{:S(2)}, u32[]{:S(2)}) collective-permute-start(bf16[64,1024]{1,0:T(8,128)(2,1)S(1)} %get-tuple-element.59), channel_id=1, source_target_pairs={{0,4},{1,5},{2,6},{3,7},{4,0},{5,1},{6,2},{7,3},{8,12},{9,13},{10,... | collective-permute-start | bytes 393224 | tf_op jit(solution)/shard_map/ppermute | solution.py:272
